TPU v7x, 128 devices: a whole 4x4x4 slice. The times are simulated.
128 devices in a mesh: ch: 32 (over z, y, core), img: 4 (over x).
Axes of the slice: x: 4, y: 4, z: 4, core: 2. Of those that a mesh axis runs over, the one named last changes fastest.
Arguments:
- features: bfloat16 [128, 165888], P('ch', 'img'), may hold values from -6 to 6
- size_group: int32 [128], P('img'), may hold values from 0 to 2
- cycle_offsets: int32 [2, 128], replicated, may hold values from -1 to 1
- norm_gain: bfloat16 [128], replicated, may hold values from 0.5 to 1.5
- norm_bias: bfloat16 [128], replicated, may hold values from -3 to 3
- height_weight: bfloat16 [128, 128], replicated, may hold values from -0.5 to 0.5
- height_bias: bfloat16 [128], replicated, may hold values from -3 to 3
- width_weight: bfloat16 [128, 128], replicated, may hold values from -0.5 to 0.5
- width_bias: bfloat16 [128], replicated, may hold values from -3 to 3
- channel_weight: bfloat16 [128, 128], replicated, may hold values from -0.5 to 0.5
- squeeze_weight: bfloat16 [128, 32], replicated, may hold values from -1.5 to 1.5
- squeeze_bias: bfloat16 [32], replicated, may hold values from -3 to 3
- excite_weight: bfloat16 [32, 384], replicated, may hold values from -1 to 1
- excite_bias: bfloat16 [384], replicated, may hold values from -3 to 3
- output_weight: bfloat16 [128, 128], replicated, may hold values from -0.75 to 0.75
- output_bias: bfloat16 [128], replicated, may hold values from -3 to 3
- second_gain: bfloat16 [128], replicated, may hold values from 0.5 to 1.5
- second_bias: bfloat16 [128], replicated, may hold values from -3 to 3
- expand_weight: bfloat16 [128, 512], replicated, may hold values from -0.5 to 0.5
- expand_bias: bfloat16 [512], replicated, may hold values from -3 to 3
- reduce_weight: bfloat16 [512, 128], replicated, may hold values from -0.375 to 0.375
- reduce_bias: bfloat16 [128], replicated, may hold values from -3 to 3
- stride_weight: bfloat16 [320, 9, 128], replicated, may hold values from -0.1875 to 0.1875
- stride_bias: bfloat16 [320], replicated, may hold values from -3 to 3
- cotangent: bfloat16 [320, 41472], P('ch', 'img'), may hold values from -6 to 6
Outputs:
- section_out: bfloat16 [320, 41472], P('ch', 'img')
- features_grad: float32 [128, 165888], P('ch', 'img')
- norm_gain_grad: float32 [128], replicated
- norm_bias_grad: float32 [128], replicated
- height_weight_grad: float32 [128, 128], replicated
- height_bias_grad: float32 [128], replicated
- width_weight_grad: float32 [128, 128], replicated
- width_bias_grad: float32 [128], replicated
- channel_weight_grad: float32 [128, 128], replicated
- squeeze_weight_grad: float32 [128, 32], replicated
- squeeze_bias_grad: float32 [32], replicated
- excite_weight_grad: float32 [32, 384], replicated
- excite_bias_grad: float32 [384], replicated
- output_weight_grad: float32 [128, 128], replicated
- output_bias_grad: float32 [128], replicated
- second_gain_grad: float32 [128], replicated
- second_bias_grad: float32 [128], replicated
- expand_weight_grad: float32 [128, 512], replicated
- expand_bias_grad: float32 [512], replicated
- reduce_weight_grad: float32 [512, 128], replicated
- reduce_bias_grad: float32 [128], replicated
- stride_weight_grad: float32 [320, 9, 128], replicated
- stride_bias_grad: float32 [320], replicated
All inputs are finite; a program needn't handle non-finite values.
Results may differ from a plain program's by a relative error of at most 0.0078.
The roundings to bfloat16 on the way count: a program that leaves them out, or rounds other values in their place, can miss the bound.
Values may be sent and summed in bfloat16 or wider, within the bound.
No kernel may reach another device: no remote copies, remote signals or barrier semaphores. Data moves between devices by JAX's collectives and lax.ppermute only.
A program may use at most 128 MiB of HBM per device.

v0:
```python
import jax
import jax.numpy as jnp
from jax import lax
from jax.sharding import PartitionSpec as P

BLOCK_CHANNELS = 128
OUT = 320
CANVAS = 36


EPS = 1e-05
HIGH = lax.Precision.HIGHEST


def tdot(left, right):
    return lax.dot_general(
        left, right, (((0,), (0,)), ((), ())), preferred_element_type=jnp.float32
    )


def rdot(left, right):
    return lax.dot_general(
        left, right, (((1,), (1,)), ((), ())), preferred_element_type=jnp.float32
    )


def exact_tdot(left, right):
    return lax.dot_general(
        left, right, (((0,), (0,)), ((), ())), precision=HIGH, preferred_element_type=jnp.float32
    )


def layer_norm(values, gain, bias):
    center = values - jnp.mean(values, axis=0, keepdims=True)
    spread = jnp.mean(center * center, axis=0, keepdims=True)
    return center * lax.rsqrt(spread + EPS) * gain[:, None] + bias[:, None]


def gelu_exact(values):
    return jax.nn.gelu(values, approximate=False)


def reweigh(means, squeeze_w, squeeze_b, excite_w, excite_b):
    inner = gelu_exact(exact_tdot(squeeze_w, means) + squeeze_b[:, None])
    logits = exact_tdot(excite_w, inner) + excite_b[:, None]
    return jax.nn.softmax(logits.reshape(3, -1, means.shape[1]), axis=0)


def pick(padded, offsets, stride, sign, count):
    result = jnp.zeros((padded.shape[0], count), padded.dtype)
    for step in (-1, 0, 1):
        begin = CANVAS + sign * step * stride
        result = jnp.where(offsets[:, None] == step, padded[:, begin : begin + count], result)
    return result


def inside(coord, offsets):
    moved = coord[None, :] + offsets[:, None]
    return (moved >= 0) & (moved < CANVAS)


def pixel_info(count, sides):
    index = jnp.arange(count, dtype=jnp.int32)
    image = index // (CANVAS * CANVAS)
    local = index % (CANVAS * CANVAS)
    row = local // CANVAS
    column = local % CANVAS
    onehot = (image[:, None] == jnp.arange(sides.shape[0], dtype=jnp.int32)[None, :]).astype(
        jnp.float32
    )
    side = jnp.sum(onehot * sides[None, :], axis=1)
    valid = ((row < side) & (column < side)).astype(jnp.float32)
    return (valid, onehot, row, column)


def out_info(sides):
    half = CANVAS // 2
    index = jnp.arange(sides.shape[0] * half * half, dtype=jnp.int32)
    image = index // (half * half)
    local = index % (half * half)
    onehot = (image[:, None] == jnp.arange(sides.shape[0], dtype=jnp.int32)[None, :]).astype(
        jnp.float32
    )
    side = jnp.sum(onehot * sides[None, :], axis=1)
    return ((2 * (local // half) < side) & (2 * (local % half) < side)).astype(jnp.float32)


def make_taps(block):
    channels = block.shape[0]
    images = block.shape[1] // (CANVAS * CANVAS)
    half = CANVAS // 2
    flat_count = images * half * half
    grid = block.reshape(channels, images, half, 2, half, 2)
    planes = jnp.transpose(grid, (3, 5, 0, 1, 2, 4)).reshape(2, 2, channels, flat_count)
    position = jnp.arange(flat_count, dtype=jnp.int32)
    row_ok = (position // half % half >= 1)[None, :]
    col_ok = (position % half >= 1)[None, :]
    parity = (1, 0, 1)
    gathered = []
    for first in range(3):
        for second in range(3):
            shifted = planes[parity[first], parity[second]]
            if first == 0:
                shifted = jnp.where(
                    row_ok, jnp.pad(shifted, ((0, 0), (half, 0)))[:, :flat_count], 0.0
                )
            if second == 0:
                shifted = jnp.where(col_ok, jnp.pad(shifted, ((0, 0), (1, 0)))[:, :flat_count], 0.0)
            gathered.append(shifted)
    return jnp.stack(gathered).reshape(9 * channels, flat_count)


def body(
    features,
    size_group,
    cycle_offsets,
    norm_gain,
    norm_bias,
    height_weight,
    height_bias,
    width_weight,
    width_bias,
    channel_weight,
    squeeze_weight,
    squeeze_bias,
    excite_weight,
    excite_bias,
    output_weight,
    output_bias,
    second_gain,
    second_bias,
    expand_weight,
    expand_bias,
    reduce_weight,
    reduce_bias,
    stride_weight,
    stride_bias,
    cotangent,
):
    shards = lax.axis_size("ch")
    rank = lax.axis_index("ch")
    local_ch = features.shape[0]
    total = features.shape[1]
    share = total // shards
    images = size_group.shape[0]
    per_dev = images // shards
    leading_entry = rank * local_ch
    sides = (CANVAS - 4 * (2 - size_group)).astype(jnp.float32)
    own_sides = lax.dynamic_slice_in_dim(sides, rank * per_dev, per_dev)
    own_counts = own_sides * own_sides
    complete_validity, full_onehot, full_row, full_col = pixel_info(total, sides)
    pix_valid, onehot, pix_row, pix_col = pixel_info(share, own_sides)
    out_valid = out_info(sides)
    own_out_valid = out_info(own_sides)
    gain_full = norm_gain.astype(jnp.float32)
    bias_full = norm_bias.astype(jnp.float32)
    own_offsets = lax.dynamic_slice_in_dim(cycle_offsets, leading_entry, local_ch, 1)
    masked_cast = features.astype(jnp.float32) * complete_validity
    sums = lax.psum(
        (jnp.sum(masked_cast, axis=0), jnp.sum(masked_cast * masked_cast, axis=0)), "ch"
    )
    mean_cast = sums[0] / BLOCK_CHANNELS
    inverse_deviation = lax.rsqrt(sums[1] / BLOCK_CHANNELS - mean_cast * mean_cast + EPS)
    centered_scaled_input = (masked_cast - mean_cast) * inverse_deviation
    gain_cast = lax.dynamic_slice_in_dim(gain_full, leading_entry, local_ch)
    bias_cast = lax.dynamic_slice_in_dim(bias_full, leading_entry, local_ch)
    normed_cast = (
        (centered_scaled_input * gain_cast[:, None] + bias_cast[:, None]) * complete_validity
    ).astype(jnp.bfloat16)
    padded_c = jnp.pad(normed_cast, ((0, 0), (CANVAS, CANVAS)))
    rows_in_c = inside(full_row, own_offsets[0])
    cols_in_c = inside(full_col, own_offsets[1])
    rows_c = jnp.where(rows_in_c, pick(padded_c, own_offsets[0], CANVAS, 1, total), 0)
    cols_c = jnp.where(cols_in_c, pick(padded_c, own_offsets[1], 1, 1, total), 0)
    input_b = jnp.where(complete_validity[None, :] > 0, features, jnp.zeros_like(features))
    payload = jnp.stack([input_b, rows_c, cols_c, normed_cast])
    moved = lax.all_to_all(payload, "ch", split_axis=2, concat_axis=1, tiled=True)
    masked = moved[0].astype(jnp.float32)
    shift_rows = moved[1]
    shift_cols = moved[2]
    normed = moved[3]
    branch_h = tdot(height_weight, shift_rows) + height_bias.astype(jnp.float32)[:, None]
    branch_w = tdot(width_weight, shift_cols) + width_bias.astype(jnp.float32)[:, None]
    branch_c = tdot(channel_weight, normed)
    partial_value = jnp.dot((branch_h + branch_w + branch_c) * pix_valid, onehot, precision=HIGH)
    means = partial_value / own_counts
    small = tuple(
        (p.astype(jnp.float32) for p in (squeeze_weight, squeeze_bias, excite_weight, excite_bias))
    )
    mix_weight, mix_pull = jax.vjp(reweigh, means, *small)
    spread = jnp.einsum("jck,pk->jcp", mix_weight, onehot, precision=HIGH)
    mixed = (spread[0] * branch_h + spread[1] * branch_w + spread[2] * branch_c).astype(
        jnp.bfloat16
    )
    resid = masked + tdot(output_weight, mixed) + output_bias.astype(jnp.float32)[:, None]
    normed2_f, second_pull = jax.vjp(
        layer_norm, resid, second_gain.astype(jnp.float32), second_bias.astype(jnp.float32)
    )
    normed2 = normed2_f.astype(jnp.bfloat16)
    pre = tdot(expand_weight, normed2) + expand_bias.astype(jnp.float32)[:, None]
    active, gelu_pull = jax.vjp(gelu_exact, pre)
    hidden = active.astype(jnp.bfloat16)
    block = (
        resid + tdot(reduce_weight, hidden) + reduce_bias.astype(jnp.float32)[:, None]
    ) * pix_valid
    block_b = block.astype(jnp.bfloat16)
    cot_masked = jnp.where(out_valid[None, :] > 0, cotangent, jnp.zeros_like(cotangent))
    taps_f, taps_pull = jax.vjp(make_taps, block_b.astype(jnp.float32))
    taps = taps_f.astype(jnp.bfloat16)
    whole_conv = stride_weight.reshape(OUT, 9 * BLOCK_CHANNELS)
    section_local = (
        (
            jnp.dot(whole_conv, taps, preferred_element_type=jnp.float32)
            + stride_bias.astype(jnp.float32)[:, None]
        )
        * own_out_valid
    ).astype(jnp.bfloat16)
    section = lax.all_to_all(section_local, "ch", split_axis=0, concat_axis=1, tiled=True)
    cot_pix = lax.all_to_all(cot_masked, "ch", split_axis=1, concat_axis=0, tiled=True)
    conv_bias_full = jnp.sum(cot_pix.astype(jnp.float32), axis=1)
    conv_full = rdot(cot_pix, taps).reshape(OUT, 9, BLOCK_CHANNELS)
    (grad_block_f,) = taps_pull(tdot(whole_conv, cot_pix))
    grad_block = grad_block_f * pix_valid
    g_reduce = grad_block.astype(jnp.bfloat16)
    reduce_grad = rdot(hidden, g_reduce)
    reduce_bias_grad = jnp.sum(g_reduce.astype(jnp.float32), axis=1)
    (g_pre_f,) = gelu_pull(jnp.dot(reduce_weight, g_reduce, preferred_element_type=jnp.float32))
    g_pre = g_pre_f.astype(jnp.bfloat16)
    expand_grad = rdot(normed2, g_pre)
    expand_bias_grad = jnp.sum(g_pre.astype(jnp.float32), axis=1)
    g_norm2 = jnp.dot(expand_weight, g_pre, preferred_element_type=jnp.float32)
    g_resid_ln, second_gain_grad, second_bias_grad = second_pull(g_norm2)
    g_resid = grad_block + g_resid_ln
    g_proj = g_resid.astype(jnp.bfloat16)
    output_grad = rdot(mixed, g_proj)
    output_bias_grad = jnp.sum(g_proj.astype(jnp.float32), axis=1)
    g_mixed = jnp.dot(output_weight, g_proj, preferred_element_type=jnp.float32)
    g_mix = jnp.stack(
        [
            jnp.dot(g_mixed * branch, onehot, precision=HIGH)
            for branch in (branch_h, branch_w, branch_c)
        ]
    )
    g_means, squeeze_grad, squeeze_bias_grad, excite_grad, excite_bias_grad = mix_pull(g_mix)
    mean_spread = jnp.dot(g_means / own_counts, onehot.T, precision=HIGH) * pix_valid
    g_height = (spread[0] * g_mixed + mean_spread).astype(jnp.bfloat16)
    g_width = (spread[1] * g_mixed + mean_spread).astype(jnp.bfloat16)
    g_chan = (spread[2] * g_mixed + mean_spread).astype(jnp.bfloat16)
    height_grad = rdot(shift_rows, g_height)
    width_grad = rdot(shift_cols, g_width)
    channel_grad = rdot(normed, g_chan)
    height_bias_grad = jnp.sum(g_height.astype(jnp.float32), axis=1)
    width_bias_grad = jnp.sum(g_width.astype(jnp.float32), axis=1)
    g_rows = jnp.dot(height_weight, g_height, preferred_element_type=jnp.float32)
    g_cols = jnp.dot(width_weight, g_width, preferred_element_type=jnp.float32)
    g_norm_chan = jnp.dot(channel_weight, g_chan, preferred_element_type=jnp.float32)
    send_back = jnp.stack([g_resid, g_rows, g_cols, g_norm_chan])
    returned = lax.all_to_all(
        send_back.astype(jnp.bfloat16), "ch", split_axis=1, concat_axis=2, tiled=True
    ).astype(send_back.dtype)
    rows_pad = jnp.pad(jnp.where(rows_in_c, returned[1], 0.0), ((0, 0), (CANVAS, CANVAS)))
    cols_pad = jnp.pad(jnp.where(cols_in_c, returned[2], 0.0), ((0, 0), (CANVAS, CANVAS)))
    g_normed_c = (
        returned[3]
        + pick(rows_pad, own_offsets[0], CANVAS, -1, total)
        + pick(cols_pad, own_offsets[1], 1, -1, total)
    )
    scaled_gradient = g_normed_c * complete_validity
    normalized_gradient = scaled_gradient * gain_cast[:, None]
    running_totals = (
        lax.psum(jnp.sum(normalized_gradient, axis=0).astype(jnp.bfloat16), "ch").astype(
            jnp.float32
        ),
        lax.psum(
            jnp.sum(normalized_gradient * centered_scaled_input, axis=0).astype(jnp.bfloat16), "ch"
        ).astype(jnp.float32),
    )
    input_gradient = inverse_deviation * (
        normalized_gradient
        - running_totals[0] / BLOCK_CHANNELS
        - centered_scaled_input * running_totals[1] / BLOCK_CHANNELS
    )
    features_grad = (returned[0] + input_gradient) * complete_validity
    gain_part = lax.dynamic_update_slice_in_dim(
        jnp.zeros((BLOCK_CHANNELS,), jnp.float32),
        jnp.sum(scaled_gradient * centered_scaled_input, axis=1),
        leading_entry,
        0,
    )
    bias_part = lax.dynamic_update_slice_in_dim(
        jnp.zeros((BLOCK_CHANNELS,), jnp.float32),
        jnp.sum(scaled_gradient, axis=1),
        leading_entry,
        0,
    )
    summed = lax.psum(
        (
            gain_part,
            bias_part,
            height_grad,
            height_bias_grad,
            width_grad,
            width_bias_grad,
            channel_grad,
            squeeze_grad,
            squeeze_bias_grad,
            excite_grad,
            excite_bias_grad,
            output_grad,
            output_bias_grad,
            second_gain_grad,
            second_bias_grad,
            expand_grad,
            expand_bias_grad,
            reduce_grad,
            reduce_bias_grad,
            conv_full,
            conv_bias_full,
        ),
        ("ch", "img"),
    )
    return (
        section,
        features_grad,
        summed[0],
        summed[1],
        summed[2],
        summed[3],
        summed[4],
        summed[5],
        summed[6],
        summed[7],
        summed[8],
        summed[9],
        summed[10],
        summed[11],
        summed[12],
        summed[13],
        summed[14],
        summed[15],
        summed[16],
        summed[17],
        summed[18],
        summed[19],
        summed[20],
    )


def solution(mesh):
    placed = (
        P("ch", "img"),
        P("img"),
        P(),
        P(),
        P(),
        P(),
        P(),
        P(),
        P(),
        P(),
        P(),
        P(),
        P(),
        P(),
        P(),
        P(),
        P(),
        P(),
        P(),
        P(),
        P(),
        P(),
        P(),
        P(),
        P("ch", "img"),
    )
    return jax.shard_map(
        body,
        mesh=mesh,
        in_specs=placed,
        out_specs=(
            P("ch", "img"),
            P("ch", "img"),
            P(),
            P(),
            P(),
            P(),
            P(),
            P(),
            P(),
            P(),
            P(),
            P(),
            P(),
            P(),
            P(),
            P(),
            P(),
            P(),
            P(),
            P(),
            P(),
            P(),
            P(),
        ),
        check_vma=False,
    )
```

profile of v0, /device:TPU:1, one launch (start us, length us, event | category | flops | bytes accessed | tf_op | source)
XLA Modules:
  0.0 980.6 jit_solution(17233170274500218682)
XLA Ops:
  11.0 9.7 all-to-all-start.2
  22.3 1.5 fusion.46
  34.3 2.1 fusion.59
  36.4 92.3 %all-reduce.36.cloned.1.call-done = (f32[41472]{0:T(1024)}, f32[41472]{0:T(1024)}) async-done(((f32[41472]{0:T(1024)}, f32[41472]{0:T(1024)}), (f32[41472]{0:T(1024)}, f32[41472]{0:T(1024)})) %all-reduce.36.cloned.1.call-update) | async-done | bytes 331792 | tf_op jit(solution)/shard_map/psum | solution.py:159
  130.7 1.5 fusion.63
  132.3 2.2 pad_maximum_fusion
  134.5 40.1 %copy.98 = bf16[4,4,41472]{1,0,2:T(4,128)(2,1)} copy(bf16[4,4,41472]{2,1,0:T(4,128)(2,1)S(1)} %pad_maximum_fusion) | data formatting | bytes 2654208 | tf_op jit(solution)/shard_map/stack | solution.py:176
  174.6 80.2 %reshape.812 = bf16[32,2,10368]{2,1,0:T(2,128)(2,1)} reshape(bf16[41472,4,4]{2,1,0:T(4,128)(2,1)} %bitcast.379) | data formatting | bytes 2654208
  254.8 17.3 %all-to-all-start = ((bf16[32,2,10368]{2,1,0:T(2,128)(2,1)}), bf16[32,2,10368]{2,1,0:T(2,128)(2,1)}, u32[]{:S(2)}, u32[]{:S(2)}) async-start(bf16[32,2,10368]{2,1,0:T(2,128)(2,1)} %reshape.812), calls=%async_computation | async-start | bytes 2654208 | tf_op jit(solution)/shard_map/all_to_all | solution.py:177
  276.4 14.9 %all-to-all-done = bf16[32,2,10368]{2,1,0:T(2,128)(2,1)} async-done(((bf16[32,2,10368]{2,1,0:T(2,128)(2,1)}), bf16[32,2,10368]{2,1,0:T(2,128)(2,1)}, u32[]{:S(2)}, u32[]{:S(2)}) %all-to-all-start) | async-done | bytes 1327136 | tf_op jit(solution)/shard_map/all_to_all | solution.py:177
  291.3 95.6 %reshape.813 = bf16[41472,4,4]{2,1,0:T(4,128)(2,1)} reshape(bf16[32,2,10368]{2,1,0:T(2,128)(2,1)} %all-to-all-done) | data formatting | bytes 2654208
  386.9 60.7 %copy.99 = bf16[4,4,32,1296]{3,1,2,0:T(4,128)(2,1)S(1)} copy(bf16[4,4,32,1296]{1,0,3,2:T(4,128)(2,1)} %bitcast.380) | data formatting | bytes 2654208 | tf_op jit(solution)/shard_map/all_to_all | solution.py:177
  447.7 1.4 fusion.156
  454.6 2.3 add_convert_fusion.5
  456.9 2.2 reshape.785
  459.1 2.2 copy.100
  461.3 1.7 fusion.158
  463.5 6.8 fusion.2
  470.4 2.0 convert_reduce_fusion
  472.3 1.5 fusion.39
  483.9 2.7 copy.109
  486.6 6.3 all-to-all-start.3
  493.0 1.5 fusion.85
  494.5 2.0 fusion.159
  496.6 2.9 fusion.151
  499.4 1.6 fusion.152
  501.1 1.7 fusion.163
  502.8 10.9 %all-to-all-done.3 = bf16[4,128,1296]{2,0,1:T(4,128)(2,1)} async-done(((bf16[4,128,1296]{2,0,1:T(4,128)(2,1)}), bf16[4,128,1296]{2,0,1:T(4,128)(2,1)}, u32[]{:S(2)}, u32[]{:S(2)}) %all-to-all-start.3) | async-done | bytes 1327136 | tf_op jit(solution)/shard_map/all_to_all | solution.py:258
  513.7 1.7 convert_bitcast_fusion
  515.4 3.0 fusion.155
  518.4 1.5 squeeze.76
  520.0 1.5 squeeze.77
  521.7 1.6 squeeze.75
  523.3 2.0 broadcast_select_fusion
  525.5 5.8 multiply_reduce_fusion
  535.4 1.9 fusion.35
  538.2 5.7 all-to-all-start.1
  545.4 9.0 all-to-all-done.1
  557.3 72.6 %all-reduce.38.cloned.1.call-done = (bf16[41472]{0:T(1024)(128)(2,1)}, bf16[41472]{0:T(1024)(128)(2,1)}) async-done(((bf16[41472]{0:T(1024)(128)(2,1)}, bf16[41472]{0:T(1024)(128)(2,1)}), (bf16[41472]{0:T(1024)(128)(2,1)}, bf16[41472]{0:T(1024)(128)(2,1)})) %all-reduce.38.cloned.1.call-update) | async-done | bytes 165904 | tf_op jit(solution)/shard_map/psum | solution.py:274
  631.7 1.5 add_multiply_fusion
  633.3 158.0 %all-reduce.34.cloned.1.call-done = (f32[128,128]{1,0:T(8,128)}, f32[128,128]{1,0:T(8,128)}, f32[128,128]{1,0:T(8,128)}, f32[128,128]{1,0:T(8,128)}, f32[128,512...) async-done(((f32[128,128]{1,0:T(8,128)}, f32[128,128]{1,0:T(8,128)}, f32[128,128]{1,0:T(8,128)}, f32[128,128]{1,0:T(8,128)}, f32[128,512]{1,0:T(8,128)}, ...) | async-done | bytes 2261008 | tf_op jit(solution)/shard_map/psum | solution.py:296
  791.3 156.1 %all-reduce.32.cloned.1.call-done = (f32[128]{0:T(128)}, f32[128]{0:T(128)}, f32[128]{0:T(128)}, f32[128]{0:T(128)}, f32[128,32]{0,1:T(8,128)}, /*index=5*/f32[3...) async-done(((f32[128]{0:T(128)}, f32[128]{0:T(128)}, ...) | async-done | bytes 74640 | tf_op jit(solution)/shard_map/psum | solution.py:296
  949.7 1.5 copy.157
  952.4 1.5 copy.159
  955.0 1.5 copy.161
  961.6 1.5 copy.166
  966.5 1.7 copy.170
  969.4 1.7 copy.172
  (385 shorter events, 64.3 us)
Async XLA Ops:
  7.2 456.3 %copy-start = (bf16[128,512]{1,0:T(8,128)(2,1)S(1)}, bf16[128,512]{1,0:T(8,128)(2,1)}, u32[]{:S(2)}) copy-start(bf16[128,512]{1,0:T(8,128)(2,1)} %param.43) | copy-start | bytes 393220
  7.2 15.0 %copy-start.1 = (bf16[4,41472]{1,0:T(4,128)(2,1)S(1)}, bf16[4,41472]{1,0:T(4,128)(2,1)}, u32[]{:S(2)}) copy-start(bf16[4,41472]{1,0:T(4,128)(2,1)} %param.25) | copy-start | bytes 995332
  7.2 16.6 %copy-start.97 = (s32[2,128]{1,0:T(2,128)S(1)}, s32[2,128]{1,0:T(2,128)}, u32[]{:S(2)}) copy-start(s32[2,128]{1,0:T(2,128)} %param.27) | copy-start | bytes 3076
  9.4 19.8 %copy-start.106 = (bf16[128]{0:T(256)(128)(2,1)S(1)}, bf16[128]{0:T(256)(128)(2,1)}, u32[]{:S(2)}) copy-start(bf16[128]{0:T(256)(128)(2,1)} %param.28) | copy-start | bytes 772
  9.4 19.9 %copy-start.107 = (bf16[128]{0:T(256)(128)(2,1)S(1)}, bf16[128]{0:T(256)(128)(2,1)}, u32[]{:S(2)}) copy-start(bf16[128]{0:T(256)(128)(2,1)} %param.29) | copy-start | bytes 772
  9.4 20.0 %copy-start.108 = (bf16[128]{0:T(256)(128)(2,1)S(1)}, bf16[128]{0:T(256)(128)(2,1)}, u32[]{:S(2)}) copy-start(bf16[128]{0:T(256)(128)(2,1)} %param.31) | copy-start | bytes 772
  9.5 20.5 %copy-start.109 = (bf16[128]{0:T(256)(128)(2,1)S(1)}, bf16[128]{0:T(256)(128)(2,1)}, u32[]{:S(2)}) copy-start(bf16[128]{0:T(256)(128)(2,1)} %param.33) | copy-start | bytes 772
  9.5 20.5 %copy-start.110 = (bf16[128]{0:T(256)(128)(2,1)S(1)}, bf16[128]{0:T(256)(128)(2,1)}, u32[]{:S(2)}) copy-start(bf16[128]{0:T(256)(128)(2,1)} %param.40) | copy-start | bytes 772
  9.5 21.0 %copy-start.111 = (bf16[128]{0:T(256)(128)(2,1)S(1)}, bf16[128]{0:T(256)(128)(2,1)}, u32[]{:S(2)}) copy-start(bf16[128]{0:T(256)(128)(2,1)} %param.41) | copy-start | bytes 772
  9.5 21.5 %copy-start.112 = (bf16[128]{0:T(256)(128)(2,1)S(1)}, bf16[128]{0:T(256)(128)(2,1)}, u32[]{:S(2)}) copy-start(bf16[128]{0:T(256)(128)(2,1)} %param.42) | copy-start | bytes 772
  9.5 22.0 %copy-start.95 = (bf16[512]{0:T(512)(128)(2,1)S(1)}, bf16[512]{0:T(512)(128)(2,1)}, u32[]{:S(2)}) copy-start(bf16[512]{0:T(512)(128)(2,1)} %param.44) | copy-start | bytes 3076
  9.5 22.6 %copy-start.45 = (bf16[320,9,128]{2,0,1:T(8,128)(2,1)S(1)}, bf16[320,9,128]{2,0,1:T(8,128)(2,1)}, u32[]{:S(2)}) copy-start(bf16[320,9,128]{2,0,1:T(8,128)(2,1)} %param.47) | copy-start | bytes 2211844
  11.0 22.2 %copy-start.113 = (bf16[128]{0:T(256)(128)(2,1)S(1)}, bf16[128]{0:T(256)(128)(2,1)}, u32[]{:S(2)}) copy-start(bf16[128]{0:T(256)(128)(2,1)} %param.46) | copy-start | bytes 772
  11.0 22.7 %copy-start.96 = (bf16[320]{0:T(512)(128)(2,1)S(1)}, bf16[320]{0:T(512)(128)(2,1)}, u32[]{:S(2)}) copy-start(bf16[320]{0:T(512)(128)(2,1)} %param.48) | copy-start | bytes 1924
  11.0 243.9 %all-to-all-start.2 = ((bf16[10,32,324]{2,0,1:T(8,128)(2,1)}), bf16[10,32,324]{2,0,1:T(8,128)(2,1)S(1)}, u32[]{:S(2)}, u32[]{:S(2)}) async-start(bf16[10,32,324]{2,0,1:T(8,128)(2,1)} %copy.105), calls=%async_computation.2 | async-start | bytes 786432 | tf_op jit(solution)/shard_map/all_to_all | solution.py:219
  20.7 108.1 %all-reduce.36.cloned.1.call-start = ((), (), s32[]{:S(2)}) async-start(), calls=%async_computation.6 | async-start | bytes 671744 | tf_op jit(solution)/shard_map/psum | solution.py:159
  22.2 108.0 %copy-start.8 = (f32[41472]{0:T(1024)}, f32[41472]{0:T(1024)S(1)}, u32[]{:S(2)}) copy-start(f32[41472]{0:T(1024)S(1)} %get-tuple-element.105) | copy-start | bytes 497668
  23.9 106.7 %copy-start.75 = (pred[4]{0:T(512)(128)(4,1)}, pred[4]{0:T(512)(128)(4,1)S(1)}, u32[]{:S(2)}) copy-start(pred[4]{0:T(512)(128)(4,1)S(1)} %get-tuple-element.110) | copy-start | bytes 16
  23.9 106.7 %copy-start.77 = (pred[4]{0:T(512)(128)(4,1)}, pred[4]{0:T(512)(128)(4,1)S(1)}, u32[]{:S(2)}) copy-start(pred[4]{0:T(512)(128)(4,1)S(1)} %get-tuple-element.111) | copy-start | bytes 16
  23.9 106.7 %copy-start.79 = (pred[4]{0:T(512)(128)(4,1)}, pred[4]{0:T(512)(128)(4,1)S(1)}, u32[]{:S(2)}) copy-start(pred[4]{0:T(512)(128)(4,1)S(1)} %get-tuple-element.112) | copy-start | bytes 16
  23.9 106.7 %copy-start.81 = (pred[4]{0:T(512)(128)(4,1)}, pred[4]{0:T(512)(128)(4,1)S(1)}, u32[]{:S(2)}) copy-start(pred[4]{0:T(512)(128)(4,1)S(1)} %get-tuple-element.113) | copy-start | bytes 16
  23.9 106.7 %copy-start.83 = (pred[4]{0:T(512)(128)(4,1)}, pred[4]{0:T(512)(128)(4,1)S(1)}, u32[]{:S(2)}) copy-start(pred[4]{0:T(512)(128)(4,1)S(1)} %get-tuple-element.114) | copy-start | bytes 16
  24.0 106.7 %copy-start.85 = (pred[4]{0:T(512)(128)(4,1)}, pred[4]{0:T(512)(128)(4,1)S(1)}, u32[]{:S(2)}) copy-start(pred[4]{0:T(512)(128)(4,1)S(1)} %get-tuple-element.115) | copy-start | bytes 16
  24.0 106.7 %copy-start.71 = (s32[4]{0:T(128)}, s32[4]{0:T(128)S(1)}, u32[]{:S(2)}) copy-start(s32[4]{0:T(128)S(1)} %get-tuple-element.108) | copy-start | bytes 52
  24.0 106.7 %copy-start.73 = (s32[4]{0:T(128)}, s32[4]{0:T(128)S(1)}, u32[]{:S(2)}) copy-start(s32[4]{0:T(128)S(1)} %get-tuple-element.109) | copy-start | bytes 52
  24.2 106.5 %copy-start.37 = (s32[41472]{0:T(1024)}, s32[41472]{0:T(1024)S(1)}, u32[]{:S(2)}) copy-start(s32[41472]{0:T(1024)S(1)} %add_select_fusion.3) | copy-start | bytes 497668
  24.3 106.4 %copy-start.39 = (s32[41472]{0:T(1024)}, s32[41472]{0:T(1024)S(1)}, u32[]{:S(2)}) copy-start(s32[41472]{0:T(1024)S(1)} %add_select_fusion.5) | copy-start | bytes 497668
  24.4 249.6 %copy-start.61 = (pred[324]{0:T(512)(128)(4,1)}, pred[324]{0:T(512)(128)(4,1)S(1)}, u32[]{:S(2)}) copy-start(pred[324]{0:T(512)(128)(4,1)S(1)} %fusion.131) | copy-start | bytes 976
  27.9 245.9 %copy-start.63 = (pred[324]{0:T(512)(128)(4,1)}, pred[324]{0:T(512)(128)(4,1)S(1)}, u32[]{:S(2)}) copy-start(pred[324]{0:T(512)(128)(4,1)S(1)} %fusion.139) | copy-start | bytes 976
  29.3 102.9 %copy-start.65 = (f32[4]{0:T(128)}, f32[4]{0:T(128)S(1)}, u32[]{:S(2)}) copy-start(f32[4]{0:T(128)S(1)} %dynamic_slice.13) | copy-start | bytes 52
  254.8 36.5 %all-to-all-start = ((bf16[32,2,10368]{2,1,0:T(2,128)(2,1)}), bf16[32,2,10368]{2,1,0:T(2,128)(2,1)}, u32[]{:S(2)}, u32[]{:S(2)}) async-start(bf16[32,2,10368]{2,1,0:T(2,128)(2,1)} %reshape.812), calls=%async_computation | async-start | bytes 2654208 | tf_op jit(solution)/shard_map/all_to_all | solution.py:177
  470.3 10.8 %copy-start.18 = (bf16[512,1296]{0,1:T(8,128)(2,1)}, bf16[512,1296]{0,1:T(8,128)(2,1)S(1)}, u32[]{:S(2)}) copy-start(bf16[512,1296]{0,1:T(8,128)(2,1)S(1)} %get-tuple-element.67) | copy-start | bytes 3981316
  477.3 66.7 %copy-start.54 = (f32[384]{0:T(512)}, f32[384]{0:T(512)S(1)}, u32[]{:S(2)}) copy-start(f32[384]{0:T(512)S(1)} %fusion.134) | copy-start | bytes 4612
  477.5 67.2 %copy-start.87 = (f32[32]{0:T(128)}, f32[32]{0:T(128)S(1)}, u32[]{:S(2)}) copy-start(f32[32]{0:T(128)S(1)} %multiply_add_fusion.2) | copy-start | bytes 388
  483.9 12.7 %copy-start.15 = (f32[128,1,18,2,18,2]{0,5,4,3,2,1:T(2,128)S(1)}, f32[128,1,18,2,18,2]{0,5,4,3,2,1:T(2,128)}, u32[]{:S(2)}) copy-start(f32[128,1,18,2,18,2]{0,5,4,3,2,1:T(2,128)} %copy.108) | copy-start | bytes 1990660
  486.6 12.8 %copy-start.17 = (bf16[512,1296]{0,1:T(8,128)(2,1)S(1)}, bf16[512,1296]{0,1:T(8,128)(2,1)}, u32[]{:S(2)}) copy-start(bf16[512,1296]{0,1:T(8,128)(2,1)} %copy-done.16) | copy-start | bytes 3981316
  486.6 12.8 %copy-start.70 = (f32[128]{0:T(128)S(1)}, f32[128]{0:T(128)}, u32[]{:S(2)}) copy-start(f32[128]{0:T(128)} %convert_element_type.278) | copy-start | bytes 1540
  486.6 12.8 %copy-start.102 = (f32[128]{0:T(128)S(1)}, f32[128]{0:T(128)}, u32[]{:S(2)}) copy-start(f32[128]{0:T(128)} %convert_element_type.279) | copy-start | bytes 1540
  486.6 27.0 %all-to-all-start.3 = ((bf16[4,128,1296]{2,0,1:T(4,128)(2,1)}), bf16[4,128,1296]{2,0,1:T(4,128)(2,1)}, u32[]{:S(2)}, u32[]{:S(2)}) async-start(bf16[4,128,1296]{2,0,1:T(4,128)(2,1)} %copy.109), calls=%async_computation.3 | async-start | bytes 2883584 | tf_op jit(solution)/shard_map/all_to_all | solution.py:258
  492.9 137.0 %all-reduce.38.cloned.1.call-start = ((), (), s32[]{:S(2)}) async-start(), calls=%async_computation.7 | async-start | bytes 335872 | tf_op jit(solution)/shard_map/psum | solution.py:274
  531.3 259.9 %all-reduce.34.cloned.1.call-start = ((), (), s32[]{:S(2)}) async-start(), calls=%async_computation.5 | async-start | bytes 4521984 | tf_op jit(solution)/shard_map/psum | solution.py:296
  533.4 11.3 %copy-start.94 = (f32[128]{0:T(128)S(1)}, f32[128]{0:T(128)}, u32[]{:S(2)}) copy-start(f32[128]{0:T(128)} %copy-done.93) | copy-start | bytes 1540
  534.7 20.9 %copy-start.32 = (f32[1,4,32,1296]{3,0,1,2:T(1,128)S(1)}, f32[1,4,32,1296]{3,0,1,2:T(1,128)}, u32[]{:S(2)}) copy-start(f32[1,4,32,1296]{3,0,1,2:T(1,128)} %get-tuple-element.76) | copy-start | bytes 1990660
  538.2 93.5 %copy-start.33 = (f32[4,41472]{1,0:T(4,128)S(1)}, f32[4,41472]{1,0:T(4,128)}, u32[]{:S(2)}) copy-start(f32[4,41472]{1,0:T(4,128)} %get-tuple-element.64) | copy-start | bytes 1990660
  538.2 16.1 %all-to-all-start.1 = ((bf16[32,10,324]{2,1,0:T(8,128)(2,1)}), bf16[32,10,324]{2,1,0:T(8,128)(2,1)S(1)}, u32[]{:S(2)}, u32[]{:S(2)}) async-start(bf16[32,10,324]{2,1,0:T(8,128)(2,1)} %all_to_all.49), calls=%async_computation.1 | async-start | bytes 786432 | tf_op jit(solution)/shard_map/all_to_all | solution.py:218
  543.9 403.5 %all-reduce.32.cloned.1.call-start = ((), (), s32[]{:S(2)}) async-start(), calls=%async_computation.4 | async-start | bytes 152576 | tf_op jit(solution)/shard_map/psum | solution.py:296
  791.3 181.0 %copy-start.41 = (f32[320,9,128]{2,0,1:T(8,128)S(1)}, f32[320,9,128]{2,0,1:T(8,128)}, u32[]{:S(2)}) copy-start(f32[320,9,128]{2,0,1:T(8,128)} %get-tuple-element.146) | copy-start | bytes 4423684
  947.4 25.9 %copy-start.92 = (f32[320]{0:T(512)S(1)}, f32[320]{0:T(512)}, u32[]{:S(2)}) copy-start(f32[320]{0:T(512)} %get-tuple-element.147) | copy-start | bytes 3844
  (77 other events, 230.5 us)
Sparse Core Ops, SparseCore 0:
  25.5 103.1 all-reduce.35
  531.5 98.4 all-reduce.37
  638.8 152.4 all-reduce.33
  799.3 148.1 all-reduce.31
where the time goes:
time: 988 us; the launch traced here: 981 us
  waiting for transfers between devices  514 us (52%)
  local copies, waits for them, and re-layouts  335 us (34%)
  other arithmetic  45 us (5%)
  starting transfers between devices  39.2 us (4%)
  matrix products  30.9 us (3%)
  between operations  17 us (2%)
    psum x2, waiting for transfers between devices, body(): lax.psum((gain_part, bias_part, height_grad, height_bias_grad, width_grad...  314 us
    unnamed x261, local copies, waits for them, and re-layouts  207 us
    psum x1, waiting for transfers between devices, body(): lax.psum((jnp.sum(masked_cast, axis=0), jnp.sum(masked_cast * masked_cast...  92.3 us
    psum x1, waiting for transfers between devices, body(): lax.psum(jnp.sum(normalized_gradient * centered_scaled_input, axis=0).ast...  72.6 us
    all_to_all x1, local copies, waits for them, and re-layouts, body(): lax.all_to_all(payload, 'ch', split_axis=2, concat_axis=1, tiled=True)  60.7 us
    another operation x1, local copies, waits for them, and re-layouts, body(): payload = jnp.stack([input_b, rows_c, cols_c, normed_cast])  40.1 us
  transfers between devices with their start and end apart: 8, of which 7 were waited for; matrix products, arithmetic and copies ran while one was open for 17% of the time, Pallas kernels for 0%

commit v1 on v0

v1 whole, which is shorter than its diff:
```python
import jax
import jax.numpy as jnp
from jax import lax
from jax.experimental import pallas as pl
from jax.experimental.pallas import tpu as pltpu
from jax.sharding import PartitionSpec as P

CH = 128
FF = 512
RED = 32
OUT = 320
SIDE = 36
PIX = SIDE * SIDE
HALF = SIDE // 2
OPIX = HALF * HALF
WIDE = 40
FLAT = SIDE * WIDE
GUARD = 48
ROWS = 288
STEPS = FLAT // ROWS
EPS = 1e-05
LANES = 128
WIN = 11
OTILE = 3
PIXROWS = 80
WROWS = 144
CHUNK = PIXROWS + WROWS
VMEM = 56 * 1024 * 1024

F32 = jnp.float32
BF16 = jnp.bfloat16

AT_CONV = 0
AT_REDUCE = 2880
AT_EXPAND = 3392
AT_HEIGHT = 3904
AT_WIDTH = 4032
AT_CHANNEL = 4160
AT_OUTPUT = 4288
AT_SQUEEZE = 4416
AT_EXCITE = 4448
AT_SQ_BIAS = 4544
AT_VECTOR = 4576


def params(**kw):
    return pltpu.CompilerParams(vmem_limit_bytes=VMEM, **kw)


def first_tile(k):
    return 10 * k + k // 8


def nn(a, b):
    return lax.dot_general(a, b, (((1,), (0,)), ((), ())), preferred_element_type=F32)


def nt(a, b):
    return lax.dot_general(a, b, (((1,), (1,)), ((), ())), preferred_element_type=F32)


def tn(a, b):
    return lax.dot_general(a, b, (((0,), (0,)), ((), ())), preferred_element_type=F32)


def lane_mean(v):
    return jnp.sum(v, axis=1, keepdims=True) * (1.0 / CH)


def col_sum(v):
    return jnp.sum(v, axis=0, keepdims=True)


def normal_parts(x):
    z = jnp.abs(x) * 0.7071067811865476
    t = 1.0 / (1.0 + 0.3275911 * z)
    bell = jnp.exp(-z * z)
    poly = 1.061405429 * t - 1.453152027
    poly = poly * t + 1.421413741
    poly = poly * t - 0.284496736
    poly = poly * t + 0.254829592
    tail = 0.5 * poly * t * bell
    return jnp.where(x < 0, tail, 1.0 - tail), bell * 0.3989422804014327


def pack_kernel(feat, cot, out, stage, cots):
    images = out.shape[0]
    cots[...] = cot[...].astype(F32)
    for k in range(images):
        base = k * PIXROWS
        begin = first_tile(k) * LANES
        for t in range(WIN):
            stage[base + 4 * t : base + 4 * t + 4, :] = feat[
                :, begin + t * LANES : begin + (t + 1) * LANES
            ].astype(F32)
        for j in range(OTILE):
            width = min(LANES, OPIX - j * LANES)
            at = k * OPIX + j * LANES
            row = base + 44 + 10 * j
            stage[row : row + 10, 0:width] = cots[:, at : at + width]
        out[k] = stage[base : base + PIXROWS, :].astype(BF16)


def main_kernel(
    info,
    recv,
    vecs,
    sqt,
    sqb,
    exw,
    kbias,
    hw,
    ww,
    cw,
    ow,
    xw,
    rw,
    kw,
    out,
    xf,
    cf,
    tall,
    canvas,
    valid,
    xhat,
    rstd,
    norm,
    rows_b,
    cols_b,
    norm_b,
    branch_h,
    branch_w,
    branch_c,
    mixed_b,
    xhat2,
    rstd2,
    norm2_b,
    hidden_b,
    slope,
    block,
    taps,
    spread,
    planes,
    gblock,
    gresid,
    gmixed,
    grows,
    gcols,
    gnorm,
    acc_r,
    acc_x,
    acc_s,
    sums,
    stage,
    gpre_b,
):
    shift = info[0]
    side = info[1]

    def vec(i):
        return vecs[i : i + 1, :]

    def put(row, value):
        value = value.astype(BF16)
        count = value.shape[0]
        done = 0
        while done < count:
            chunk, inner = divmod(row + done, WROWS)
            size = min(count - done, WROWS - inner)
            out[chunk, PIXROWS + inner : PIXROWS + inner + size, :] = value[done : done + size, :]
            done += size

    cf[...] = jnp.zeros_like(cf)
    for s in range(recv.shape[0]):
        piece = recv[s].astype(F32)
        for t in range(WIN):
            xf[4 * s : 4 * s + 4, t * LANES : (t + 1) * LANES] = piece[4 * t : 4 * t + 4, :]
        for j in range(OTILE):
            cf[10 * s : 10 * s + 10, j * LANES : (j + 1) * LANES] = piece[
                44 + 10 * j : 54 + 10 * j, :
            ]
    begin = pl.multiple_of(112 - shift, 16)
    for t in range(WIN):
        tall[pl.ds(begin + t * LANES, LANES), :] = xf[:, t * LANES : (t + 1) * LANES].T

    column = lax.broadcasted_iota(jnp.int32, (WIDE, CH), 0)
    for r in range(SIDE):
        keep = (column < side) & (r < side)
        canvas[r * WIDE : (r + 1) * WIDE, :] = jnp.where(
            keep, tall[112 + r * SIDE : 112 + r * SIDE + WIDE, :], 0.0
        )
        valid[r * WIDE : (r + 1) * WIDE, :] = jnp.where(keep, 1.0, 0.0)
    edge = jnp.zeros((GUARD, CH), F32)
    for ref in (norm, block, grows, gcols):
        ref[0:GUARD, :] = edge
        ref[GUARD + FLAT : FLAT + 2 * GUARD, :] = edge
    acc_r[...] = jnp.zeros_like(acc_r)
    acc_x[...] = jnp.zeros_like(acc_x)
    acc_s[...] = jnp.zeros_like(acc_s)
    sums[...] = jnp.zeros_like(sums)

    def rows_at(i):
        return pl.ds(pl.multiple_of(i * ROWS, 16), ROWS)

    def guarded(i, extra=0, size=ROWS):
        return pl.ds(pl.multiple_of(i * ROWS + GUARD + extra, 8), size)

    def first_norm(i, carry):
        here = rows_at(i)
        x = canvas[here, :]
        center = x - lane_mean(x)
        scale = lax.rsqrt(lane_mean(center * center) + EPS)
        unit = center * scale
        xhat[here, :] = unit
        rstd[here, :] = jnp.broadcast_to(scale, unit.shape)
        value = jnp.where(valid[here, :] > 0, unit * vec(0) + vec(1), 0.0)
        norm[guarded(i), :] = value.astype(BF16).astype(F32)
        return carry

    lax.fori_loop(0, STEPS, first_norm, 0)

    def near(ref, i):
        wide = ref[guarded(i, -8, ROWS + 16), :]
        back = pltpu.roll(wide, 1, 0)[8 : 8 + ROWS, :]
        ahead = pltpu.roll(wide, ROWS + 15, 0)[8 : 8 + ROWS, :]
        return back, ahead

    def branches(i, total):
        here = rows_at(i)
        plain = norm[guarded(i), :]
        above = norm[guarded(i, -WIDE), :]
        below = norm[guarded(i, WIDE), :]
        left, right = near(norm, i)
        by_row = vec(15)
        by_col = vec(16)
        sr = jnp.where(by_row < 0, above, jnp.where(by_row > 0, below, plain)).astype(BF16)
        sc = jnp.where(by_col < 0, left, jnp.where(by_col > 0, right, plain)).astype(BF16)
        nb = plain.astype(BF16)
        rows_b[here, :] = sr
        cols_b[here, :] = sc
        norm_b[here, :] = nb
        bh = nn(sr, hw[...]) + vec(2)
        bw = nn(sc, ww[...]) + vec(3)
        bc = nn(nb, cw[...])
        branch_h[here, :] = bh
        branch_w[here, :] = bw
        branch_c[here, :] = bc
        return total + col_sum(valid[here, :] * (bh + bw + bc))

    total = lax.fori_loop(0, STEPS, branches, jnp.zeros((1, CH), F32))

    count = jnp.full((1, CH), side * side, jnp.int32).astype(F32)
    means = total / count
    inner_pre = jnp.sum(sqt[...] * means, axis=1, keepdims=True) + sqb[...]
    inner_cdf, inner_density = normal_parts(inner_pre)
    inner = inner_pre * inner_cdf
    inner_slope = inner_cdf + inner_pre * inner_density
    logit = [col_sum(exw[:, j * CH : (j + 1) * CH] * inner) + vec(12 + j) for j in range(3)]
    top = jnp.maximum(jnp.maximum(logit[0], logit[1]), logit[2])
    grown = [jnp.exp(v - top) for v in logit]
    whole = grown[0] + grown[1] + grown[2]
    mix = [v / whole for v in grown]

    def forward(i, carry):
        here = rows_at(i)
        mixed = mix[0] * branch_h[here, :] + mix[1] * branch_w[here, :] + mix[2] * branch_c[here, :]
        mixed = mixed.astype(BF16)
        mixed_b[here, :] = mixed
        resid = canvas[here, :] + nn(mixed, ow[...]) + vec(4)
        center = resid - lane_mean(resid)
        scale = lax.rsqrt(lane_mean(center * center) + EPS)
        unit = center * scale
        xhat2[here, :] = unit
        rstd2[here, :] = jnp.broadcast_to(scale, unit.shape)
        n2 = (unit * vec(5) + vec(6)).astype(BF16)
        norm2_b[here, :] = n2
        total2 = resid + vec(7)
        for j in range(FF // CH):
            lanes = slice(j * CH, (j + 1) * CH)
            pre = nn(n2, xw[:, lanes]) + vec(8 + j)
            cdf, density = normal_parts(pre)
            hid = (pre * cdf).astype(BF16)
            hidden_b[here, lanes] = hid
            slope[here, lanes] = cdf + pre * density
        total2 = total2 + nn(hidden_b[here, :], rw[...])
        value = jnp.where(valid[here, :] > 0, total2, 0.0)
        block[guarded(i), :] = value.astype(BF16).astype(F32)
        return carry

    lax.fori_loop(0, STEPS, forward, 0)

    taps[OPIX:, :] = jnp.zeros((taps.shape[0] - OPIX, taps.shape[1]), F32)
    for a in range(3):
        for b in range(3):
            lanes = slice((3 * a + b) * CH, (3 * a + b + 1) * CH)
            for i in range(HALF):
                at = GUARD + (2 * i + a - 1) * WIDE + b - 1
                taps[i * HALF : (i + 1) * HALF, lanes] = block[pl.ds(at, HALF, stride=2), :]
    tap_b = taps[...].astype(BF16)
    index = lax.broadcasted_iota(jnp.int32, (1, OTILE * LANES), 1)
    out_row = ((index.astype(F32) + 0.5) * (1.0 / HALF)).astype(jnp.int32)
    out_col = index - out_row * HALF
    out_keep = (2 * out_row < side) & (2 * out_col < side)
    cot = jnp.where(out_keep, cf[...], 0.0)
    cot_b = cot[0:OUT, :].astype(BF16)
    cot_t = cot.T.astype(BF16)[:, 0:OUT]
    section = nt(kw[...], tap_b) + kbias[...]
    section = jnp.where(out_keep, section, 0.0)
    conv = nn(cot_b, tap_b)
    for t in range(9):
        put(AT_CONV + t * OUT, conv[:, t * CH : (t + 1) * CH])
    kb_rows = jnp.sum(cot, axis=1, keepdims=True)
    spread[...] = nn(cot_t, kw[...])
    row_id = lax.broadcasted_iota(jnp.int32, (OPIX, CH), 0)
    row_of = ((row_id.astype(F32) + 0.5) * (1.0 / HALF)).astype(jnp.int32)
    inside = row_id - row_of * HALF < HALF - 1

    def part(tap, ahead, masked):
        value = spread[ahead : ahead + OPIX, tap * CH : (tap + 1) * CH]
        return jnp.where(inside, value, 0.0) if masked else value

    found = (
        part(4, 0, False),
        part(5, 0, False) + part(3, 1, True),
        part(7, 0, False) + part(1, HALF, False),
        (part(8, 0, False) + part(6, 1, True)) + (part(2, HALF, False) + part(0, HALF + 1, True)),
    )
    for p in range(4):
        planes[p, 0:OPIX, :] = found[p]
        for i in range(HALF):
            at = (2 * i + p // 2) * WIDE + p % 2
            gblock[pl.ds(at, HALF, stride=2), :] = planes[p, i * HALF : (i + 1) * HALF, :]

    def add(row, value):
        sums[row : row + 1, :] += value

    def backward(i, carry):
        here = rows_at(i)
        gb = jnp.where(valid[here, :] > 0, gblock[here, :], 0.0)
        gred = gb.astype(BF16)
        add(7, col_sum(gred.astype(F32)))
        acc_r[...] += tn(gred, hidden_b[here, :])
        n2 = norm2_b[here, :]
        for j in range(FF // CH):
            lanes = slice(j * CH, (j + 1) * CH)
            gpre = (nt(gred, rw[lanes, :]) * slope[here, lanes]).astype(BF16)
            add(8 + j, col_sum(gpre.astype(F32)))
            gpre_b[:, lanes] = gpre
        acc_x[...] += tn(n2, gpre_b[...])
        gn2 = nt(gpre_b[...], xw[...])
        unit = xhat2[here, :]
        add(5, col_sum(gn2 * unit))
        add(6, col_sum(gn2))
        gy = gn2 * vec(5)
        gr = gb + rstd2[here, :] * (gy - lane_mean(gy) - unit * lane_mean(gy * unit))
        gresid[here, :] = gr
        gproj = gr.astype(BF16)
        add(4, col_sum(gproj.astype(F32)))
        acc_s[3] += tn(mixed_b[here, :], gproj)
        gm = nt(gproj, ow[...])
        gmixed[here, :] = gm
        add(20, col_sum(gm * branch_h[here, :]))
        add(21, col_sum(gm * branch_w[here, :]))
        add(22, col_sum(gm * branch_c[here, :]))
        return carry

    lax.fori_loop(0, STEPS, backward, 0)

    gmix = [sums[20 + j : 21 + j, :] for j in range(3)]
    inner_dot = mix[0] * gmix[0] + mix[1] * gmix[1] + mix[2] * gmix[2]
    glogit = [mix[j] * (gmix[j] - inner_dot) for j in range(3)]
    ginner = jnp.zeros((RED, 1), F32)
    for j in range(3):
        ginner += jnp.sum(exw[:, j * CH : (j + 1) * CH] * glogit[j], axis=1, keepdims=True)
        put(AT_EXCITE + RED * j, inner * glogit[j])
        sums[12 + j : 13 + j, :] = glogit[j]
    ginner = ginner * inner_slope
    put(AT_SQUEEZE, ginner * means)
    put(AT_SQ_BIAS, jnp.broadcast_to(ginner, (RED, CH)))
    gmeans = col_sum(sqt[...] * ginner) / count

    def branch_back(i, carry):
        here = rows_at(i)
        gm = gmixed[here, :]
        level = valid[here, :] * gmeans
        gh = (mix[0] * gm + level).astype(BF16)
        gw = (mix[1] * gm + level).astype(BF16)
        gc = (mix[2] * gm + level).astype(BF16)
        add(2, col_sum(gh.astype(F32)))
        add(3, col_sum(gw.astype(F32)))
        acc_s[0] += tn(rows_b[here, :], gh)
        acc_s[1] += tn(cols_b[here, :], gw)
        acc_s[2] += tn(norm_b[here, :], gc)
        grows[guarded(i), :] = nt(gh, hw[...])
        gcols[guarded(i), :] = nt(gw, ww[...])
        gnorm[here, :] = nt(gc, cw[...])
        return carry

    lax.fori_loop(0, STEPS, branch_back, 0)

    def last(i, carry):
        here = rows_at(i)
        by_row = vec(15)
        by_col = vec(16)
        plain = grows[guarded(i), :]
        above = grows[guarded(i, -WIDE), :]
        below = grows[guarded(i, WIDE), :]
        left, right = near(gcols, i)
        level = gcols[guarded(i), :]
        value = (
            gnorm[here, :]
            + jnp.where(by_row < 0, below, jnp.where(by_row > 0, above, plain))
            + jnp.where(by_col < 0, right, jnp.where(by_col > 0, left, level))
        )
        keep = valid[here, :] > 0
        value = jnp.where(keep, value, 0.0)
        unit = xhat[here, :]
        add(0, col_sum(value * unit))
        add(1, col_sum(value))
        gy = value * vec(0)
        back = rstd[here, :] * (gy - lane_mean(gy) - unit * lane_mean(gy * unit))
        canvas[here, :] = jnp.where(keep, gresid[here, :] + back, 0.0)
        return carry

    lax.fori_loop(0, STEPS, last, 0)

    tall[0:112, :] = jnp.zeros((112, CH), F32)
    tall[112 + PIX :, :] = jnp.zeros((tall.shape[0] - 112 - PIX, CH), F32)
    for r in range(SIDE):
        tall[112 + r * SIDE : 112 + (r + 1) * SIDE, :] = canvas[r * WIDE : r * WIDE + SIDE, :]
    for t in range(WIN):
        xf[:, t * LANES : (t + 1) * LANES] = tall[pl.ds(begin + t * LANES, LANES), :].T
    cf[0:OUT, :] = section
    for s in range(recv.shape[0]):
        for t in range(WIN):
            stage[4 * t : 4 * t + 4, :] = xf[4 * s : 4 * s + 4, t * LANES : (t + 1) * LANES]
        for j in range(OTILE):
            stage[44 + 10 * j : 54 + 10 * j, :] = cf[
                10 * s : 10 * s + 10, j * LANES : (j + 1) * LANES
            ]
        out[s, 0:PIXROWS, :] = stage[...].astype(BF16)

    for j in range(FF // CH):
        put(AT_REDUCE + j * CH, acc_r[:, j * CH : (j + 1) * CH].T)
        put(AT_EXPAND + j * CH, acc_x[:, j * CH : (j + 1) * CH])
    for j, at in enumerate((AT_HEIGHT, AT_WIDTH, AT_CHANNEL, AT_OUTPUT)):
        put(at, acc_s[j])
    same = lax.broadcasted_iota(jnp.int32, (LANES, LANES), 0) == lax.broadcasted_iota(
        jnp.int32, (LANES, LANES), 1
    )
    for j in range(OTILE):
        add(15 + j, col_sum(jnp.where(same, kb_rows[j * LANES : (j + 1) * LANES, :], 0.0)))
    put(AT_VECTOR, sums[...])


def add_kernel(recv, out):
    total = recv[0, PIXROWS:, :].astype(F32)
    for s in range(1, recv.shape[0]):
        total += recv[s, PIXROWS:, :].astype(F32)
    out[...] = total.astype(BF16)


def pixel_kernel(recv, feat, section, stage):
    images = recv.shape[0]
    for k in range(images):
        piece = recv[k, 0:PIXROWS, :].astype(F32)
        tile = first_tile(k)
        for t in range(WIN):
            lanes = slice((tile + t) * LANES, (tile + t + 1) * LANES)
            value = piece[4 * t : 4 * t + 4, :]
            if t == 0 and k % 8:
                feat[:, lanes] += value
            else:
                feat[:, lanes] = value
        for j in range(OTILE):
            width = min(LANES, OPIX - j * LANES)
            at = k * OPIX + j * LANES
            stage[:, at : at + width] = piece[44 + 10 * j : 54 + 10 * j, 0:width]
    section[...] = stage[...].astype(BF16)


def weight_kernel(
    recv, conv, red, exp, height, width, chan, outw, squeeze, excite, sq_bias, vectors
):
    def rows(at, count):
        return recv[at : at + count, :].astype(F32)

    for t in range(9):
        conv[:, t, :] = rows(AT_CONV + t * OUT, OUT)
    red[...] = rows(AT_REDUCE, FF)
    for j in range(FF // CH):
        exp[:, j * CH : (j + 1) * CH] = rows(AT_EXPAND + j * CH, CH)
    for at, ref in (
        (AT_HEIGHT, height),
        (AT_WIDTH, width),
        (AT_CHANNEL, chan),
        (AT_OUTPUT, outw),
    ):
        ref[...] = rows(at, CH)
    squeeze[...] = rows(AT_SQUEEZE, RED).T
    for j in range(3):
        excite[:, j * CH : (j + 1) * CH] = rows(AT_EXCITE + j * RED, RED)
    sq_bias[...] = rows(AT_SQ_BIAS, RED).T[0:8, :]
    vectors[...] = rows(AT_VECTOR, RED)


def body(
    features,
    size_group,
    cycle_offsets,
    norm_gain,
    norm_bias,
    height_weight,
    height_bias,
    width_weight,
    width_bias,
    channel_weight,
    squeeze_weight,
    squeeze_bias,
    excite_weight,
    excite_bias,
    output_weight,
    output_bias,
    second_gain,
    second_bias,
    expand_weight,
    expand_bias,
    reduce_weight,
    reduce_bias,
    stride_weight,
    stride_bias,
    cotangent,
):
    shards = lax.axis_size("ch")
    rank = lax.axis_index("ch")
    side = SIDE - 4 * (2 - lax.dynamic_index_in_dim(size_group, rank, keepdims=False))
    info = jnp.stack([16 * (rank % 8), side]).astype(jnp.int32)
    vecs = jnp.concatenate(
        [
            v.astype(F32)
            for v in (
                norm_gain,
                norm_bias,
                height_bias,
                width_bias,
                output_bias,
                second_gain,
                second_bias,
                reduce_bias,
                expand_bias,
                excite_bias,
                cycle_offsets[0],
                cycle_offsets[1],
            )
        ]
    ).reshape(17, CH)

    chunks = pl.pallas_call(
        pack_kernel,
        out_shape=jax.ShapeDtypeStruct((shards, PIXROWS, LANES), BF16),
        scratch_shapes=[
            pltpu.VMEM((shards * PIXROWS, LANES), F32),
            pltpu.VMEM(cotangent.shape, F32),
        ],
        compiler_params=params(),
    )(features, cotangent)
    arrived = lax.all_to_all(chunks, "ch", split_axis=0, concat_axis=0, tiled=True)

    canvas = pltpu.VMEM((FLAT, CH), F32)
    guarded = pltpu.VMEM((FLAT + 2 * GUARD, CH), F32)
    narrow = pltpu.VMEM((FLAT, CH), BF16)
    whole = pl.BlockSpec(memory_space=pltpu.VMEM)
    made = pl.pallas_call(
        main_kernel,
        out_shape=jax.ShapeDtypeStruct((shards, CHUNK, LANES), BF16),
        in_specs=[pl.BlockSpec(memory_space=pltpu.SMEM)] + [whole] * 13,
        out_specs=whole,
        scratch_shapes=[
            pltpu.VMEM((CH, WIN * LANES), F32),
            pltpu.VMEM((3 * LANES, OTILE * LANES), F32),
            pltpu.VMEM((112 + WIN * LANES, CH), F32),
            canvas,
            canvas,
            canvas,
            canvas,
            guarded,
            narrow,
            narrow,
            narrow,
            canvas,
            canvas,
            canvas,
            narrow,
            canvas,
            canvas,
            narrow,
            pltpu.VMEM((FLAT, FF), BF16),
            pltpu.VMEM((FLAT, FF), F32),
            guarded,
            pltpu.VMEM((OTILE * LANES, 9 * CH), F32),
            pltpu.VMEM((OTILE * LANES, 9 * CH), F32),
            pltpu.VMEM((4, 328, CH), F32),
            canvas,
            canvas,
            canvas,
            guarded,
            guarded,
            canvas,
            pltpu.VMEM((CH, FF), F32),
            pltpu.VMEM((CH, FF), F32),
            pltpu.VMEM((4, CH, CH), F32),
            pltpu.VMEM((RED, CH), F32),
            pltpu.VMEM((PIXROWS, LANES), F32),
            pltpu.VMEM((ROWS, FF), BF16),
        ],
        compiler_params=params(),
    )(
        info,
        arrived,
        vecs,
        squeeze_weight.astype(F32).T,
        squeeze_bias.astype(F32)[:, None],
        excite_weight.astype(F32),
        stride_bias.astype(F32)[:, None],
        height_weight,
        width_weight,
        channel_weight,
        output_weight,
        expand_weight,
        reduce_weight,
        stride_weight.reshape(OUT, 9 * CH),
    )
    back = lax.all_to_all(made, "ch", split_axis=0, concat_axis=0, tiled=True)

    mine = pl.pallas_call(
        add_kernel,
        out_shape=jax.ShapeDtypeStruct((WROWS, LANES), BF16),
        compiler_params=params(),
    )(back)
    groups = lax.axis_size("img")
    other = [
        lax.ppermute(mine, "img", [(i, (i + d) % groups) for i in range(groups)]).astype(F32)
        for d in (1, 2, 3)
    ]
    owned = ((mine.astype(F32) + other[1]) + (other[0] + other[2])).astype(BF16)
    copies = jnp.broadcast_to(owned, (shards, WROWS, LANES))
    summed = lax.all_to_all(copies, "ch", split_axis=0, concat_axis=0, tiled=True)

    features_grad, section = pl.pallas_call(
        pixel_kernel,
        out_shape=(
            jax.ShapeDtypeStruct(features.shape, F32),
            jax.ShapeDtypeStruct(cotangent.shape, BF16),
        ),
        scratch_shapes=[pltpu.VMEM(cotangent.shape, F32)],
        compiler_params=params(),
    )(back)

    def like(*shape):
        return jax.ShapeDtypeStruct(shape, F32)

    (
        conv_grad,
        reduce_grad,
        expand_grad,
        height_grad,
        width_grad,
        channel_grad,
        output_grad,
        squeeze_grad,
        excite_grad,
        squeeze_rows,
        vectors,
    ) = pl.pallas_call(
        weight_kernel,
        out_shape=(
            like(OUT, 9, CH),
            like(FF, CH),
            like(CH, FF),
            like(CH, CH),
            like(CH, CH),
            like(CH, CH),
            like(CH, CH),
            like(CH, RED),
            like(RED, 3 * CH),
            like(8, RED),
            like(RED, CH),
        ),
        compiler_params=params(),
    )(summed.reshape(shards * WROWS, LANES))
    flat = vectors.reshape(RED * CH)

    def vector(row, count=CH):
        return flat[row * CH : row * CH + count]

    return (
        section,
        features_grad,
        vector(0),
        vector(1),
        height_grad,
        vector(2),
        width_grad,
        vector(3),
        channel_grad,
        squeeze_grad,
        squeeze_rows[0],
        excite_grad,
        vector(12, 3 * CH),
        output_grad,
        vector(4),
        vector(5),
        vector(6),
        expand_grad,
        vector(8, FF),
        reduce_grad,
        vector(7),
        conv_grad,
        vector(15, OUT),
    )


def solution(mesh):
    split = P("ch", "img")
    return jax.shard_map(
        body,
        mesh=mesh,
        in_specs=(split, P("img")) + (P(),) * 22 + (split,),
        out_specs=(split, split) + (P(),) * 21,
        check_vma=False,
    )
```

time: 988 us -> 131 us (0.13)
  waiting for transfers between devices: 514 us -> 23.5 us
  local copies, waits for them, and re-layouts: 335 us -> 19.1 us
  other arithmetic: 45 us -> 2.7 us
  Pallas kernels: 0 us -> 33.3 us
  matrix products: 30.9 us -> 0 us
  blocking collectives: 0 us -> 30.5 us
  starting transfers between devices: 39.2 us -> 19.2 us
  between operations: 17 us -> 1.7 us
    psum x4 -> x0, waiting for transfers between devices: 479 us -> none  [the longest x2 314 us: body(): lax.psum((gain_part, bias_part, height_grad, height_bias_grad, width_grad...]
    unnamed x261 -> x43, local copies, waits for them, and re-layouts: 207 us -> 7.88 us
    all_to_all x8 -> x0, local copies, waits for them, and re-layouts: 65.2 us -> none  [the longest x1 60.7 us: body(): lax.all_to_all(payload, 'ch', split_axis=2, concat_axis=1, tiled=True)]
    another operation x5 -> x0, local copies, waits for them, and re-layouts: 44.4 us -> none  [the longest x1 40.1 us: body(): payload = jnp.stack([input_b, rows_c, cols_c, normed_cast])]
    pallas_call x0 -> x5, Pallas kernels: none -> 33.3 us  [the longest x1 21.9 us: body(): pl.pallas_call(main_kernel, out_shape=jax.ShapeDtypeStruct((shards, CHUNK...]
    dot_general x29 -> x0, matrix products: 30.9 us -> none  [the longest x7 10.9 us: rdot(): lax.dot_general(left, right, (((1,), (1,)), ((), ())), preferred_element_...]
    all_to_all x0 -> x1, blocking collectives: none -> 30.5 us  [body(): back = lax.all_to_all(made, 'ch', split_axis=0, concat_axis=0, tiled=True)]
    all_to_all x4 -> x2, starting transfers between devices: 39 us -> 15 us  [the longest x1 9.6 us: body(): lax.all_to_all(chunks, 'ch', split_axis=0, concat_axis=0, tiled=True)]
  transfers between devices with their start and end apart: 8 -> 5, of which waited for: 7 -> 4; matrix products, arithmetic and copies ran while one was open for 17% -> 5% of each run, Pallas kernels for 0% -> 2%
where the time goes in v1:
time: 131 us; the launch traced here: 130 us
  Pallas kernels  33.3 us (25%)
  blocking collectives  30.5 us (23%)
  waiting for transfers between devices  23.5 us (18%)
  starting transfers between devices  19.2 us (15%)
  local copies, waits for them, and re-layouts  19.1 us (15%)
  other arithmetic  2.7 us (2%)
  between operations  1.7 us (1%)
    all_to_all x1, blocking collectives, body(): back = lax.all_to_all(made, 'ch', split_axis=0, concat_axis=0, tiled=True)  30.5 us
    pallas_call x1, Pallas kernels, body(): pl.pallas_call(main_kernel, out_shape=jax.ShapeDtypeStruct((shards, CHUNK...  21.9 us
    all_to_all x1, waiting for transfers between devices, body(): lax.all_to_all(copies, 'ch', split_axis=0, concat_axis=0, tiled=True)  15.1 us
    all_to_all x1, starting transfers between devices, body(): lax.all_to_all(chunks, 'ch', split_axis=0, concat_axis=0, tiled=True)  9.6 us
    unnamed x43, local copies, waits for them, and re-layouts  7.88 us
    all_to_all x1, starting transfers between devices, body(): lax.all_to_all(copies, 'ch', split_axis=0, concat_axis=0, tiled=True)  5.42 us
    all_to_all x1, waiting for transfers between devices, body(): lax.all_to_all(chunks, 'ch', split_axis=0, concat_axis=0, tiled=True)  5.36 us
    slice x4, local copies, waits for them, and re-layouts, vector(): return flat[row * CH:row * CH + count]  5.33 us
  transfers between devices with their start and end apart: 5, of which 4 were waited for; matrix products, arithmetic and copies ran while one was open for 5% of the time, Pallas kernels for 2%

profile of v1, /device:TPU:1, one launch (start us, length us, event | category | flops | bytes accessed | tf_op | source)
XLA Modules:
  0.0 130.0 jit_solution(10356721941234120623)
XLA Ops:
  0.7 2.5 %shard_map.416 = bf16[32,80,128]{2,1,0:T(8,128)(2,1)} custom-call(bf16[4,41472]{1,0:T(4,128)(2,1)} %feat.1, bf16[10,10368]{1,0:T(8,128)(2,1)} %cot.1), custom_call_target="tpu_custom_call" | custom-call | tf_op jit(solution)/shard_map/pallas_call | solution.py:558
  3.2 9.6 %all-to-all-start = ((bf16[32,80,128]{2,1,0:T(8,128)(2,1)}), bf16[32,80,128]{2,1,0:T(8,128)(2,1)S(1)}, u32[]{:S(2)}, u32[]{:S(2)}) async-start(bf16[32,80,128]{2,1,0:T(8,128)(2,1)} %shard_map.416), calls=%async_computation | async-start | bytes 1310720 | tf_op jit(solution)/shard_map/all_to_all | solution.py:567
  12.9 0.0 copy-start.11
  12.9 0.0 copy-start.12
  12.9 0.0 copy-start.13
  12.9 0.0 copy-start.14
  12.9 0.0 copy-start.15
  12.9 0.0 copy-start.16
  12.9 0.0 copy-start.17
  12.9 0.0 copy-start.18
  13.0 0.0 copy-start.19
  13.0 0.0 copy-start.7
  13.0 0.0 copy-start.8
  13.0 0.0 copy-start.9
  13.0 0.0 copy-start.5
  13.1 0.7 copy.53.sqb
  13.8 0.6 convert_element_type.77.exw
  14.4 0.8 reshape.83.kbias
  15.2 1.1 copy.52
  16.3 1.4 %copy.55.kw = bf16[320,1152]{1,0:T(8,128)(2,1)} copy(bf16[320,1152]{0,1:T(8,128)(2,1)S(1)} %bitcast.37) | data formatting | bytes 1474560 | tf_op jit(solution)/shard_map/reshape | solution.py:631
  17.7 0.6 dynamic_slice.4
  18.9 0.6 pad_add_fusion.info
  19.8 0.0 copy-start.4
  19.8 0.6 convert_bitcast_fusion.sqt
  20.4 5.4 %all-to-all-done.recv = bf16[32,80,128]{2,1,0:T(8,128)(2,1)S(1)} async-done(((bf16[32,80,128]{2,1,0:T(8,128)(2,1)}), bf16[32,80,128]{2,1,0:T(8,128)(2,1)S(1)}, u32[]{:S(2)}, u32[]{:S(2)}) %all-to-all-start) | async-done | bytes 655392 | tf_op jit(solution)/shard_map/all_to_all | solution.py:567
  25.8 0.8 copy-done.1
  26.6 21.9 %shard_map.417 = bf16[32,224,128]{2,1,0:T(8,128)(2,1)} custom-call(s32[2]{0:T(128)} %pad_add_fusion.info, bf16[32,80,128]{2,1,0:T(8,128)(2,1)} %copy-done.1, f32[17,128]{1,0:T(8,128)} %bitcast.38, f32[32,128]{1,0:T(8,128)} %convert_bitcast_fusion.sqt, f32[32,1]{1,0:T(8,128)} %copy.53.sqb, f32[32,384]{1,0:T(8,128)} %convert_element_type.77.exw, ...), custom_call_target="tpu_custom_call" | custom-call | tf_op jit(solution)/shard_map/pallas_call | solution.py:573
  48.5 30.5 %all_to_all.15.recv = bf16[32,224,128]{2,1,0:T(8,128)(2,1)} all-to-all(bf16[32,224,128]{2,1,0:T(8,128)(2,1)} %shard_map.417), channel_id=1, replica_groups=mesh['ch'=32,'img'=4] {'ch'}, dimensions={0} | all-to-all | bytes 3670016 | tf_op jit(solution)/shard_map/all_to_all | solution.py:633
  78.9 2.3 %shard_map.419 = bf16[144,128]{1,0:T(8,128)(2,1)} custom-call(bf16[32,224,128]{2,1,0:T(8,128)(2,1)} %all_to_all.15.recv), custom_call_target="tpu_custom_call" | custom-call | tf_op jit(solution)/shard_map/pallas_call | solution.py:635
  81.2 2.5 %collective-permute-start.2 = (bf16[144,128]{1,0:T(8,128)(2,1)}, bf16[144,128]{1,0:T(8,128)(2,1)S(1)}, u32[]{:S(2)}, u32[]{:S(2)}) collective-permute-start(bf16[144,128]{1,0:T(8,128)(2,1)} %shard_map.419), channel_id=1, source_target_pairs={{0,3},{1,0},{2,1},{3,2},{4,7},{5,4},{6,5},{7,6},{8,11},{9,8},{10,9... | collective-permute-start | bytes 110600 | tf_op jit(solution)/shard_map/ppermute | solution.py:642
  83.7 0.0 collective-permute-start.1
  83.7 1.7 %collective-permute-start = (bf16[144,128]{1,0:T(8,128)(2,1)}, bf16[144,128]{1,0:T(8,128)(2,1)S(1)}, u32[]{:S(2)}, u32[]{:S(2)}) collective-permute-start(bf16[144,128]{1,0:T(8,128)(2,1)} %shard_map.419), channel_id=1, source_target_pairs={{0,2},{1,3},{2,0},{3,1},{4,6},{5,7},{6,4},{7,5},{8,10},{9,11},{10,... | collective-permute-start | bytes 110600 | tf_op jit(solution)/shard_map/ppermute | solution.py:642
  85.4 2.5 %collective-permute-done.1 = bf16[144,128]{1,0:T(8,128)(2,1)S(1)} collective-permute-done((bf16[144,128]{1,0:T(8,128)(2,1)}, bf16[144,128]{1,0:T(8,128)(2,1)S(1)}, u32[]{:S(2)}, u32[]{:S(2)}) %collective-permute-start.1) | collective-permute-done | bytes 36896 | tf_op jit(solution)/shard_map/ppermute | solution.py:642
  87.9 0.6 collective-permute-done
  88.5 0.8 add_convert_fusion
  89.3 1.2 broadcast_in_dim.17
  90.5 5.4 %all-to-all-start.2 = ((bf16[32,144,128]{2,1,0:T(8,128)(2,1)}), bf16[32,144,128]{2,1,0:T(8,128)(2,1)S(1)}, u32[]{:S(2)}, u32[]{:S(2)}) async-start(bf16[32,144,128]{2,1,0:T(8,128)(2,1)} %broadcast_in_dim.17), calls=%async_computation.2 | async-start | bytes 2359296 | tf_op jit(solution)/shard_map/all_to_all | solution.py:647
  95.9 2.7 %shard_map.418 = (f32[4,41472]{1,0:T(4,128)}, bf16[10,10368]{1,0:T(8,128)(2,1)}) custom-call(bf16[32,224,128]{2,1,0:T(8,128)(2,1)} %all_to_all.15.recv), custom_call_target="tpu_custom_call" | custom-call | tf_op jit(solution)/shard_map/pallas_call | solution.py:649
  98.6 15.1 %all-to-all-done.2 = bf16[32,144,128]{2,1,0:T(8,128)(2,1)S(1)} async-done(((bf16[32,144,128]{2,1,0:T(8,128)(2,1)}), bf16[32,144,128]{2,1,0:T(8,128)(2,1)S(1)}, u32[]{:S(2)}, u32[]{:S(2)}) %all-to-all-start.2) | async-done | bytes 1179680 | tf_op jit(solution)/shard_map/all_to_all | solution.py:647
  113.7 1.0 copy-done
  114.7 3.9 %shard_map.420 = (f32[320,9,128]{2,1,0:T(8,128)}, f32[512,128]{1,0:T(8,128)}, f32[128,512]{1,0:T(8,128)}, f32[128,128]{1,0:T(8,128)}, f32[128,128]{1,0:T(8,128)}...) custom-call(bf16[4608,128]{1,0:T(8,128)(2,1)} %bitcast.36), custom_call_target="tpu_custom_call" | custom-call | tf_op jit(solution)/shard_map/pallas_call | solution.py:674
  118.6 1.3 slice_bitcast_fusion
  119.9 1.3 slice_bitcast_fusion.1
  121.1 1.5 %slice_bitcast_fusion.2 = (f32[128]{0:T(128)}, f32[128]{0:T(128)}, f32[128]{0:T(128)}, f32[128]{0:T(128)}, f32[128]{0:T(128)}, /*index=5*/f32[128]{0:T(128)}, f32[128]{0:T(128)}, f32[128]{0:T(128)}) fusion(f32[32,128]{1,0:T(8,128)} %get-tuple-element.38), kind=kLoop, calls=%fused_computation.18 | loop fusion | bytes 8192 | tf_op jit(solution)/shard_map/slice | solution.py:694
  122.7 1.2 slice_bitcast_fusion.6
  123.9 1.3 slice.96
  125.1 1.5 %copy.56 = f32[128,32]{0,1:T(8,128)} copy(f32[128,32]{1,0:T(8,128)} %get-tuple-element.81) | data formatting | bytes 32768
  126.6 3.3 %copy.57 = f32[320,9,128]{2,0,1:T(8,128)} copy(f32[320,9,128]{2,1,0:T(8,128)} %get-tuple-element.93) | data formatting | bytes 2949120
  (39 shorter events, 0.1 us)
Async XLA Ops:
  0.7 12.4 %copy-start.10 = (bf16[32]{0:T(256)(128)(2,1)S(1)}, bf16[32]{0:T(256)(128)(2,1)}, u32[]{:S(2)}) copy-start(bf16[32]{0:T(256)(128)(2,1)} %param.36) | copy-start | bytes 196
  0.7 13.1 %copy-start.3 = (bf16[32,384]{1,0:T(8,128)(2,1)S(1)}, bf16[32,384]{1,0:T(8,128)(2,1)}, u32[]{:S(2)}) copy-start(bf16[32,384]{1,0:T(8,128)(2,1)} %param.37) | copy-start | bytes 73732
  0.7 13.7 %copy-start.6 = (bf16[320]{0:T(512)(128)(2,1)S(1)}, bf16[320]{0:T(512)(128)(2,1)}, u32[]{:S(2)}) copy-start(bf16[320]{0:T(512)(128)(2,1)} %param.48) | copy-start | bytes 1924
  0.7 14.5 %copy-start.2 = (bf16[320,9,128]{2,0,1:T(8,128)(2,1)S(1)}, bf16[320,9,128]{2,0,1:T(8,128)(2,1)}, u32[]{:S(2)}) copy-start(bf16[320,9,128]{2,0,1:T(8,128)(2,1)} %param.47) | copy-start | bytes 2211844
  3.2 22.5 %all-to-all-start = ((bf16[32,80,128]{2,1,0:T(8,128)(2,1)}), bf16[32,80,128]{2,1,0:T(8,128)(2,1)S(1)}, u32[]{:S(2)}, u32[]{:S(2)}) async-start(bf16[32,80,128]{2,1,0:T(8,128)(2,1)} %shard_map.416), calls=%async_computation | async-start | bytes 1310720 | tf_op jit(solution)/shard_map/all_to_all | solution.py:567
  12.9 4.8 %copy-start.11 = (s32[32]{0:T(128)S(1)}, s32[32]{0:T(128)}, u32[]{:S(2)}) copy-start(s32[32]{0:T(128)} %param.26) | copy-start | bytes 388
  12.9 6.7 %copy-start.12 = (bf16[128]{0:T(256)(128)(2,1)S(1)}, bf16[128]{0:T(256)(128)(2,1)}, u32[]{:S(2)}) copy-start(bf16[128]{0:T(256)(128)(2,1)} %param.28) | copy-start | bytes 772
  12.9 6.6 %copy-start.13 = (bf16[128]{0:T(256)(128)(2,1)S(1)}, bf16[128]{0:T(256)(128)(2,1)}, u32[]{:S(2)}) copy-start(bf16[128]{0:T(256)(128)(2,1)} %param.29) | copy-start | bytes 772
  12.9 6.7 %copy-start.14 = (bf16[128]{0:T(256)(128)(2,1)S(1)}, bf16[128]{0:T(256)(128)(2,1)}, u32[]{:S(2)}) copy-start(bf16[128]{0:T(256)(128)(2,1)} %param.31) | copy-start | bytes 772
  12.9 6.7 %copy-start.15 = (bf16[128]{0:T(256)(128)(2,1)S(1)}, bf16[128]{0:T(256)(128)(2,1)}, u32[]{:S(2)}) copy-start(bf16[128]{0:T(256)(128)(2,1)} %param.33) | copy-start | bytes 772
  12.9 6.7 %copy-start.16 = (bf16[128]{0:T(256)(128)(2,1)S(1)}, bf16[128]{0:T(256)(128)(2,1)}, u32[]{:S(2)}) copy-start(bf16[128]{0:T(256)(128)(2,1)} %param.40) | copy-start | bytes 772
  12.9 6.7 %copy-start.17 = (bf16[128]{0:T(256)(128)(2,1)S(1)}, bf16[128]{0:T(256)(128)(2,1)}, u32[]{:S(2)}) copy-start(bf16[128]{0:T(256)(128)(2,1)} %param.41) | copy-start | bytes 772
  12.9 6.7 %copy-start.18 = (bf16[128]{0:T(256)(128)(2,1)S(1)}, bf16[128]{0:T(256)(128)(2,1)}, u32[]{:S(2)}) copy-start(bf16[128]{0:T(256)(128)(2,1)} %param.42) | copy-start | bytes 772
  13.0 6.7 %copy-start.19 = (bf16[128]{0:T(256)(128)(2,1)S(1)}, bf16[128]{0:T(256)(128)(2,1)}, u32[]{:S(2)}) copy-start(bf16[128]{0:T(256)(128)(2,1)} %param.46) | copy-start | bytes 772
  13.0 6.7 %copy-start.7 = (bf16[512]{0:T(512)(128)(2,1)S(1)}, bf16[512]{0:T(512)(128)(2,1)}, u32[]{:S(2)}) copy-start(bf16[512]{0:T(512)(128)(2,1)} %param.44) | copy-start | bytes 3076
  13.0 6.7 %copy-start.8 = (bf16[384]{0:T(512)(128)(2,1)S(1)}, bf16[384]{0:T(512)(128)(2,1)}, u32[]{:S(2)}) copy-start(bf16[384]{0:T(512)(128)(2,1)} %param.38) | copy-start | bytes 2308
  13.0 6.8 %copy-start.9 = (s32[2,128]{1,0:T(2,128)S(1)}, s32[2,128]{1,0:T(2,128)}, u32[]{:S(2)}) copy-start(s32[2,128]{1,0:T(2,128)} %param.27) | copy-start | bytes 3076
  13.0 6.8 %copy-start.5 = (bf16[128,32]{0,1:T(8,128)(2,1)S(1)}, bf16[128,32]{0,1:T(8,128)(2,1)}, u32[]{:S(2)}) copy-start(bf16[128,32]{0,1:T(8,128)(2,1)} %param.35) | copy-start | bytes 24580
  19.8 6.0 %copy-start.4 = (f32[2176]{0:T(1024)}, f32[2176]{0:T(1024)S(1)}, u32[]{:S(2)}) copy-start(f32[2176]{0:T(1024)S(1)} %constant_dynamic-update-slice_fusion) | copy-start | bytes 26116
  25.8 0.8 copy-start.1
  81.2 4.2 %collective-permute-start.2 = (bf16[144,128]{1,0:T(8,128)(2,1)}, bf16[144,128]{1,0:T(8,128)(2,1)S(1)}, u32[]{:S(2)}, u32[]{:S(2)}) collective-permute-start(bf16[144,128]{1,0:T(8,128)(2,1)} %shard_map.419), channel_id=1, source_target_pairs={{0,3},{1,0},{2,1},{3,2},{4,7},{5,4},{6,5},{7,6},{8,11},{9,8},{10,9... | collective-permute-start | bytes 110600 | tf_op jit(solution)/shard_map/ppermute | solution.py:642
  83.7 4.2 %collective-permute-start.1 = (bf16[144,128]{1,0:T(8,128)(2,1)}, bf16[144,128]{1,0:T(8,128)(2,1)S(1)}, u32[]{:S(2)}, u32[]{:S(2)}) collective-permute-start(bf16[144,128]{1,0:T(8,128)(2,1)} %shard_map.419), channel_id=1, source_target_pairs={{0,1},{1,2},{2,3},{3,0},{4,5},{5,6},{6,7},{7,4},{8,9},{9,10},{10,1... | collective-permute-start | bytes 110600 | tf_op jit(solution)/shard_map/ppermute | solution.py:642
  83.7 4.8 %collective-permute-start = (bf16[144,128]{1,0:T(8,128)(2,1)}, bf16[144,128]{1,0:T(8,128)(2,1)S(1)}, u32[]{:S(2)}, u32[]{:S(2)}) collective-permute-start(bf16[144,128]{1,0:T(8,128)(2,1)} %shard_map.419), channel_id=1, source_target_pairs={{0,2},{1,3},{2,0},{3,1},{4,6},{5,7},{6,4},{7,5},{8,10},{9,11},{10,... | collective-permute-start | bytes 110600 | tf_op jit(solution)/shard_map/ppermute | solution.py:642
  90.5 23.2 %all-to-all-start.2 = ((bf16[32,144,128]{2,1,0:T(8,128)(2,1)}), bf16[32,144,128]{2,1,0:T(8,128)(2,1)S(1)}, u32[]{:S(2)}, u32[]{:S(2)}) async-start(bf16[32,144,128]{2,1,0:T(8,128)(2,1)} %broadcast_in_dim.17), calls=%async_computation.2 | async-start | bytes 2359296 | tf_op jit(solution)/shard_map/all_to_all | solution.py:647
  113.7 1.0 copy-start

commit v2 on v1

--- a/solution.py
+++ b/solution.py
@@ -24,7 +24,6 @@
 OTILE = 3
 PIXROWS = 80
 WROWS = 144
-CHUNK = PIXROWS + WROWS
 VMEM = 56 * 1024 * 1024
 
 F32 = jnp.float32
@@ -41,10 +40,16 @@
 AT_EXCITE = 4448
 AT_SQ_BIAS = 4544
 AT_VECTOR = 4576
+VECTOR_ROWS = (0, 1, 2, 3, 4, 5, 6, 7, 8, 12, 15)
+VECTOR_SIZES = (CH,) * 8 + (FF, 3 * CH, OUT)
 
 
 def params(**kw):
     return pltpu.CompilerParams(vmem_limit_bytes=VMEM, **kw)
+
+
+def cost(micros):
+    return pl.CostEstimate(flops=0, bytes_accessed=int(micros * 3.69e6), transcendentals=0)
 
 
 def first_tile(k):
@@ -116,7 +121,10 @@
     xw,
     rw,
     kw,
-    out,
+    keep_out,
+    send_out,
+    grad,
+    section_out,
     xf,
     cf,
     tall,
@@ -151,23 +159,24 @@
     acc_x,
     acc_s,
     sums,
-    stage,
     gpre_b,
+    rows_out,
 ):
     shift = info[0]
     side = info[1]
+    core = info[2]
 
     def vec(i):
         return vecs[i : i + 1, :]
 
     def put(row, value):
-        value = value.astype(BF16)
         count = value.shape[0]
         done = 0
         while done < count:
             chunk, inner = divmod(row + done, WROWS)
             size = min(count - done, WROWS - inner)
-            out[chunk, PIXROWS + inner : PIXROWS + inner + size, :] = value[done : done + size, :]
+            slot = core if chunk % 2 == 0 else 1 - core
+            rows_out[slot, chunk // 2, inner : inner + size, :] = value[done : done + size, :]
             done += size
 
     cf[...] = jnp.zeros_like(cf)
@@ -305,7 +314,7 @@
     cot_b = cot[0:OUT, :].astype(BF16)
     cot_t = cot.T.astype(BF16)[:, 0:OUT]
     section = nt(kw[...], tap_b) + kbias[...]
-    section = jnp.where(out_keep, section, 0.0)
+    section_out[...] = jnp.where(out_keep, section, 0.0)
     conv = nn(cot_b, tap_b)
     for t in range(9):
         put(AT_CONV + t * OUT, conv[:, t * CH : (t + 1) * CH])
@@ -419,26 +428,10 @@
         add(1, col_sum(value))
         gy = value * vec(0)
         back = rstd[here, :] * (gy - lane_mean(gy) - unit * lane_mean(gy * unit))
-        canvas[here, :] = jnp.where(keep, gresid[here, :] + back, 0.0)
+        grad[here, :] = jnp.where(keep, gresid[here, :] + back, 0.0)
         return carry
 
     lax.fori_loop(0, STEPS, last, 0)
-
-    tall[0:112, :] = jnp.zeros((112, CH), F32)
-    tall[112 + PIX :, :] = jnp.zeros((tall.shape[0] - 112 - PIX, CH), F32)
-    for r in range(SIDE):
-        tall[112 + r * SIDE : 112 + (r + 1) * SIDE, :] = canvas[r * WIDE : r * WIDE + SIDE, :]
-    for t in range(WIN):
-        xf[:, t * LANES : (t + 1) * LANES] = tall[pl.ds(begin + t * LANES, LANES), :].T
-    cf[0:OUT, :] = section
-    for s in range(recv.shape[0]):
-        for t in range(WIN):
-            stage[4 * t : 4 * t + 4, :] = xf[4 * s : 4 * s + 4, t * LANES : (t + 1) * LANES]
-        for j in range(OTILE):
-            stage[44 + 10 * j : 54 + 10 * j, :] = cf[
-                10 * s : 10 * s + 10, j * LANES : (j + 1) * LANES
-            ]
-        out[s, 0:PIXROWS, :] = stage[...].astype(BF16)
 
     for j in range(FF // CH):
         put(AT_REDUCE + j * CH, acc_r[:, j * CH : (j + 1) * CH].T)
@@ -451,19 +444,58 @@
     for j in range(OTILE):
         add(15 + j, col_sum(jnp.where(same, kb_rows[j * LANES : (j + 1) * LANES, :], 0.0)))
     put(AT_VECTOR, sums[...])
+    keep_out[...] = rows_out[0]
+    send_out[...] = rows_out[1].astype(BF16)
+
+
+def send_kernel(info, grad, section, out, tall, turned, stage):
+    begin = pl.multiple_of(112 - info[0], 16)
+    tall[0:112, :] = jnp.zeros((112, CH), F32)
+    tall[112 + PIX :, :] = jnp.zeros((tall.shape[0] - 112 - PIX, CH), F32)
+    for r in range(SIDE):
+        tall[112 + r * SIDE : 112 + (r + 1) * SIDE, :] = grad[r * WIDE : r * WIDE + SIDE, :]
+    for t in range(WIN):
+        turned[:, t * LANES : (t + 1) * LANES] = tall[pl.ds(begin + t * LANES, LANES), :].T
+    for s in range(out.shape[0]):
+        base = s * PIXROWS
+        for t in range(WIN):
+            stage[base + 4 * t : base + 4 * t + 4, :] = turned[
+                4 * s : 4 * s + 4, t * LANES : (t + 1) * LANES
+            ]
+        for j in range(OTILE):
+            stage[base + 44 + 10 * j : base + 54 + 10 * j, :] = section[
+                10 * s : 10 * s + 10, j * LANES : (j + 1) * LANES
+            ]
+        out[s] = stage[base : base + PIXROWS, :].astype(BF16)
+
+
+def pair_kernel(kept, met, out):
+    out[...] = (kept[...] + met[...].astype(F32)).astype(BF16)
 
 
 def add_kernel(recv, out):
-    total = recv[0, PIXROWS:, :].astype(F32)
+    total = recv[0].astype(F32)
     for s in range(1, recv.shape[0]):
-        total += recv[s, PIXROWS:, :].astype(F32)
+        total += recv[s].astype(F32)
     out[...] = total.astype(BF16)
 
 
-def pixel_kernel(recv, feat, section, stage):
-    images = recv.shape[0]
-    for k in range(images):
-        piece = recv[k, 0:PIXROWS, :].astype(F32)
+def copies_kernel(mine, one, two, three, out):
+    total = (mine[...].astype(F32) + two[...].astype(F32)) + (
+        one[...].astype(F32) + three[...].astype(F32)
+    )
+    total = total.astype(BF16)
+    for s in range(out.shape[0]):
+        out[s] = total
+
+
+def pixel_kernel(info, near, far, feat, section, stage, recv):
+    core = info[2]
+    for i in range(near.shape[0]):
+        recv[2 * i + core] = near[i]
+        recv[2 * i + 1 - core] = far[i]
+    for k in range(recv.shape[0]):
+        piece = recv[k].astype(F32)
         tile = first_tile(k)
         for t in range(WIN):
             lanes = slice((tile + t) * LANES, (tile + t + 1) * LANES)
@@ -479,14 +511,27 @@
     section[...] = stage[...].astype(BF16)
 
 
-def weight_kernel(
-    recv, conv, red, exp, height, width, chan, outw, squeeze, excite, sq_bias, vectors
-):
+def weight_kernel(info, own, other, *refs):
+    outs = refs[:-1]
+    both = refs[-1]
+    core = info[2]
+    for i in range(own.shape[0]):
+        both[2 * i + core] = own[i]
+        both[2 * i + 1 - core] = other[i]
+
     def rows(at, count):
-        return recv[at : at + count, :].astype(F32)
-
+        found = []
+        done = 0
+        while done < count:
+            chunk, inner = divmod(at + done, WROWS)
+            size = min(count - done, WROWS - inner)
+            found.append(both[chunk, inner : inner + size, :])
+            done += size
+        return jnp.concatenate(found).astype(F32)
+
+    conv, red, exp, height, width, chan, outw, squeeze, excite, sq_bias = outs[:10]
     for t in range(9):
-        conv[:, t, :] = rows(AT_CONV + t * OUT, OUT)
+        conv[t] = rows(AT_CONV + t * OUT, OUT)
     red[...] = rows(AT_REDUCE, FF)
     for j in range(FF // CH):
         exp[:, j * CH : (j + 1) * CH] = rows(AT_EXPAND + j * CH, CH)
@@ -497,11 +542,19 @@
         (AT_OUTPUT, outw),
     ):
         ref[...] = rows(at, CH)
-    squeeze[...] = rows(AT_SQUEEZE, RED).T
+    squeeze[...] = rows(AT_SQUEEZE, RED)
     for j in range(3):
         excite[:, j * CH : (j + 1) * CH] = rows(AT_EXCITE + j * RED, RED)
-    sq_bias[...] = rows(AT_SQ_BIAS, RED).T[0:8, :]
-    vectors[...] = rows(AT_VECTOR, RED)
+    same = lax.broadcasted_iota(jnp.int32, (RED, CH), 0) == lax.broadcasted_iota(
+        jnp.int32, (RED, CH), 1
+    )
+    sq_bias[...] = jnp.sum(jnp.where(same, rows(AT_SQ_BIAS, RED), 0.0), axis=0)[0:RED]
+    vectors = rows(AT_VECTOR, RED)
+    for ref, row in zip(outs[10:], VECTOR_ROWS):
+        size = ref.shape[0]
+        for j in range(-(-size // CH)):
+            width = min(CH, size - j * CH)
+            ref[j * CH : j * CH + width] = vectors[row + j, 0:width]
 
 
 def body(
@@ -534,7 +587,7 @@
     shards = lax.axis_size("ch")
     rank = lax.axis_index("ch")
     side = SIDE - 4 * (2 - lax.dynamic_index_in_dim(size_group, rank, keepdims=False))
-    info = jnp.stack([16 * (rank % 8), side]).astype(jnp.int32)
+    info = jnp.stack([16 * (rank % 8), side, rank % 2]).astype(jnp.int32)
     vecs = jnp.concatenate(
         [
             v.astype(F32)
@@ -557,6 +610,7 @@
 
     chunks = pl.pallas_call(
         pack_kernel,
+        cost_estimate=cost(2.5),
         out_shape=jax.ShapeDtypeStruct((shards, PIXROWS, LANES), BF16),
         scratch_shapes=[
             pltpu.VMEM((shards * PIXROWS, LANES), F32),
@@ -570,11 +624,17 @@
     guarded = pltpu.VMEM((FLAT + 2 * GUARD, CH), F32)
     narrow = pltpu.VMEM((FLAT, CH), BF16)
     whole = pl.BlockSpec(memory_space=pltpu.VMEM)
-    made = pl.pallas_call(
+    kept, sent, grad, section_part = pl.pallas_call(
         main_kernel,
-        out_shape=jax.ShapeDtypeStruct((shards, CHUNK, LANES), BF16),
+        cost_estimate=cost(22),
+        out_shape=(
+            jax.ShapeDtypeStruct((shards // 2, WROWS, LANES), F32),
+            jax.ShapeDtypeStruct((shards // 2, WROWS, LANES), BF16),
+            jax.ShapeDtypeStruct((FLAT, CH), F32),
+            jax.ShapeDtypeStruct((OUT, OTILE * LANES), F32),
+        ),
         in_specs=[pl.BlockSpec(memory_space=pltpu.SMEM)] + [whole] * 13,
-        out_specs=whole,
+        out_specs=(whole,) * 4,
         scratch_shapes=[
             pltpu.VMEM((CH, WIN * LANES), F32),
             pltpu.VMEM((3 * LANES, OTILE * LANES), F32),
@@ -610,8 +670,8 @@
             pltpu.VMEM((CH, FF), F32),
             pltpu.VMEM((4, CH, CH), F32),
             pltpu.VMEM((RED, CH), F32),
-            pltpu.VMEM((PIXROWS, LANES), F32),
             pltpu.VMEM((ROWS, FF), BF16),
+            pltpu.VMEM((2, shards // 2, WROWS, LANES), F32),
         ],
         compiler_params=params(),
     )(
@@ -630,31 +690,81 @@
         reduce_weight,
         stride_weight.reshape(OUT, 9 * CH),
     )
-    back = lax.all_to_all(made, "ch", split_axis=0, concat_axis=0, tiled=True)
+    other_core = [(i, i ^ 1) for i in range(shards)]
+    same_core = [[2 * i + c for i in range(shards // 2)] for c in range(2)]
+    met = lax.ppermute(sent, "ch", other_core)
+    pixels = pl.pallas_call(
+        send_kernel,
+        cost_estimate=cost(2.5),
+        out_shape=jax.ShapeDtypeStruct((shards, PIXROWS, LANES), BF16),
+        in_specs=[pl.BlockSpec(memory_space=pltpu.SMEM)] + [whole] * 2,
+        out_specs=whole,
+        scratch_shapes=[
+            pltpu.VMEM((112 + WIN * LANES, CH), F32),
+            pltpu.VMEM((CH, WIN * LANES), F32),
+            pltpu.VMEM((shards * PIXROWS, LANES), F32),
+        ],
+        compiler_params=params(),
+    )(info, grad, section_part)
+    kept, pixels = lax.optimization_barrier((kept, pixels))
+    partial = pl.pallas_call(
+        pair_kernel,
+        cost_estimate=cost(2.3),
+        out_shape=jax.ShapeDtypeStruct(kept.shape, BF16),
+        compiler_params=params(),
+    )(kept, met)
+
+    def exchange(v):
+        return lax.all_to_all(
+            v, "ch", split_axis=0, concat_axis=0, tiled=True, axis_index_groups=same_core
+        )
+
+    parts = exchange(partial)
+    parts, pixels = lax.optimization_barrier((parts, pixels))
+    back = exchange(pixels.reshape(shards // 2, 2, PIXROWS, LANES))
 
     mine = pl.pallas_call(
         add_kernel,
+        cost_estimate=cost(1.7),
         out_shape=jax.ShapeDtypeStruct((WROWS, LANES), BF16),
         compiler_params=params(),
-    )(back)
+    )(parts)
     groups = lax.axis_size("img")
     other = [
-        lax.ppermute(mine, "img", [(i, (i + d) % groups) for i in range(groups)]).astype(F32)
+        lax.ppermute(mine, "img", [(i, (i + d) % groups) for i in range(groups)])
         for d in (1, 2, 3)
     ]
-    owned = ((mine.astype(F32) + other[1]) + (other[0] + other[2])).astype(BF16)
-    copies = jnp.broadcast_to(owned, (shards, WROWS, LANES))
-    summed = lax.all_to_all(copies, "ch", split_axis=0, concat_axis=0, tiled=True)
+    copies = pl.pallas_call(
+        copies_kernel,
+        cost_estimate=cost(1.7),
+        out_shape=jax.ShapeDtypeStruct((shards // 2, WROWS, LANES), BF16),
+        compiler_params=params(),
+    )(mine, *other)
+    copies, back = lax.optimization_barrier((copies, back))
+    own_half = exchange(copies)
+    core = rank % 2
+    near = lax.dynamic_index_in_dim(back, core, axis=1, keepdims=False)
+    far = lax.dynamic_index_in_dim(back, 1 - core, axis=1, keepdims=False)
+    far = lax.ppermute(far, "ch", other_core)
 
     features_grad, section = pl.pallas_call(
         pixel_kernel,
+        cost_estimate=cost(2.5),
         out_shape=(
             jax.ShapeDtypeStruct(features.shape, F32),
             jax.ShapeDtypeStruct(cotangent.shape, BF16),
         ),
-        scratch_shapes=[pltpu.VMEM(cotangent.shape, F32)],
+        in_specs=[pl.BlockSpec(memory_space=pltpu.SMEM)] + [whole] * 2,
+        out_specs=(whole,) * 2,
+        scratch_shapes=[
+            pltpu.VMEM(cotangent.shape, F32),
+            pltpu.VMEM((shards, PIXROWS, LANES), BF16),
+        ],
         compiler_params=params(),
-    )(back)
+    )(info, near, far)
+
+    own_half, features_grad, section = lax.optimization_barrier((own_half, features_grad, section))
+    other_half = lax.ppermute(own_half, "ch", other_core)
 
     def like(*shape):
         return jax.ShapeDtypeStruct(shape, F32)
@@ -669,54 +779,63 @@
         output_grad,
         squeeze_grad,
         excite_grad,
-        squeeze_rows,
-        vectors,
+        squeeze_bias_grad,
+        norm_gain_grad,
+        norm_bias_grad,
+        height_bias_grad,
+        width_bias_grad,
+        output_bias_grad,
+        second_gain_grad,
+        second_bias_grad,
+        reduce_bias_grad,
+        expand_bias_grad,
+        excite_bias_grad,
+        conv_bias_grad,
     ) = pl.pallas_call(
         weight_kernel,
+        cost_estimate=cost(2.8),
         out_shape=(
-            like(OUT, 9, CH),
+            like(9, OUT, CH),
             like(FF, CH),
             like(CH, FF),
             like(CH, CH),
             like(CH, CH),
             like(CH, CH),
             like(CH, CH),
-            like(CH, RED),
+            like(RED, CH),
             like(RED, 3 * CH),
-            like(8, RED),
-            like(RED, CH),
-        ),
+            like(RED),
+        )
+        + tuple(like(size) for size in VECTOR_SIZES),
+        in_specs=[pl.BlockSpec(memory_space=pltpu.SMEM)] + [whole] * 2,
+        out_specs=(whole,) * 21,
+        scratch_shapes=[pltpu.VMEM((shards, WROWS, LANES), BF16)],
         compiler_params=params(),
-    )(summed.reshape(shards * WROWS, LANES))
-    flat = vectors.reshape(RED * CH)
-
-    def vector(row, count=CH):
-        return flat[row * CH : row * CH + count]
-
+    )(info, own_half, other_half)
     return (
         section,
         features_grad,
-        vector(0),
-        vector(1),
+        norm_gain_grad,
+        norm_bias_grad,
         height_grad,
-        vector(2),
+        height_bias_grad,
         width_grad,
-        vector(3),
+        width_bias_grad,
         channel_grad,
-        squeeze_grad,
-        squeeze_rows[0],
+        squeeze_grad.T,
+        squeeze_bias_grad,
         excite_grad,
-        vector(12, 3 * CH),
+        excite_bias_grad,
         output_grad,
-        vector(4),
-        vector(5),
-        vector(6),
+        output_bias_grad,
+        second_gain_grad,
+        second_bias_grad,
         expand_grad,
-        vector(8, FF),
+        expand_bias_grad,
         reduce_grad,
-        vector(7),
-        conv_grad,
-        vector(15, OUT),
+        reduce_bias_grad,
+        jnp.transpose(conv_grad, (1, 0, 2)),
+        conv_bias_grad,
     )
 
 

time: 131 us -> 112 us (0.85)
  blocking collectives: 30.5 us -> 16.7 us
  starting transfers between devices: 19.2 us -> 30.2 us
  waiting for transfers between devices: 23.5 us -> 13.6 us
  local copies, waits for them, and re-layouts: 19.1 us -> 9.42 us
  Pallas kernels: 33.3 us -> 37.8 us
    all_to_all x1, blocking collectives: 30.5 us -> 16.7 us  [exchange(): lax.all_to_all(v, 'ch', split_axis=0, concat_axis=0, tiled=True, axis_ind...]
    all_to_all x1 -> x2, waiting for transfers between devices: 15.1 us -> 3.25 us  [exchange(): lax.all_to_all(v, 'ch', split_axis=0, concat_axis=0, tiled=True, axis_ind...]
    ppermute x0 -> x3, starting transfers between devices: none -> 6.17 us  [the longest x1 3.19 us: body(): other_half = lax.ppermute(own_half, 'ch', other_core)]
    slice x4 -> x0, local copies, waits for them, and re-layouts: 5.33 us -> none  [vector(): return flat[row * CH:row * CH + count]]
    pallas_call x5 -> x8, Pallas kernels: 33.3 us -> 37.8 us  [the longest x1 21.8 us: body(): pl.pallas_call(main_kernel, cost_estimate=cost(22), out_shape=(jax.ShapeD...]
    all_to_all x1 -> x2, starting transfers between devices: 5.42 us -> 9.66 us  [exchange(): lax.all_to_all(v, 'ch', split_axis=0, concat_axis=0, tiled=True, axis_ind...]
    ppermute x0 -> x3, waiting for transfers between devices: none -> 2.89 us  [the longest x1 1.63 us: body(): other_half = lax.ppermute(own_half, 'ch', other_core)]
    unnamed x43 -> x53, local copies, waits for them, and re-layouts: 7.88 us -> 5.12 us
  transfers between devices with their start and end apart: 5 -> 9, of which waited for: 4 -> 7; matrix products, arithmetic and copies ran while one was open for 5% -> 7% of each run, Pallas kernels for 2% -> 8%
where the time goes in v2:
time: 112 us; the launch traced here: 111 us
  Pallas kernels  37.8 us (34%)
  starting transfers between devices  30.2 us (27%)
  blocking collectives  16.7 us (15%)
  waiting for transfers between devices  13.6 us (12%)
  local copies, waits for them, and re-layouts  9.42 us (8%)
  other arithmetic  1.98 us (2%)
  between operations  1.72 us (2%)
    pallas_call x1, Pallas kernels, body(): pl.pallas_call(main_kernel, cost_estimate=cost(22), out_shape=(jax.ShapeD...  21.8 us
    all_to_all x1, blocking collectives, exchange(): lax.all_to_all(v, 'ch', split_axis=0, concat_axis=0, tiled=True, axis_ind...  16.7 us
    all_to_all x2, starting transfers between devices, exchange(): lax.all_to_all(v, 'ch', split_axis=0, concat_axis=0, tiled=True, axis_ind...  9.66 us
    all_to_all x1, starting transfers between devices, body(): lax.all_to_all(chunks, 'ch', split_axis=0, concat_axis=0, tiled=True)  9.6 us
    all_to_all x1, waiting for transfers between devices, body(): lax.all_to_all(chunks, 'ch', split_axis=0, concat_axis=0, tiled=True)  5.2 us
    unnamed x53, local copies, waits for them, and re-layouts  5.12 us
    ppermute x3, starting transfers between devices, body(): lax.ppermute(mine, 'img', [(i, (i + d) % groups) for i in range(groups)])  4.81 us
    all_to_all x2, waiting for transfers between devices, exchange(): lax.all_to_all(v, 'ch', split_axis=0, concat_axis=0, tiled=True, axis_ind...  3.25 us
  transfers between devices with their start and end apart: 9, of which 7 were waited for; matrix products, arithmetic and copies ran while one was open for 7% of the time, Pallas kernels for 8%

profile of v2, /device:TPU:1, one launch (start us, length us, event | category | flops | bytes accessed | tf_op | source)
XLA Modules:
  0.0 111.4 jit_solution(14923635939553352835)
XLA Ops:
  0.7 2.5 %shard_map.416 = bf16[32,80,128]{2,1,0:T(8,128)(2,1)} custom-call(bf16[4,41472]{1,0:T(4,128)(2,1)} %feat.1, bf16[10,10368]{1,0:T(8,128)(2,1)} %cot.1), custom_call_target="tpu_custom_call" | custom-call | bytes 9225000 | tf_op jit(solution)/shard_map/pallas_call | solution.py:611
  3.2 9.6 %all-to-all-start = ((bf16[32,80,128]{2,1,0:T(8,128)(2,1)}), bf16[32,80,128]{2,1,0:T(8,128)(2,1)S(1)}, u32[]{:S(2)}, u32[]{:S(2)}) async-start(bf16[32,80,128]{2,1,0:T(8,128)(2,1)} %shard_map.416), calls=%async_computation | async-start | bytes 1310720 | tf_op jit(solution)/shard_map/all_to_all | solution.py:621
  12.9 0.0 copy-start.12
  12.9 0.0 copy-start.9
  12.9 0.0 copy-start.16
  12.9 0.0 copy-start.18
  12.9 0.0 copy-start.19
  13.0 0.0 copy-start.22
  13.0 0.0 copy-start.23
  13.0 0.0 copy-start.13
  13.0 0.0 copy-start.14
  13.1 1.1 copy.56
  14.2 1.5 %copy.59.kw = bf16[320,1152]{1,0:T(8,128)(2,1)} copy(bf16[320,1152]{0,1:T(8,128)(2,1)S(1)} %bitcast.20) | data formatting | bytes 1474560 | tf_op jit(solution)/shard_map/reshape | solution.py:691
  15.6 0.8 reshape.69.kbias
  16.4 0.6 convert_element_type.62.exw
  17.0 0.7 copy.57.sqb
  17.7 0.6 dynamic_slice.11
  19.2 0.7 pad_add_fusion.info
  19.9 0.6 convert_bitcast_fusion.sqt
  20.5 5.2 %all-to-all-done.recv = bf16[32,80,128]{2,1,0:T(8,128)(2,1)S(1)} async-done(((bf16[32,80,128]{2,1,0:T(8,128)(2,1)}), bf16[32,80,128]{2,1,0:T(8,128)(2,1)S(1)}, u32[]{:S(2)}, u32[]{:S(2)}) %all-to-all-start) | async-done | bytes 655392 | tf_op jit(solution)/shard_map/all_to_all | solution.py:621
  25.7 0.8 copy-done
  26.6 21.8 %shard_map.417 = (f32[16,144,128]{2,1,0:T(8,128)}, bf16[16,144,128]{2,1,0:T(8,128)(2,1)}, f32[1440,128]{1,0:T(8,128)}, f32[320,384]{1,0:T(8,128)}) custom-call(s32[3]{0:T(128)} %pad_add_fusion.info, bf16[32,80,128]{2,1,0:T(8,128)(2,1)} %copy-done, f32[17,128]{1,0:T(8,128)} %bitcast.21, f32[32,128]{1,0:T(8,128)} %convert_bitcast_fusion.sqt, ...), custom_call_target="tpu_custom_call" | custom-call | bytes 81180000 | tf_op jit(solution)/shard_map/pallas_call | solution.py:627
  48.3 0.5 collective-permute-start
  48.9 2.6 %shard_map.418 = bf16[32,80,128]{2,1,0:T(8,128)(2,1)} custom-call(s32[3]{0:T(128)} %pad_add_fusion.info, f32[1440,128]{1,0:T(8,128)} %get-tuple-element.60.grad, f32[320,384]{1,0:T(8,128)} %get-tuple-element.61.section), custom_call_target="tpu_custom_call" | custom-call | bytes 9225000 | tf_op jit(solution)/shard_map/pallas_call | solution.py:696
  51.5 0.8 copy-done.4
  52.3 2.3 %shard_map.419 = bf16[16,144,128]{2,1,0:T(8,128)(2,1)} custom-call(f32[16,144,128]{2,1,0:T(8,128)} %get-tuple-element.62.kept, bf16[16,144,128]{2,1,0:T(8,128)(2,1)} %copy-done.4), custom_call_target="tpu_custom_call" | custom-call | bytes 8487000 | tf_op jit(solution)/shard_map/pallas_call | solution.py:710
  54.6 16.7 %all_to_all.20.recv = bf16[16,144,128]{2,1,0:T(8,128)(2,1)} all-to-all(bf16[16,144,128]{2,1,0:T(8,128)(2,1)} %shard_map.419), channel_id=1, replica_groups={{0,8,16,24,32,40,48,56,64,72,80,88,96,104,112,120},{4,12,20,28,36,44,52..., dimensions={0} | all-to-all | bytes 1179648 | tf_op jit(solution)/shard_map/all_to_all | solution.py:718
  71.3 3.6 %all-to-all-start.2 = ((bf16[16,2,80,128]{3,2,1,0:T(8,128)(2,1)}), bf16[16,2,80,128]{3,2,1,0:T(8,128)(2,1)S(1)}, u32[]{:S(2)}, u32[]{:S(2)}) async-start(bf16[16,2,80,128]{3,2,1,0:T(8,128)(2,1)} %bitcast.8), calls=%async_computation.2 | async-start | bytes 1310720 | tf_op jit(solution)/shard_map/all_to_all | solution.py:718
  74.9 1.8 %shard_map.420.mine = bf16[144,128]{1,0:T(8,128)(2,1)} custom-call(bf16[16,144,128]{2,1,0:T(8,128)(2,1)} %all_to_all.20.recv), custom_call_target="tpu_custom_call" | custom-call | bytes 6273000 | tf_op jit(solution)/shard_map/pallas_call | solution.py:726
  76.7 1.2 %collective-permute-start.1 = (bf16[144,128]{1,0:T(8,128)(2,1)}, bf16[144,128]{1,0:T(8,128)(2,1)S(1)}, u32[]{:S(2)}, u32[]{:S(2)}) collective-permute-start(bf16[144,128]{1,0:T(8,128)(2,1)} %shard_map.420.mine), channel_id=1, source_target_pairs={{0,1},{1,2},{2,3},{3,0},{4,5},{5,6},{6,7},{7,4},{8,9},{9,10},{10,1... | collective-permute-start | bytes 110600 | tf_op jit(solution)/shard_map/ppermute | solution.py:734
  77.9 2.5 %collective-permute-start.2 = (bf16[144,128]{1,0:T(8,128)(2,1)}, bf16[144,128]{1,0:T(8,128)(2,1)S(1)}, u32[]{:S(2)}, u32[]{:S(2)}) collective-permute-start(bf16[144,128]{1,0:T(8,128)(2,1)} %shard_map.420.mine), channel_id=1, source_target_pairs={{0,2},{1,3},{2,0},{3,1},{4,6},{5,7},{6,4},{7,5},{8,10},{9,11},{10,... | collective-permute-start | bytes 110600 | tf_op jit(solution)/shard_map/ppermute | solution.py:734
  80.3 1.1 %collective-permute-start.3 = (bf16[144,128]{1,0:T(8,128)(2,1)}, bf16[144,128]{1,0:T(8,128)(2,1)S(1)}, u32[]{:S(2)}, u32[]{:S(2)}) collective-permute-start(bf16[144,128]{1,0:T(8,128)(2,1)} %shard_map.420.mine), channel_id=1, source_target_pairs={{0,3},{1,0},{2,1},{3,2},{4,7},{5,4},{6,5},{7,6},{8,11},{9,8},{10,9... | collective-permute-start | bytes 110600 | tf_op jit(solution)/shard_map/ppermute | solution.py:734
  81.5 1.2 %collective-permute-done.2.two = bf16[144,128]{1,0:T(8,128)(2,1)S(1)} collective-permute-done((bf16[144,128]{1,0:T(8,128)(2,1)}, bf16[144,128]{1,0:T(8,128)(2,1)S(1)}, u32[]{:S(2)}, u32[]{:S(2)}) %collective-permute-start.2) | collective-permute-done | bytes 36896 | tf_op jit(solution)/shard_map/ppermute | solution.py:734
  82.7 1.0 collective-permute-done.3.three
  83.7 0.6 copy-done.8
  84.3 1.7 %shard_map.421 = bf16[16,144,128]{2,1,0:T(8,128)(2,1)} custom-call(bf16[144,128]{1,0:T(8,128)(2,1)} %shard_map.420.mine, bf16[144,128]{1,0:T(8,128)(2,1)} %copy-done.6, bf16[144,128]{1,0:T(8,128)(2,1)} %copy-done.7, bf16[144,128]{1,0:T(8,128)(2,1)} %copy-done.8), custom_call_target="tpu_custom_call" | custom-call | bytes 6273000 | tf_op jit(solution)/shard_map/pallas_call | solution.py:737
  86.0 0.8 all-to-all-done.2
  86.8 6.1 %all-to-all-start.3 = ((bf16[16,144,128]{2,1,0:T(8,128)(2,1)}), bf16[16,144,128]{2,1,0:T(8,128)(2,1)S(1)}, u32[]{:S(2)}, u32[]{:S(2)}) async-start(bf16[16,144,128]{2,1,0:T(8,128)(2,1)} %shard_map.421), calls=%async_computation.3 | async-start | bytes 1179648 | tf_op jit(solution)/shard_map/all_to_all | solution.py:718
  92.9 0.8 dynamic-slice_bitcast_fusion
  93.7 2.4 %collective-permute-start.4 = (bf16[16,80,128]{2,1,0:T(8,128)(2,1)S(1)}, bf16[16,80,128]{2,1,0:T(8,128)(2,1)S(1)}, u32[]{:S(2)}, u32[]{:S(2)}) collective-permute-start(bf16[16,80,128]{2,1,0:T(8,128)(2,1)S(1)} %get-tuple-element.95), channel_id=1, source_target_pairs={{0,4},{4,0},{8,12},{12,8},{16,20},{20,16},{24,28},{28,24},{32,36},... | collective-permute-start | bytes 983048 | tf_op jit(solution)/shard_map/ppermute | solution.py:748
  96.1 1.3 %collective-permute-done.4.far = bf16[16,80,128]{2,1,0:T(8,128)(2,1)S(1)} collective-permute-done((bf16[16,80,128]{2,1,0:T(8,128)(2,1)S(1)}, bf16[16,80,128]{2,1,0:T(8,128)(2,1)S(1)}, u32[]{:S(2)}, u32[]{:S(2)}) %collective-permute-start.4) | collective-permute-done | bytes 327712 | tf_op jit(solution)/shard_map/ppermute | solution.py:748
  97.4 0.7 copy-done.5
  98.1 2.4 %shard_map.422 = (f32[4,41472]{1,0:T(4,128)}, bf16[10,10368]{1,0:T(8,128)(2,1)}) custom-call(s32[3]{0:T(128)} %pad_add_fusion.info, bf16[16,80,128]{2,1,0:T(8,128)(2,1)} %get-tuple-element.96.near, bf16[16,80,128]{2,1,0:T(8,128)(2,1)} %copy-done.5), custom_call_target="tpu_custom_call" | custom-call | bytes 9225000 | tf_op jit(solution)/shard_map/pallas_call | solution.py:750
  100.5 2.4 %all-to-all-done.3.own = bf16[16,144,128]{2,1,0:T(8,128)(2,1)S(1)} async-done(((bf16[16,144,128]{2,1,0:T(8,128)(2,1)}), bf16[16,144,128]{2,1,0:T(8,128)(2,1)S(1)}, u32[]{:S(2)}, u32[]{:S(2)}) %all-to-all-start.3) | async-done | bytes 589856 | tf_op jit(solution)/shard_map/all_to_all | solution.py:718
  102.9 3.2 %collective-permute-start.5 = (bf16[16,144,128]{2,1,0:T(8,128)(2,1)S(1)}, bf16[16,144,128]{2,1,0:T(8,128)(2,1)S(1)}, u32[]{:S(2)}, u32[]{:S(2)}) collective-permute-start(bf16[16,144,128]{2,1,0:T(8,128)(2,1)S(1)} %all-to-all-done.3.own), channel_id=1, source_target_pairs={{0,4},{4,0},{8,12},{12,8},{16,20},{20,16},{24,28},{28,24},{32,36},... | collective-permute-start | bytes 1769480 | tf_op jit(solution)/shard_map/ppermute | solution.py:767
  106.1 1.6 %collective-permute-done.5.other = bf16[16,144,128]{2,1,0:T(8,128)(2,1)S(1)} collective-permute-done((bf16[16,144,128]{2,1,0:T(8,128)(2,1)S(1)}, bf16[16,144,128]{2,1,0:T(8,128)(2,1)S(1)}, u32[]{:S(2)}, u32[]{:S(2)}) %collective-permute-start.5) | collective-permute-done | bytes 589856 | tf_op jit(solution)/shard_map/ppermute | solution.py:767
  107.8 0.8 copy-done.3
  108.6 2.8 %shard_map.423 = (f32[9,320,128]{2,1,0:T(8,128)}, f32[512,128]{1,0:T(8,128)}, f32[128,512]{1,0:T(8,128)}, f32[128,128]{1,0:T(8,128)}, f32[128,128]{1,0:T(8,128)}...) custom-call(s32[3]{0:T(128)} %pad_add_fusion.info, ...), custom_call_target="tpu_custom_call" | custom-call | bytes 10332000 | tf_op jit(solution)/shard_map/pallas_call | solution.py:794
  (54 shorter events, 0.2 us)
Async XLA Ops:
  0.7 12.2 %copy-start.2 = (bf16[320,9,128]{2,0,1:T(8,128)(2,1)S(1)}, bf16[320,9,128]{2,0,1:T(8,128)(2,1)}, u32[]{:S(2)}) copy-start(bf16[320,9,128]{2,0,1:T(8,128)(2,1)} %param.47) | copy-start | bytes 2211844
  3.2 22.5 %all-to-all-start = ((bf16[32,80,128]{2,1,0:T(8,128)(2,1)}), bf16[32,80,128]{2,1,0:T(8,128)(2,1)S(1)}, u32[]{:S(2)}, u32[]{:S(2)}) async-start(bf16[32,80,128]{2,1,0:T(8,128)(2,1)} %shard_map.416), calls=%async_computation | async-start | bytes 1310720 | tf_op jit(solution)/shard_map/all_to_all | solution.py:621
  12.9 2.8 %copy-start.12 = (bf16[320]{0:T(512)(128)(2,1)S(1)}, bf16[320]{0:T(512)(128)(2,1)}, u32[]{:S(2)}) copy-start(bf16[320]{0:T(512)(128)(2,1)} %param.48) | copy-start | bytes 1924
  12.9 3.5 %copy-start.9 = (bf16[32,384]{1,0:T(8,128)(2,1)S(1)}, bf16[32,384]{1,0:T(8,128)(2,1)}, u32[]{:S(2)}) copy-start(bf16[32,384]{1,0:T(8,128)(2,1)} %param.37) | copy-start | bytes 73732
  12.9 4.2 %copy-start.16 = (bf16[32]{0:T(256)(128)(2,1)S(1)}, bf16[32]{0:T(256)(128)(2,1)}, u32[]{:S(2)}) copy-start(bf16[32]{0:T(256)(128)(2,1)} %param.36) | copy-start | bytes 196
  12.9 4.8 %copy-start.17 = (s32[32]{0:T(128)S(1)}, s32[32]{0:T(128)}, u32[]{:S(2)}) copy-start(s32[32]{0:T(128)} %param.26) | copy-start | bytes 388
  12.9 6.1 %copy-start.18 = (bf16[128]{0:T(256)(128)(2,1)S(1)}, bf16[128]{0:T(256)(128)(2,1)}, u32[]{:S(2)}) copy-start(bf16[128]{0:T(256)(128)(2,1)} %param.28) | copy-start | bytes 772
  12.9 6.1 %copy-start.19 = (bf16[128]{0:T(256)(128)(2,1)S(1)}, bf16[128]{0:T(256)(128)(2,1)}, u32[]{:S(2)}) copy-start(bf16[128]{0:T(256)(128)(2,1)} %param.29) | copy-start | bytes 772
  12.9 6.1 %copy-start.20 = (bf16[128]{0:T(256)(128)(2,1)S(1)}, bf16[128]{0:T(256)(128)(2,1)}, u32[]{:S(2)}) copy-start(bf16[128]{0:T(256)(128)(2,1)} %param.31) | copy-start | bytes 772
  12.9 6.1 %copy-start.21 = (bf16[128]{0:T(256)(128)(2,1)S(1)}, bf16[128]{0:T(256)(128)(2,1)}, u32[]{:S(2)}) copy-start(bf16[128]{0:T(256)(128)(2,1)} %param.33) | copy-start | bytes 772
  13.0 6.1 %copy-start.22 = (bf16[128]{0:T(256)(128)(2,1)S(1)}, bf16[128]{0:T(256)(128)(2,1)}, u32[]{:S(2)}) copy-start(bf16[128]{0:T(256)(128)(2,1)} %param.40) | copy-start | bytes 772
  13.0 6.1 %copy-start.23 = (bf16[128]{0:T(256)(128)(2,1)S(1)}, bf16[128]{0:T(256)(128)(2,1)}, u32[]{:S(2)}) copy-start(bf16[128]{0:T(256)(128)(2,1)} %param.41) | copy-start | bytes 772
  13.0 6.1 %copy-start.24 = (bf16[128]{0:T(256)(128)(2,1)S(1)}, bf16[128]{0:T(256)(128)(2,1)}, u32[]{:S(2)}) copy-start(bf16[128]{0:T(256)(128)(2,1)} %param.42) | copy-start | bytes 772
  13.0 6.2 %copy-start.25 = (bf16[128]{0:T(256)(128)(2,1)S(1)}, bf16[128]{0:T(256)(128)(2,1)}, u32[]{:S(2)}) copy-start(bf16[128]{0:T(256)(128)(2,1)} %param.46) | copy-start | bytes 772
  13.0 6.2 %copy-start.13 = (bf16[512]{0:T(512)(128)(2,1)S(1)}, bf16[512]{0:T(512)(128)(2,1)}, u32[]{:S(2)}) copy-start(bf16[512]{0:T(512)(128)(2,1)} %param.44) | copy-start | bytes 3076
  13.0 6.2 %copy-start.14 = (bf16[384]{0:T(512)(128)(2,1)S(1)}, bf16[384]{0:T(512)(128)(2,1)}, u32[]{:S(2)}) copy-start(bf16[384]{0:T(512)(128)(2,1)} %param.38) | copy-start | bytes 2308
  13.0 6.9 %copy-start.15 = (s32[2,128]{1,0:T(2,128)S(1)}, s32[2,128]{1,0:T(2,128)}, u32[]{:S(2)}) copy-start(s32[2,128]{1,0:T(2,128)} %param.27) | copy-start | bytes 3076
  13.0 6.9 %copy-start.11 = (bf16[128,32]{0,1:T(8,128)(2,1)S(1)}, bf16[128,32]{0,1:T(8,128)(2,1)}, u32[]{:S(2)}) copy-start(bf16[128,32]{0,1:T(8,128)(2,1)} %param.35) | copy-start | bytes 24580
  19.9 5.8 %copy-start.10 = (f32[2176]{0:T(1024)}, f32[2176]{0:T(1024)S(1)}, u32[]{:S(2)}) copy-start(f32[2176]{0:T(1024)S(1)} %constant_dynamic-update-slice_fusion) | copy-start | bytes 26116
  25.7 0.8 copy-start
  48.3 3.1 %collective-permute-start = (bf16[16,144,128]{2,1,0:T(8,128)(2,1)}, bf16[16,144,128]{2,1,0:T(8,128)(2,1)S(1)}, u32[]{:S(2)}, u32[]{:S(2)}) collective-permute-start(bf16[16,144,128]{2,1,0:T(8,128)(2,1)} %get-tuple-element.63), channel_id=1, source_target_pairs={{0,4},{4,0},{8,12},{12,8},{16,20},{20,16},{24,28},{28,24},{32,36},... | collective-permute-start | bytes 1769480 | tf_op jit(solution)/shard_map/ppermute | solution.py:695
  51.5 0.8 copy-start.4
  71.3 15.5 %all-to-all-start.2 = ((bf16[16,2,80,128]{3,2,1,0:T(8,128)(2,1)}), bf16[16,2,80,128]{3,2,1,0:T(8,128)(2,1)S(1)}, u32[]{:S(2)}, u32[]{:S(2)}) async-start(bf16[16,2,80,128]{3,2,1,0:T(8,128)(2,1)} %bitcast.8), calls=%async_computation.2 | async-start | bytes 1310720 | tf_op jit(solution)/shard_map/all_to_all | solution.py:718
  76.7 4.8 %collective-permute-start.1 = (bf16[144,128]{1,0:T(8,128)(2,1)}, bf16[144,128]{1,0:T(8,128)(2,1)S(1)}, u32[]{:S(2)}, u32[]{:S(2)}) collective-permute-start(bf16[144,128]{1,0:T(8,128)(2,1)} %shard_map.420.mine), channel_id=1, source_target_pairs={{0,1},{1,2},{2,3},{3,0},{4,5},{5,6},{6,7},{7,4},{8,9},{9,10},{10,1... | collective-permute-start | bytes 110600 | tf_op jit(solution)/shard_map/ppermute | solution.py:734
  77.9 4.8 %collective-permute-start.2 = (bf16[144,128]{1,0:T(8,128)(2,1)}, bf16[144,128]{1,0:T(8,128)(2,1)S(1)}, u32[]{:S(2)}, u32[]{:S(2)}) collective-permute-start(bf16[144,128]{1,0:T(8,128)(2,1)} %shard_map.420.mine), channel_id=1, source_target_pairs={{0,2},{1,3},{2,0},{3,1},{4,6},{5,7},{6,4},{7,5},{8,10},{9,11},{10,... | collective-permute-start | bytes 110600 | tf_op jit(solution)/shard_map/ppermute | solution.py:734
  80.3 3.4 %collective-permute-start.3 = (bf16[144,128]{1,0:T(8,128)(2,1)}, bf16[144,128]{1,0:T(8,128)(2,1)S(1)}, u32[]{:S(2)}, u32[]{:S(2)}) collective-permute-start(bf16[144,128]{1,0:T(8,128)(2,1)} %shard_map.420.mine), channel_id=1, source_target_pairs={{0,3},{1,0},{2,1},{3,2},{4,7},{5,4},{6,5},{7,6},{8,11},{9,8},{10,9... | collective-permute-start | bytes 110600 | tf_op jit(solution)/shard_map/ppermute | solution.py:734
  81.5 2.2 %copy-start.6 = (bf16[144,128]{1,0:T(8,128)(2,1)}, bf16[144,128]{1,0:T(8,128)(2,1)S(1)}, u32[]{:S(2)}) copy-start(bf16[144,128]{1,0:T(8,128)(2,1)S(1)} %collective-permute-done.1.one) | copy-start | bytes 110596
  82.7 1.0 copy-start.7
  83.7 0.6 copy-start.8
  86.8 16.1 %all-to-all-start.3 = ((bf16[16,144,128]{2,1,0:T(8,128)(2,1)}), bf16[16,144,128]{2,1,0:T(8,128)(2,1)S(1)}, u32[]{:S(2)}, u32[]{:S(2)}) async-start(bf16[16,144,128]{2,1,0:T(8,128)(2,1)} %shard_map.421), calls=%async_computation.3 | async-start | bytes 1179648 | tf_op jit(solution)/shard_map/all_to_all | solution.py:718
  93.7 3.7 %collective-permute-start.4 = (bf16[16,80,128]{2,1,0:T(8,128)(2,1)S(1)}, bf16[16,80,128]{2,1,0:T(8,128)(2,1)S(1)}, u32[]{:S(2)}, u32[]{:S(2)}) collective-permute-start(bf16[16,80,128]{2,1,0:T(8,128)(2,1)S(1)} %get-tuple-element.95), channel_id=1, source_target_pairs={{0,4},{4,0},{8,12},{12,8},{16,20},{20,16},{24,28},{28,24},{32,36},... | collective-permute-start | bytes 983048 | tf_op jit(solution)/shard_map/ppermute | solution.py:748
  97.4 0.7 copy-start.5
  102.9 4.8 %copy-start.1 = (bf16[16,144,128]{2,1,0:T(8,128)(2,1)}, bf16[16,144,128]{2,1,0:T(8,128)(2,1)S(1)}, u32[]{:S(2)}) copy-start(bf16[16,144,128]{2,1,0:T(8,128)(2,1)S(1)} %all-to-all-done.3.own) | copy-start | bytes 1769476
  102.9 4.8 %collective-permute-start.5 = (bf16[16,144,128]{2,1,0:T(8,128)(2,1)S(1)}, bf16[16,144,128]{2,1,0:T(8,128)(2,1)S(1)}, u32[]{:S(2)}, u32[]{:S(2)}) collective-permute-start(bf16[16,144,128]{2,1,0:T(8,128)(2,1)S(1)} %all-to-all-done.3.own), channel_id=1, source_target_pairs={{0,4},{4,0},{8,12},{12,8},{16,20},{20,16},{24,28},{28,24},{32,36},... | collective-permute-start | bytes 1769480 | tf_op jit(solution)/shard_map/ppermute | solution.py:767
  107.7 0.8 copy-start.3

commit v3 on v2

--- a/solution.py
+++ b/solution.py
@@ -24,7 +24,6 @@
 OTILE = 3
 PIXROWS = 80
 WROWS = 144
-VMEM = 56 * 1024 * 1024
 
 F32 = jnp.float32
 BF16 = jnp.bfloat16
@@ -44,8 +43,8 @@
 VECTOR_SIZES = (CH,) * 8 + (FF, 3 * CH, OUT)
 
 
-def params(**kw):
-    return pltpu.CompilerParams(vmem_limit_bytes=VMEM, **kw)
+def params(mebibytes):
+    return pltpu.CompilerParams(vmem_limit_bytes=mebibytes * 1024 * 1024)
 
 
 def cost(micros):
@@ -616,7 +615,7 @@
             pltpu.VMEM((shards * PIXROWS, LANES), F32),
             pltpu.VMEM(cotangent.shape, F32),
         ],
-        compiler_params=params(),
+        compiler_params=params(8),
     )(features, cotangent)
     arrived = lax.all_to_all(chunks, "ch", split_axis=0, concat_axis=0, tiled=True)
 
@@ -673,7 +672,7 @@
             pltpu.VMEM((ROWS, FF), BF16),
             pltpu.VMEM((2, shards // 2, WROWS, LANES), F32),
         ],
-        compiler_params=params(),
+        compiler_params=params(42),
     )(
         info,
         arrived,
@@ -704,14 +703,14 @@
             pltpu.VMEM((CH, WIN * LANES), F32),
             pltpu.VMEM((shards * PIXROWS, LANES), F32),
         ],
-        compiler_params=params(),
+        compiler_params=params(10),
     )(info, grad, section_part)
     kept, pixels = lax.optimization_barrier((kept, pixels))
     partial = pl.pallas_call(
         pair_kernel,
         cost_estimate=cost(2.3),
         out_shape=jax.ShapeDtypeStruct(kept.shape, BF16),
-        compiler_params=params(),
+        compiler_params=params(8),
     )(kept, met)
 
     def exchange(v):
@@ -727,7 +726,7 @@
         add_kernel,
         cost_estimate=cost(1.7),
         out_shape=jax.ShapeDtypeStruct((WROWS, LANES), BF16),
-        compiler_params=params(),
+        compiler_params=params(4),
     )(parts)
     groups = lax.axis_size("img")
     other = [
@@ -738,7 +737,7 @@
         copies_kernel,
         cost_estimate=cost(1.7),
         out_shape=jax.ShapeDtypeStruct((shards // 2, WROWS, LANES), BF16),
-        compiler_params=params(),
+        compiler_params=params(4),
     )(mine, *other)
     copies, back = lax.optimization_barrier((copies, back))
     own_half = exchange(copies)
@@ -760,7 +759,7 @@
             pltpu.VMEM(cotangent.shape, F32),
             pltpu.VMEM((shards, PIXROWS, LANES), BF16),
         ],
-        compiler_params=params(),
+        compiler_params=params(8),
     )(info, near, far)
 
     own_half, features_grad, section = lax.optimization_barrier((own_half, features_grad, section))
@@ -810,7 +809,7 @@
         in_specs=[pl.BlockSpec(memory_space=pltpu.SMEM)] + [whole] * 2,
         out_specs=(whole,) * 21,
         scratch_shapes=[pltpu.VMEM((shards, WROWS, LANES), BF16)],
-        compiler_params=params(),
+        compiler_params=params(12),
     )(info, own_half, other_half)
     return (
         section,

time: 112 us -> 98.8 us (0.88)
  Pallas kernels: 37.8 us -> 27.3 us
  waiting for transfers between devices: 13.6 us -> 19.8 us
  local copies, waits for them, and re-layouts: 9.42 us -> 4.84 us
  blocking collectives: 16.7 us -> 14.2 us
  other arithmetic: 1.98 us -> 0.17 us
    all_to_all x1, waiting for transfers between devices: 5.2 us -> 8.8 us  [body(): lax.all_to_all(chunks, 'ch', split_axis=0, concat_axis=0, tiled=True)]
    all_to_all x2, waiting for transfers between devices: 3.25 us -> 6.12 us  [exchange(): lax.all_to_all(v, 'ch', split_axis=0, concat_axis=0, tiled=True, axis_ind...]
    pallas_call x1, Pallas kernels: 21.8 us -> 19.2 us  [body(): pl.pallas_call(main_kernel, cost_estimate=cost(22), out_shape=(jax.ShapeD...]
    all_to_all x2, starting transfers between devices: 9.66 us -> 7.18 us  [exchange(): lax.all_to_all(v, 'ch', split_axis=0, concat_axis=0, tiled=True, axis_ind...]
    all_to_all x1, blocking collectives: 16.7 us -> 14.2 us  [exchange(): lax.all_to_all(v, 'ch', split_axis=0, concat_axis=0, tiled=True, axis_ind...]
    pallas_call x1, Pallas kernels: 2.33 us -> 0.16 us  [body(): pl.pallas_call(pair_kernel, cost_estimate=cost(2.3), out_shape=jax.ShapeD...]
    unnamed x53 -> x51, local copies, waits for them, and re-layouts: 5.12 us -> 3.19 us
    pallas_call x1, Pallas kernels: 1.76 us -> 0.08 us  [body(): pl.pallas_call(add_kernel, cost_estimate=cost(1.7), out_shape=jax.ShapeDt...]
  transfers between devices with their start and end apart: 9 -> 9, of which waited for: 7 -> 7; matrix products, arithmetic and copies ran while one was open for 7% -> 3% of each run, Pallas kernels for 8% -> 5%
where the time goes in v3:
time: 98.8 us; the launch traced here: 98.3 us
  starting transfers between devices  30.3 us (31%)
  Pallas kernels  27.3 us (28%)
  waiting for transfers between devices  19.8 us (20%)
  blocking collectives  14.2 us (14%)
  local copies, waits for them, and re-layouts  4.84 us (5%)
  between operations  1.87 us (2%)
    pallas_call x1, Pallas kernels, body(): pl.pallas_call(main_kernel, cost_estimate=cost(22), out_shape=(jax.ShapeD...  19.2 us
    all_to_all x1, blocking collectives, exchange(): lax.all_to_all(v, 'ch', split_axis=0, concat_axis=0, tiled=True, axis_ind...  14.2 us
    all_to_all x1, starting transfers between devices, body(): lax.all_to_all(chunks, 'ch', split_axis=0, concat_axis=0, tiled=True)  9.6 us
    all_to_all x1, waiting for transfers between devices, body(): lax.all_to_all(chunks, 'ch', split_axis=0, concat_axis=0, tiled=True)  8.8 us
    all_to_all x2, starting transfers between devices, exchange(): lax.all_to_all(v, 'ch', split_axis=0, concat_axis=0, tiled=True, axis_ind...  7.18 us
    all_to_all x2, waiting for transfers between devices, exchange(): lax.all_to_all(v, 'ch', split_axis=0, concat_axis=0, tiled=True, axis_ind...  6.12 us
    ppermute x3, starting transfers between devices, body(): lax.ppermute(mine, 'img', [(i, (i + d) % groups) for i in range(groups)])  4.88 us
    ppermute x1, starting transfers between devices, body(): other_half = lax.ppermute(own_half, 'ch', other_core)  4.54 us
  transfers between devices with their start and end apart: 9, of which 7 were waited for; matrix products, arithmetic and copies ran while one was open for 3% of the time, Pallas kernels for 5%

profile of v3, /device:TPU:1, one launch (start us, length us, event | category | flops | bytes accessed | tf_op | source)
XLA Modules:
  0.0 98.3 jit_solution(1666425018293577648)
XLA Ops:
  0.7 1.0 copy-done
  1.6 1.0 copy-done.1
  2.6 1.2 %shard_map.416 = bf16[32,80,128]{2,1,0:T(8,128)(2,1)} custom-call(bf16[4,41472]{1,0:T(4,128)(2,1)S(1)} %copy-done, bf16[10,10368]{1,0:T(8,128)(2,1)S(1)} %copy-done.1), custom_call_target="tpu_custom_call" | custom-call | bytes 9225000 | tf_op jit(solution)/shard_map/pallas_call | solution.py:610
  3.8 9.6 %all-to-all-start = ((bf16[32,80,128]{2,1,0:T(8,128)(2,1)}), bf16[32,80,128]{2,1,0:T(8,128)(2,1)S(1)}, u32[]{:S(2)}, u32[]{:S(2)}) async-start(bf16[32,80,128]{2,1,0:T(8,128)(2,1)} %shard_map.416), calls=%async_computation | async-start | bytes 1310720 | tf_op jit(solution)/shard_map/all_to_all | solution.py:620
  13.4 0.0 copy-start.11
  13.5 0.0 copy-start.9
  13.5 0.0 copy-start.15
  13.5 0.0 copy-start.16
  13.5 0.0 copy-start.18
  13.5 0.0 copy-start.19
  13.6 0.0 copy-start.22
  13.6 0.0 copy-start.23
  13.6 0.0 copy-start.12
  13.6 0.0 copy-start.13
  13.6 0.0 copy-start.2
  13.7 0.0 copy-start.3
  13.7 0.0 copy-start.6
  13.7 0.0 copy-start.7
  13.7 1.1 %copy.56 = bf16[320,9,128]{0,2,1:T(8,128)(2,1)S(1)} copy(bf16[320,9,128]{2,0,1:T(8,128)(2,1)S(1)} %copy-done.8) | data formatting | bytes 1474560 | tf_op args[22]
  14.8 0.8 copy.59.kw
  15.7 0.1 reshape.69.kbias
  15.8 0.1 copy.57.sqb
  15.9 0.6 dynamic_slice.11
  17.4 0.1 pad_add_fusion.info
  17.5 8.8 %all-to-all-done.recv = bf16[32,80,128]{2,1,0:T(8,128)(2,1)S(1)} async-done(((bf16[32,80,128]{2,1,0:T(8,128)(2,1)}), bf16[32,80,128]{2,1,0:T(8,128)(2,1)S(1)}, u32[]{:S(2)}, u32[]{:S(2)}) %all-to-all-start) | async-done | bytes 655392 | tf_op jit(solution)/shard_map/all_to_all | solution.py:620
  26.4 19.2 %shard_map.417 = (f32[16,144,128]{2,1,0:T(8,128)S(1)}, bf16[16,144,128]{2,1,0:T(8,128)(2,1)S(1)}, f32[1440,128]{1,0:T(8,128)S(1)}, f32[320,384]{1,0:T(8,128)S(1)}) custom-call(s32[3]{0:T(128)S(1)} %pad_add_fusion.info, bf16[32,80,128]{2,1,0:T(8,128)(2,1)S(1)} %all-to-all-done.recv, f32[17,128]{1,0:T(8,128)S(1)} %bitcast.20, ...), custom_call_target="tpu_custom_call" | custom-call | bytes 81180000 | tf_op jit(solution)/shard_map/pallas_call | solution.py:626
  45.6 0.6 collective-permute-start
  46.2 1.8 %shard_map.418 = bf16[32,80,128]{2,1,0:T(8,128)(2,1)} custom-call(s32[3]{0:T(128)S(1)} %pad_add_fusion.info, f32[1440,128]{1,0:T(8,128)S(1)} %get-tuple-element.60.grad, f32[320,384]{1,0:T(8,128)S(1)} %get-tuple-element.61.section), custom_call_target="tpu_custom_call" | custom-call | bytes 9225000 | tf_op jit(solution)/shard_map/pallas_call | solution.py:695
  48.0 0.2 shard_map.419
  48.2 14.2 %all_to_all.20.recv = bf16[16,144,128]{2,1,0:T(8,128)(2,1)S(1)} all-to-all(bf16[16,144,128]{2,1,0:T(8,128)(2,1)S(1)} %shard_map.419), channel_id=1, replica_groups={{0,8,16,24,32,40,48,56,64,72,80,88,96,104,112,120},{4,12,20,28,36,44,52..., dimensions={0} | all-to-all | bytes 1179648 | tf_op jit(solution)/shard_map/all_to_all | solution.py:717
  62.4 3.6 %all-to-all-start.2 = ((bf16[16,2,80,128]{3,2,1,0:T(8,128)(2,1)}), bf16[16,2,80,128]{3,2,1,0:T(8,128)(2,1)S(1)}, u32[]{:S(2)}, u32[]{:S(2)}) async-start(bf16[16,2,80,128]{3,2,1,0:T(8,128)(2,1)} %bitcast.8), calls=%async_computation.2 | async-start | bytes 1310720 | tf_op jit(solution)/shard_map/all_to_all | solution.py:717
  66.0 0.1 shard_map.420.mine
  66.1 1.3 %collective-permute-start.1 = (bf16[144,128]{1,0:T(8,128)(2,1)S(1)}, bf16[144,128]{1,0:T(8,128)(2,1)S(1)}, u32[]{:S(2)}, u32[]{:S(2)}) collective-permute-start(bf16[144,128]{1,0:T(8,128)(2,1)S(1)} %shard_map.420.mine), channel_id=1, source_target_pairs={{0,1},{1,2},{2,3},{3,0},{4,5},{5,6},{6,7},{7,4},{8,9},{9,10},{10,1... | collective-permute-start | bytes 110600 | tf_op jit(solution)/shard_map/ppermute | solution.py:733
  67.4 2.4 %collective-permute-start.2 = (bf16[144,128]{1,0:T(8,128)(2,1)S(1)}, bf16[144,128]{1,0:T(8,128)(2,1)S(1)}, u32[]{:S(2)}, u32[]{:S(2)}) collective-permute-start(bf16[144,128]{1,0:T(8,128)(2,1)S(1)} %shard_map.420.mine), channel_id=1, source_target_pairs={{0,2},{1,3},{2,0},{3,1},{4,6},{5,7},{6,4},{7,5},{8,10},{9,11},{10,... | collective-permute-start | bytes 110600 | tf_op jit(solution)/shard_map/ppermute | solution.py:733
  69.8 1.2 %collective-permute-start.3 = (bf16[144,128]{1,0:T(8,128)(2,1)S(1)}, bf16[144,128]{1,0:T(8,128)(2,1)S(1)}, u32[]{:S(2)}, u32[]{:S(2)}) collective-permute-start(bf16[144,128]{1,0:T(8,128)(2,1)S(1)} %shard_map.420.mine), channel_id=1, source_target_pairs={{0,3},{1,0},{2,1},{3,2},{4,7},{5,4},{6,5},{7,6},{8,11},{9,8},{10,9... | collective-permute-start | bytes 110600 | tf_op jit(solution)/shard_map/ppermute | solution.py:733
  71.0 0.7 collective-permute-done.2.two
  71.7 1.2 %collective-permute-done.3.three = bf16[144,128]{1,0:T(8,128)(2,1)S(1)} collective-permute-done((bf16[144,128]{1,0:T(8,128)(2,1)S(1)}, bf16[144,128]{1,0:T(8,128)(2,1)S(1)}, u32[]{:S(2)}, u32[]{:S(2)}) %collective-permute-start.3) | collective-permute-done | bytes 36896 | tf_op jit(solution)/shard_map/ppermute | solution.py:733
  72.9 0.9 shard_map.421
  73.8 3.4 %all-to-all-done.2 = bf16[16,2,80,128]{3,2,1,0:T(8,128)(2,1)S(1)} async-done(((bf16[16,2,80,128]{3,2,1,0:T(8,128)(2,1)}), bf16[16,2,80,128]{3,2,1,0:T(8,128)(2,1)S(1)}, u32[]{:S(2)}, u32[]{:S(2)}) %all-to-all-start.2) | async-done | bytes 655392 | tf_op jit(solution)/shard_map/all_to_all | solution.py:717
  77.2 3.6 %all-to-all-start.3 = ((bf16[16,144,128]{2,1,0:T(8,128)(2,1)}), bf16[16,144,128]{2,1,0:T(8,128)(2,1)S(1)}, u32[]{:S(2)}, u32[]{:S(2)}) async-start(bf16[16,144,128]{2,1,0:T(8,128)(2,1)} %shard_map.421), calls=%async_computation.3 | async-start | bytes 1179648 | tf_op jit(solution)/shard_map/all_to_all | solution.py:717
  80.8 0.1 dynamic-slice_bitcast_fusion
  80.8 3.4 %collective-permute-start.4 = (bf16[16,80,128]{2,1,0:T(8,128)(2,1)S(1)}, bf16[16,80,128]{2,1,0:T(8,128)(2,1)S(1)}, u32[]{:S(2)}, u32[]{:S(2)}) collective-permute-start(bf16[16,80,128]{2,1,0:T(8,128)(2,1)S(1)} %get-tuple-element.95), channel_id=1, source_target_pairs={{0,4},{4,0},{8,12},{12,8},{16,20},{20,16},{24,28},{28,24},{32,36},... | collective-permute-start | bytes 983048 | tf_op jit(solution)/shard_map/ppermute | solution.py:747
  84.3 1.3 %collective-permute-done.4.far = bf16[16,80,128]{2,1,0:T(8,128)(2,1)S(1)} collective-permute-done((bf16[16,80,128]{2,1,0:T(8,128)(2,1)S(1)}, bf16[16,80,128]{2,1,0:T(8,128)(2,1)S(1)}, u32[]{:S(2)}, u32[]{:S(2)}) %collective-permute-start.4) | collective-permute-done | bytes 327712 | tf_op jit(solution)/shard_map/ppermute | solution.py:747
  85.5 1.8 %shard_map.422 = (f32[4,41472]{1,0:T(4,128)}, bf16[10,10368]{1,0:T(8,128)(2,1)}) custom-call(s32[3]{0:T(128)S(1)} %pad_add_fusion.info, bf16[16,80,128]{2,1,0:T(8,128)(2,1)S(1)} %get-tuple-element.96.near, bf16[16,80,128]{2,1,0:T(8,128)(2,1)S(1)} %collective-permute-done.4.far), custom_call_target="tpu_custom_call" | custom-call | bytes 9225000 | tf_op jit(solution)/shard_map/pallas_call | solution.py:749
  87.4 2.7 %all-to-all-done.3.own = bf16[16,144,128]{2,1,0:T(8,128)(2,1)S(1)} async-done(((bf16[16,144,128]{2,1,0:T(8,128)(2,1)}), bf16[16,144,128]{2,1,0:T(8,128)(2,1)S(1)}, u32[]{:S(2)}, u32[]{:S(2)}) %all-to-all-start.3) | async-done | bytes 589856 | tf_op jit(solution)/shard_map/all_to_all | solution.py:717
  90.1 4.5 %collective-permute-start.5 = (bf16[16,144,128]{2,1,0:T(8,128)(2,1)S(1)}, bf16[16,144,128]{2,1,0:T(8,128)(2,1)S(1)}, u32[]{:S(2)}, u32[]{:S(2)}) collective-permute-start(bf16[16,144,128]{2,1,0:T(8,128)(2,1)S(1)} %all-to-all-done.3.own), channel_id=1, source_target_pairs={{0,4},{4,0},{8,12},{12,8},{16,20},{20,16},{24,28},{28,24},{32,36},... | collective-permute-start | bytes 1769480 | tf_op jit(solution)/shard_map/ppermute | solution.py:766
  94.6 1.6 %collective-permute-done.5.other = bf16[16,144,128]{2,1,0:T(8,128)(2,1)S(1)} collective-permute-done((bf16[16,144,128]{2,1,0:T(8,128)(2,1)S(1)}, bf16[16,144,128]{2,1,0:T(8,128)(2,1)S(1)}, u32[]{:S(2)}, u32[]{:S(2)}) %collective-permute-start.5) | collective-permute-done | bytes 589856 | tf_op jit(solution)/shard_map/ppermute | solution.py:766
  96.3 2.1 %shard_map.423 = (f32[9,320,128]{2,1,0:T(8,128)}, f32[512,128]{1,0:T(8,128)}, f32[128,512]{1,0:T(8,128)}, f32[128,128]{1,0:T(8,128)}, f32[128,128]{1,0:T(8,128)}...) custom-call(s32[3]{0:T(128)S(1)} %pad_add_fusion.info, ...), custom_call_target="tpu_custom_call" | custom-call | bytes 10332000 | tf_op jit(solution)/shard_map/pallas_call | solution.py:793
  (52 shorter events, 0.2 us)
Async XLA Ops:
  0.7 1.0 copy-start
  1.6 1.0 copy-start.1
  2.6 10.8 %copy-start.8 = (bf16[320,9,128]{2,0,1:T(8,128)(2,1)S(1)}, bf16[320,9,128]{2,0,1:T(8,128)(2,1)}, u32[]{:S(2)}) copy-start(bf16[320,9,128]{2,0,1:T(8,128)(2,1)} %param.47) | copy-start | bytes 2211844
  3.8 22.5 %all-to-all-start = ((bf16[32,80,128]{2,1,0:T(8,128)(2,1)}), bf16[32,80,128]{2,1,0:T(8,128)(2,1)S(1)}, u32[]{:S(2)}, u32[]{:S(2)}) async-start(bf16[32,80,128]{2,1,0:T(8,128)(2,1)} %shard_map.416), calls=%async_computation | async-start | bytes 1310720 | tf_op jit(solution)/shard_map/all_to_all | solution.py:620
  13.4 2.2 %copy-start.11 = (bf16[320]{0:T(512)(128)(2,1)S(1)}, bf16[320]{0:T(512)(128)(2,1)}, u32[]{:S(2)}) copy-start(bf16[320]{0:T(512)(128)(2,1)} %param.48) | copy-start | bytes 1924
  13.5 2.3 %copy-start.9 = (bf16[32,384]{1,0:T(8,128)(2,1)S(1)}, bf16[32,384]{1,0:T(8,128)(2,1)}, u32[]{:S(2)}) copy-start(bf16[32,384]{1,0:T(8,128)(2,1)} %param.37) | copy-start | bytes 73732
  13.5 2.3 %copy-start.15 = (bf16[32]{0:T(256)(128)(2,1)S(1)}, bf16[32]{0:T(256)(128)(2,1)}, u32[]{:S(2)}) copy-start(bf16[32]{0:T(256)(128)(2,1)} %param.36) | copy-start | bytes 196
  13.5 2.4 %copy-start.16 = (s32[32]{0:T(128)S(1)}, s32[32]{0:T(128)}, u32[]{:S(2)}) copy-start(s32[32]{0:T(128)} %param.26) | copy-start | bytes 388
  13.5 3.7 %copy-start.17 = (bf16[128]{0:T(256)(128)(2,1)S(1)}, bf16[128]{0:T(256)(128)(2,1)}, u32[]{:S(2)}) copy-start(bf16[128]{0:T(256)(128)(2,1)} %param.28) | copy-start | bytes 772
  13.5 3.7 %copy-start.18 = (bf16[128]{0:T(256)(128)(2,1)S(1)}, bf16[128]{0:T(256)(128)(2,1)}, u32[]{:S(2)}) copy-start(bf16[128]{0:T(256)(128)(2,1)} %param.29) | copy-start | bytes 772
  13.5 3.7 %copy-start.19 = (bf16[128]{0:T(256)(128)(2,1)S(1)}, bf16[128]{0:T(256)(128)(2,1)}, u32[]{:S(2)}) copy-start(bf16[128]{0:T(256)(128)(2,1)} %param.31) | copy-start | bytes 772
  13.5 3.7 %copy-start.20 = (bf16[128]{0:T(256)(128)(2,1)S(1)}, bf16[128]{0:T(256)(128)(2,1)}, u32[]{:S(2)}) copy-start(bf16[128]{0:T(256)(128)(2,1)} %param.33) | copy-start | bytes 772
  13.5 3.7 %copy-start.21 = (bf16[128]{0:T(256)(128)(2,1)S(1)}, bf16[128]{0:T(256)(128)(2,1)}, u32[]{:S(2)}) copy-start(bf16[128]{0:T(256)(128)(2,1)} %param.40) | copy-start | bytes 772
  13.6 3.7 %copy-start.22 = (bf16[128]{0:T(256)(128)(2,1)S(1)}, bf16[128]{0:T(256)(128)(2,1)}, u32[]{:S(2)}) copy-start(bf16[128]{0:T(256)(128)(2,1)} %param.41) | copy-start | bytes 772
  13.6 3.7 %copy-start.23 = (bf16[128]{0:T(256)(128)(2,1)S(1)}, bf16[128]{0:T(256)(128)(2,1)}, u32[]{:S(2)}) copy-start(bf16[128]{0:T(256)(128)(2,1)} %param.42) | copy-start | bytes 772
  13.6 3.7 %copy-start.24 = (bf16[128]{0:T(256)(128)(2,1)S(1)}, bf16[128]{0:T(256)(128)(2,1)}, u32[]{:S(2)}) copy-start(bf16[128]{0:T(256)(128)(2,1)} %param.46) | copy-start | bytes 772
  13.6 3.8 %copy-start.12 = (bf16[512]{0:T(512)(128)(2,1)S(1)}, bf16[512]{0:T(512)(128)(2,1)}, u32[]{:S(2)}) copy-start(bf16[512]{0:T(512)(128)(2,1)} %param.44) | copy-start | bytes 3076
  13.6 3.8 %copy-start.13 = (bf16[384]{0:T(512)(128)(2,1)S(1)}, bf16[384]{0:T(512)(128)(2,1)}, u32[]{:S(2)}) copy-start(bf16[384]{0:T(512)(128)(2,1)} %param.38) | copy-start | bytes 2308
  13.6 3.9 %copy-start.14 = (s32[2,128]{1,0:T(2,128)S(1)}, s32[2,128]{1,0:T(2,128)}, u32[]{:S(2)}) copy-start(s32[2,128]{1,0:T(2,128)} %param.27) | copy-start | bytes 3076
  13.6 3.9 %copy-start.10 = (bf16[128,32]{0,1:T(8,128)(2,1)S(1)}, bf16[128,32]{0,1:T(8,128)(2,1)}, u32[]{:S(2)}) copy-start(bf16[128,32]{0,1:T(8,128)(2,1)} %param.35) | copy-start | bytes 24580
  13.6 12.7 %copy-start.2 = (bf16[128,512]{1,0:T(8,128)(2,1)S(1)}, bf16[128,512]{1,0:T(8,128)(2,1)}, u32[]{:S(2)}) copy-start(bf16[128,512]{1,0:T(8,128)(2,1)} %xw.1) | copy-start | bytes 393220
  13.7 12.7 %copy-start.3 = (bf16[512,128]{1,0:T(8,128)(2,1)S(1)}, bf16[512,128]{1,0:T(8,128)(2,1)}, u32[]{:S(2)}) copy-start(bf16[512,128]{1,0:T(8,128)(2,1)} %rw.1) | copy-start | bytes 393220
  13.7 12.7 %copy-start.4 = (bf16[128,128]{1,0:T(8,128)(2,1)S(1)}, bf16[128,128]{1,0:T(8,128)(2,1)}, u32[]{:S(2)}) copy-start(bf16[128,128]{1,0:T(8,128)(2,1)} %hw.1) | copy-start | bytes 98308
  13.7 12.7 %copy-start.5 = (bf16[128,128]{1,0:T(8,128)(2,1)S(1)}, bf16[128,128]{1,0:T(8,128)(2,1)}, u32[]{:S(2)}) copy-start(bf16[128,128]{1,0:T(8,128)(2,1)} %ww.1) | copy-start | bytes 98308
  13.7 12.7 %copy-start.6 = (bf16[128,128]{1,0:T(8,128)(2,1)S(1)}, bf16[128,128]{1,0:T(8,128)(2,1)}, u32[]{:S(2)}) copy-start(bf16[128,128]{1,0:T(8,128)(2,1)} %cw.1) | copy-start | bytes 98308
  13.7 12.7 %copy-start.7 = (bf16[128,128]{1,0:T(8,128)(2,1)S(1)}, bf16[128,128]{1,0:T(8,128)(2,1)}, u32[]{:S(2)}) copy-start(bf16[128,128]{1,0:T(8,128)(2,1)} %ow.1) | copy-start | bytes 98308
  45.6 2.5 %collective-permute-start = (bf16[16,144,128]{2,1,0:T(8,128)(2,1)S(1)}, bf16[16,144,128]{2,1,0:T(8,128)(2,1)S(1)}, u32[]{:S(2)}, u32[]{:S(2)}) collective-permute-start(bf16[16,144,128]{2,1,0:T(8,128)(2,1)S(1)} %get-tuple-element.63), channel_id=1, source_target_pairs={{0,4},{4,0},{8,12},{12,8},{16,20},{20,16},{24,28},{28,24},{32,36},... | collective-permute-start | bytes 1769480 | tf_op jit(solution)/shard_map/ppermute | solution.py:694
  62.4 14.8 %all-to-all-start.2 = ((bf16[16,2,80,128]{3,2,1,0:T(8,128)(2,1)}), bf16[16,2,80,128]{3,2,1,0:T(8,128)(2,1)S(1)}, u32[]{:S(2)}, u32[]{:S(2)}) async-start(bf16[16,2,80,128]{3,2,1,0:T(8,128)(2,1)} %bitcast.8), calls=%async_computation.2 | async-start | bytes 1310720 | tf_op jit(solution)/shard_map/all_to_all | solution.py:717
  66.1 4.9 %collective-permute-start.1 = (bf16[144,128]{1,0:T(8,128)(2,1)S(1)}, bf16[144,128]{1,0:T(8,128)(2,1)S(1)}, u32[]{:S(2)}, u32[]{:S(2)}) collective-permute-start(bf16[144,128]{1,0:T(8,128)(2,1)S(1)} %shard_map.420.mine), channel_id=1, source_target_pairs={{0,1},{1,2},{2,3},{3,0},{4,5},{5,6},{6,7},{7,4},{8,9},{9,10},{10,1... | collective-permute-start | bytes 110600 | tf_op jit(solution)/shard_map/ppermute | solution.py:733
  67.4 4.3 %collective-permute-start.2 = (bf16[144,128]{1,0:T(8,128)(2,1)S(1)}, bf16[144,128]{1,0:T(8,128)(2,1)S(1)}, u32[]{:S(2)}, u32[]{:S(2)}) collective-permute-start(bf16[144,128]{1,0:T(8,128)(2,1)S(1)} %shard_map.420.mine), channel_id=1, source_target_pairs={{0,2},{1,3},{2,0},{3,1},{4,6},{5,7},{6,4},{7,5},{8,10},{9,11},{10,... | collective-permute-start | bytes 110600 | tf_op jit(solution)/shard_map/ppermute | solution.py:733
  69.8 3.1 %collective-permute-start.3 = (bf16[144,128]{1,0:T(8,128)(2,1)S(1)}, bf16[144,128]{1,0:T(8,128)(2,1)S(1)}, u32[]{:S(2)}, u32[]{:S(2)}) collective-permute-start(bf16[144,128]{1,0:T(8,128)(2,1)S(1)} %shard_map.420.mine), channel_id=1, source_target_pairs={{0,3},{1,0},{2,1},{3,2},{4,7},{5,4},{6,5},{7,6},{8,11},{9,8},{10,9... | collective-permute-start | bytes 110600 | tf_op jit(solution)/shard_map/ppermute | solution.py:733
  77.2 12.9 %all-to-all-start.3 = ((bf16[16,144,128]{2,1,0:T(8,128)(2,1)}), bf16[16,144,128]{2,1,0:T(8,128)(2,1)S(1)}, u32[]{:S(2)}, u32[]{:S(2)}) async-start(bf16[16,144,128]{2,1,0:T(8,128)(2,1)} %shard_map.421), calls=%async_computation.3 | async-start | bytes 1179648 | tf_op jit(solution)/shard_map/all_to_all | solution.py:717
  80.8 4.7 %collective-permute-start.4 = (bf16[16,80,128]{2,1,0:T(8,128)(2,1)S(1)}, bf16[16,80,128]{2,1,0:T(8,128)(2,1)S(1)}, u32[]{:S(2)}, u32[]{:S(2)}) collective-permute-start(bf16[16,80,128]{2,1,0:T(8,128)(2,1)S(1)} %get-tuple-element.95), channel_id=1, source_target_pairs={{0,4},{4,0},{8,12},{12,8},{16,20},{20,16},{24,28},{28,24},{32,36},... | collective-permute-start | bytes 983048 | tf_op jit(solution)/shard_map/ppermute | solution.py:747
  90.1 6.2 %collective-permute-start.5 = (bf16[16,144,128]{2,1,0:T(8,128)(2,1)S(1)}, bf16[16,144,128]{2,1,0:T(8,128)(2,1)S(1)}, u32[]{:S(2)}, u32[]{:S(2)}) collective-permute-start(bf16[16,144,128]{2,1,0:T(8,128)(2,1)S(1)} %all-to-all-done.3.own), channel_id=1, source_target_pairs={{0,4},{4,0},{8,12},{12,8},{16,20},{20,16},{24,28},{28,24},{32,36},... | collective-permute-start | bytes 1769480 | tf_op jit(solution)/shard_map/ppermute | solution.py:766

commit v4 on v3

--- a/solution.py
+++ b/solution.py
@@ -16,7 +16,7 @@
 WIDE = 40
 FLAT = SIDE * WIDE
 GUARD = 48
-ROWS = 288
+ROWS = 1440
 STEPS = FLAT // ROWS
 EPS = 1e-05
 LANES = 128
@@ -76,20 +76,17 @@
 
 
 def normal_parts(x):
-    z = jnp.abs(x) * 0.7071067811865476
-    t = 1.0 / (1.0 + 0.3275911 * z)
-    bell = jnp.exp(-z * z)
-    poly = 1.061405429 * t - 1.453152027
-    poly = poly * t + 1.421413741
-    poly = poly * t - 0.284496736
-    poly = poly * t + 0.254829592
-    tail = 0.5 * poly * t * bell
-    return jnp.where(x < 0, tail, 1.0 - tail), bell * 0.3989422804014327
-
-
-def pack_kernel(feat, cot, out, stage, cots):
+    cdf = 0.5 + 0.5 * lax.erf(x * 0.7071067811865476)
+    return cdf, (x * 0.3989422804014327) * jnp.exp(x * (x * -0.5))
+
+
+def pack_kernel(feat_hbm, cot_hbm, out, stage, cots, feat, cot, ready):
     images = out.shape[0]
-    cots[...] = cot[...].astype(F32)
+    first = pltpu.make_async_copy(feat_hbm, feat, ready.at[0])
+    second = pltpu.make_async_copy(cot_hbm, cot, ready.at[1])
+    first.start()
+    second.start()
+    first.wait()
     for k in range(images):
         base = k * PIXROWS
         begin = first_tile(k) * LANES
@@ -97,6 +94,10 @@
             stage[base + 4 * t : base + 4 * t + 4, :] = feat[
                 :, begin + t * LANES : begin + (t + 1) * LANES
             ].astype(F32)
+    second.wait()
+    cots[...] = cot[...].astype(F32)
+    for k in range(images):
+        base = k * PIXROWS
         for j in range(OTILE):
             width = min(LANES, OPIX - j * LANES)
             at = k * OPIX + j * LANES
@@ -262,7 +263,7 @@
     inner_pre = jnp.sum(sqt[...] * means, axis=1, keepdims=True) + sqb[...]
     inner_cdf, inner_density = normal_parts(inner_pre)
     inner = inner_pre * inner_cdf
-    inner_slope = inner_cdf + inner_pre * inner_density
+    inner_slope = inner_cdf + inner_density
     logit = [col_sum(exw[:, j * CH : (j + 1) * CH] * inner) + vec(12 + j) for j in range(3)]
     top = jnp.maximum(jnp.maximum(logit[0], logit[1]), logit[2])
     grown = [jnp.exp(v - top) for v in logit]
@@ -289,7 +290,7 @@
             cdf, density = normal_parts(pre)
             hid = (pre * cdf).astype(BF16)
             hidden_b[here, lanes] = hid
-            slope[here, lanes] = cdf + pre * density
+            slope[here, lanes] = cdf + density
         total2 = total2 + nn(hidden_b[here, :], rw[...])
         value = jnp.where(valid[here, :] > 0, total2, 0.0)
         block[guarded(i), :] = value.astype(BF16).astype(F32)
@@ -607,22 +608,27 @@
         ]
     ).reshape(17, CH)
 
+    whole = pl.BlockSpec(memory_space=pltpu.VMEM)
     chunks = pl.pallas_call(
         pack_kernel,
         cost_estimate=cost(2.5),
         out_shape=jax.ShapeDtypeStruct((shards, PIXROWS, LANES), BF16),
+        in_specs=[pl.BlockSpec(memory_space=pltpu.HBM)] * 2,
+        out_specs=whole,
         scratch_shapes=[
             pltpu.VMEM((shards * PIXROWS, LANES), F32),
             pltpu.VMEM(cotangent.shape, F32),
+            pltpu.VMEM(features.shape, BF16),
+            pltpu.VMEM(cotangent.shape, BF16),
+            pltpu.SemaphoreType.DMA((2,)),
         ],
-        compiler_params=params(8),
+        compiler_params=params(56),
     )(features, cotangent)
     arrived = lax.all_to_all(chunks, "ch", split_axis=0, concat_axis=0, tiled=True)
 
     canvas = pltpu.VMEM((FLAT, CH), F32)
     guarded = pltpu.VMEM((FLAT + 2 * GUARD, CH), F32)
     narrow = pltpu.VMEM((FLAT, CH), BF16)
-    whole = pl.BlockSpec(memory_space=pltpu.VMEM)
     kept, sent, grad, section_part = pl.pallas_call(
         main_kernel,
         cost_estimate=cost(22),
@@ -703,14 +709,14 @@
             pltpu.VMEM((CH, WIN * LANES), F32),
             pltpu.VMEM((shards * PIXROWS, LANES), F32),
         ],
-        compiler_params=params(10),
+        compiler_params=params(8),
     )(info, grad, section_part)
     kept, pixels = lax.optimization_barrier((kept, pixels))
     partial = pl.pallas_call(
         pair_kernel,
         cost_estimate=cost(2.3),
         out_shape=jax.ShapeDtypeStruct(kept.shape, BF16),
-        compiler_params=params(8),
+        compiler_params=params(3),
     )(kept, met)
 
     def exchange(v):
@@ -726,7 +732,7 @@
         add_kernel,
         cost_estimate=cost(1.7),
         out_shape=jax.ShapeDtypeStruct((WROWS, LANES), BF16),
-        compiler_params=params(4),
+        compiler_params=params(2),
     )(parts)
     groups = lax.axis_size("img")
     other = [
@@ -737,7 +743,7 @@
         copies_kernel,
         cost_estimate=cost(1.7),
         out_shape=jax.ShapeDtypeStruct((shards // 2, WROWS, LANES), BF16),
-        compiler_params=params(4),
+        compiler_params=params(2),
     )(mine, *other)
     copies, back = lax.optimization_barrier((copies, back))
     own_half = exchange(copies)
@@ -759,7 +765,7 @@
             pltpu.VMEM(cotangent.shape, F32),
             pltpu.VMEM((shards, PIXROWS, LANES), BF16),
         ],
-        compiler_params=params(8),
+        compiler_params=params(5),
     )(info, near, far)
 
     own_half, features_grad, section = lax.optimization_barrier((own_half, features_grad, section))
@@ -809,7 +815,7 @@
         in_specs=[pl.BlockSpec(memory_space=pltpu.SMEM)] + [whole] * 2,
         out_specs=(whole,) * 21,
         scratch_shapes=[pltpu.VMEM((shards, WROWS, LANES), BF16)],
-        compiler_params=params(12),
+        compiler_params=params(6),
     )(info, own_half, other_half)
     return (
         section,

time: 98.8 us -> 89.5 us (0.906)
  Pallas kernels: 27.3 us -> 19.6 us
  local copies, waits for them, and re-layouts: 4.84 us -> 2.9 us
    pallas_call x1, Pallas kernels: 19.2 us -> 10.2 us  [body(): pl.pallas_call(main_kernel, cost_estimate=cost(22), out_shape=(jax.ShapeD...]
    unnamed x51 -> x47, local copies, waits for them, and re-layouts: 3.19 us -> 1.25 us
    pallas_call x1, Pallas kernels: 1.19 us -> 2.56 us  [body(): pl.pallas_call(pack_kernel, cost_estimate=cost(2.5), out_shape=jax.ShapeD...]
where the time goes in v4:
time: 89.5 us; the launch traced here: 89.1 us
  starting transfers between devices  30.4 us (34%)
  waiting for transfers between devices  19.8 us (22%)
  Pallas kernels  19.6 us (22%)
  blocking collectives  14.2 us (16%)
  local copies, waits for them, and re-layouts  2.9 us (3%)
  between operations  2.03 us (2%)
    all_to_all x1, blocking collectives, exchange(): lax.all_to_all(v, 'ch', split_axis=0, concat_axis=0, tiled=True, axis_ind...  14.2 us
    pallas_call x1, Pallas kernels, body(): pl.pallas_call(main_kernel, cost_estimate=cost(22), out_shape=(jax.ShapeD...  10.2 us
    all_to_all x1, starting transfers between devices, body(): lax.all_to_all(chunks, 'ch', split_axis=0, concat_axis=0, tiled=True)  9.61 us
    all_to_all x1, waiting for transfers between devices, body(): lax.all_to_all(chunks, 'ch', split_axis=0, concat_axis=0, tiled=True)  8.8 us
    all_to_all x2, starting transfers between devices, exchange(): lax.all_to_all(v, 'ch', split_axis=0, concat_axis=0, tiled=True, axis_ind...  7.18 us
    all_to_all x2, waiting for transfers between devices, exchange(): lax.all_to_all(v, 'ch', split_axis=0, concat_axis=0, tiled=True, axis_ind...  6.13 us
    ppermute x3, starting transfers between devices, body(): lax.ppermute(mine, 'img', [(i, (i + d) % groups) for i in range(groups)])  4.89 us
    ppermute x1, starting transfers between devices, body(): other_half = lax.ppermute(own_half, 'ch', other_core)  4.53 us
  transfers between devices with their start and end apart: 9, of which 7 were waited for; matrix products, arithmetic and copies ran while one was open for 3% of the time, Pallas kernels for 5%

profile of v4, /device:TPU:1, one launch (start us, length us, event | category | flops | bytes accessed | tf_op | source)
XLA Modules:
  0.0 89.1 jit_solution(9267634165612339364)
XLA Ops:
  0.7 2.6 %shard_map.416 = bf16[32,80,128]{2,1,0:T(8,128)(2,1)} custom-call(bf16[4,41472]{1,0:T(4,128)(2,1)} %feat_hbm.1, bf16[10,10368]{1,0:T(8,128)(2,1)} %cot_hbm.1), custom_call_target="tpu_custom_call" | custom-call | bytes 9225000 | tf_op jit(solution)/shard_map/pallas_call | solution.py:612
  3.2 9.6 %all-to-all-start = ((bf16[32,80,128]{2,1,0:T(8,128)(2,1)}), bf16[32,80,128]{2,1,0:T(8,128)(2,1)S(1)}, u32[]{:S(2)}, u32[]{:S(2)}) async-start(bf16[32,80,128]{2,1,0:T(8,128)(2,1)} %shard_map.416), calls=%async_computation | async-start | bytes 1310720 | tf_op jit(solution)/shard_map/all_to_all | solution.py:627
  12.9 0.0 copy-start.9
  12.9 0.0 copy-start.7
  12.9 0.0 copy-start.13
  12.9 0.0 copy-start.14
  12.9 0.0 copy-start.15
  13.0 0.0 copy-start.16
  13.0 0.0 copy-start.17
  13.0 0.0 copy-start.18
  13.0 0.0 copy-start.19
  13.0 0.0 copy-start.20
  13.0 0.0 copy-start.10
  13.1 0.0 copy-start.11
  13.1 0.0 copy-start.8
  13.1 0.0 copy-start
  13.1 0.0 copy-start.3
  13.1 0.0 copy-start.4
  13.2 1.1 %copy.56 = bf16[320,9,128]{0,2,1:T(8,128)(2,1)S(1)} copy(bf16[320,9,128]{2,0,1:T(8,128)(2,1)S(1)} %copy-done.6) | data formatting | bytes 1474560 | tf_op args[22]
  14.3 0.8 copy.59.kw
  15.1 0.1 reshape.69.kbias
  15.3 0.1 copy.57.sqb
  15.4 0.6 dynamic_slice.11
  16.8 0.1 pad_add_fusion.info
  17.0 8.8 %all-to-all-done.recv = bf16[32,80,128]{2,1,0:T(8,128)(2,1)S(1)} async-done(((bf16[32,80,128]{2,1,0:T(8,128)(2,1)}), bf16[32,80,128]{2,1,0:T(8,128)(2,1)S(1)}, u32[]{:S(2)}, u32[]{:S(2)}) %all-to-all-start) | async-done | bytes 655392 | tf_op jit(solution)/shard_map/all_to_all | solution.py:627
  25.8 10.2 %shard_map.417 = (f32[16,144,128]{2,1,0:T(8,128)S(1)}, bf16[16,144,128]{2,1,0:T(8,128)(2,1)S(1)}, f32[1440,128]{1,0:T(8,128)S(1)}, f32[320,384]{1,0:T(8,128)S(1)}) custom-call(s32[3]{0:T(128)S(1)} %pad_add_fusion.info, bf16[32,80,128]{2,1,0:T(8,128)(2,1)S(1)} %all-to-all-done.recv, f32[17,128]{1,0:T(8,128)S(1)} %bitcast.20, ...), custom_call_target="tpu_custom_call" | custom-call | bytes 81180000 | tf_op jit(solution)/shard_map/pallas_call | solution.py:632
  36.0 0.8 collective-permute-start
  36.8 1.8 %shard_map.418 = bf16[32,80,128]{2,1,0:T(8,128)(2,1)} custom-call(s32[3]{0:T(128)S(1)} %pad_add_fusion.info, f32[1440,128]{1,0:T(8,128)S(1)} %get-tuple-element.60.grad, f32[320,384]{1,0:T(8,128)S(1)} %get-tuple-element.61.section), custom_call_target="tpu_custom_call" | custom-call | bytes 9225000 | tf_op jit(solution)/shard_map/pallas_call | solution.py:701
  38.7 0.1 shard_map.419
  38.8 14.2 %all_to_all.20.recv = bf16[16,144,128]{2,1,0:T(8,128)(2,1)S(1)} all-to-all(bf16[16,144,128]{2,1,0:T(8,128)(2,1)S(1)} %shard_map.419), channel_id=1, replica_groups={{0,8,16,24,32,40,48,56,64,72,80,88,96,104,112,120},{4,12,20,28,36,44,52..., dimensions={0} | all-to-all | bytes 1179648 | tf_op jit(solution)/shard_map/all_to_all | solution.py:723
  53.0 3.6 %all-to-all-start.2 = ((bf16[16,2,80,128]{3,2,1,0:T(8,128)(2,1)}), bf16[16,2,80,128]{3,2,1,0:T(8,128)(2,1)S(1)}, u32[]{:S(2)}, u32[]{:S(2)}) async-start(bf16[16,2,80,128]{3,2,1,0:T(8,128)(2,1)} %bitcast.8), calls=%async_computation.2 | async-start | bytes 1310720 | tf_op jit(solution)/shard_map/all_to_all | solution.py:723
  56.6 0.1 shard_map.420.mine
  56.7 1.3 %collective-permute-start.1 = (bf16[144,128]{1,0:T(8,128)(2,1)S(1)}, bf16[144,128]{1,0:T(8,128)(2,1)S(1)}, u32[]{:S(2)}, u32[]{:S(2)}) collective-permute-start(bf16[144,128]{1,0:T(8,128)(2,1)S(1)} %shard_map.420.mine), channel_id=1, source_target_pairs={{0,1},{1,2},{2,3},{3,0},{4,5},{5,6},{6,7},{7,4},{8,9},{9,10},{10,1... | collective-permute-start | bytes 110600 | tf_op jit(solution)/shard_map/ppermute | solution.py:739
  57.9 2.4 %collective-permute-start.2 = (bf16[144,128]{1,0:T(8,128)(2,1)S(1)}, bf16[144,128]{1,0:T(8,128)(2,1)S(1)}, u32[]{:S(2)}, u32[]{:S(2)}) collective-permute-start(bf16[144,128]{1,0:T(8,128)(2,1)S(1)} %shard_map.420.mine), channel_id=1, source_target_pairs={{0,2},{1,3},{2,0},{3,1},{4,6},{5,7},{6,4},{7,5},{8,10},{9,11},{10,... | collective-permute-start | bytes 110600 | tf_op jit(solution)/shard_map/ppermute | solution.py:739
  60.4 1.2 %collective-permute-start.3 = (bf16[144,128]{1,0:T(8,128)(2,1)S(1)}, bf16[144,128]{1,0:T(8,128)(2,1)S(1)}, u32[]{:S(2)}, u32[]{:S(2)}) collective-permute-start(bf16[144,128]{1,0:T(8,128)(2,1)S(1)} %shard_map.420.mine), channel_id=1, source_target_pairs={{0,3},{1,0},{2,1},{3,2},{4,7},{5,4},{6,5},{7,6},{8,11},{9,8},{10,9... | collective-permute-start | bytes 110600 | tf_op jit(solution)/shard_map/ppermute | solution.py:739
  61.5 0.7 collective-permute-done.2.two
  62.2 1.2 %collective-permute-done.3.three = bf16[144,128]{1,0:T(8,128)(2,1)S(1)} collective-permute-done((bf16[144,128]{1,0:T(8,128)(2,1)S(1)}, bf16[144,128]{1,0:T(8,128)(2,1)S(1)}, u32[]{:S(2)}, u32[]{:S(2)}) %collective-permute-start.3) | collective-permute-done | bytes 36896 | tf_op jit(solution)/shard_map/ppermute | solution.py:739
  63.5 0.9 shard_map.421
  64.4 3.4 %all-to-all-done.2 = bf16[16,2,80,128]{3,2,1,0:T(8,128)(2,1)S(1)} async-done(((bf16[16,2,80,128]{3,2,1,0:T(8,128)(2,1)}), bf16[16,2,80,128]{3,2,1,0:T(8,128)(2,1)S(1)}, u32[]{:S(2)}, u32[]{:S(2)}) %all-to-all-start.2) | async-done | bytes 655392 | tf_op jit(solution)/shard_map/all_to_all | solution.py:723
  67.8 3.6 %all-to-all-start.3 = ((bf16[16,144,128]{2,1,0:T(8,128)(2,1)}), bf16[16,144,128]{2,1,0:T(8,128)(2,1)S(1)}, u32[]{:S(2)}, u32[]{:S(2)}) async-start(bf16[16,144,128]{2,1,0:T(8,128)(2,1)} %shard_map.421), calls=%async_computation.3 | async-start | bytes 1179648 | tf_op jit(solution)/shard_map/all_to_all | solution.py:723
  71.4 0.1 dynamic-slice_bitcast_fusion
  71.4 3.4 %collective-permute-start.4 = (bf16[16,80,128]{2,1,0:T(8,128)(2,1)S(1)}, bf16[16,80,128]{2,1,0:T(8,128)(2,1)S(1)}, u32[]{:S(2)}, u32[]{:S(2)}) collective-permute-start(bf16[16,80,128]{2,1,0:T(8,128)(2,1)S(1)} %get-tuple-element.95), channel_id=1, source_target_pairs={{0,4},{4,0},{8,12},{12,8},{16,20},{20,16},{24,28},{28,24},{32,36},... | collective-permute-start | bytes 983048 | tf_op jit(solution)/shard_map/ppermute | solution.py:753
  74.9 1.3 %collective-permute-done.4.far = bf16[16,80,128]{2,1,0:T(8,128)(2,1)S(1)} collective-permute-done((bf16[16,80,128]{2,1,0:T(8,128)(2,1)S(1)}, bf16[16,80,128]{2,1,0:T(8,128)(2,1)S(1)}, u32[]{:S(2)}, u32[]{:S(2)}) %collective-permute-start.4) | collective-permute-done | bytes 327712 | tf_op jit(solution)/shard_map/ppermute | solution.py:753
  76.1 1.8 %shard_map.422 = (f32[4,41472]{1,0:T(4,128)}, bf16[10,10368]{1,0:T(8,128)(2,1)}) custom-call(s32[3]{0:T(128)S(1)} %pad_add_fusion.info, bf16[16,80,128]{2,1,0:T(8,128)(2,1)S(1)} %get-tuple-element.96.near, bf16[16,80,128]{2,1,0:T(8,128)(2,1)S(1)} %collective-permute-done.4.far), custom_call_target="tpu_custom_call" | custom-call | bytes 9225000 | tf_op jit(solution)/shard_map/pallas_call | solution.py:755
  77.9 2.7 %all-to-all-done.3.own = bf16[16,144,128]{2,1,0:T(8,128)(2,1)S(1)} async-done(((bf16[16,144,128]{2,1,0:T(8,128)(2,1)}), bf16[16,144,128]{2,1,0:T(8,128)(2,1)S(1)}, u32[]{:S(2)}, u32[]{:S(2)}) %all-to-all-start.3) | async-done | bytes 589856 | tf_op jit(solution)/shard_map/all_to_all | solution.py:723
  80.7 4.5 %collective-permute-start.5 = (bf16[16,144,128]{2,1,0:T(8,128)(2,1)S(1)}, bf16[16,144,128]{2,1,0:T(8,128)(2,1)S(1)}, u32[]{:S(2)}, u32[]{:S(2)}) collective-permute-start(bf16[16,144,128]{2,1,0:T(8,128)(2,1)S(1)} %all-to-all-done.3.own), channel_id=1, source_target_pairs={{0,4},{4,0},{8,12},{12,8},{16,20},{20,16},{24,28},{28,24},{32,36},... | collective-permute-start | bytes 1769480 | tf_op jit(solution)/shard_map/ppermute | solution.py:772
  85.2 1.6 %collective-permute-done.5.other = bf16[16,144,128]{2,1,0:T(8,128)(2,1)S(1)} collective-permute-done((bf16[16,144,128]{2,1,0:T(8,128)(2,1)S(1)}, bf16[16,144,128]{2,1,0:T(8,128)(2,1)S(1)}, u32[]{:S(2)}, u32[]{:S(2)}) %collective-permute-start.5) | collective-permute-done | bytes 589856 | tf_op jit(solution)/shard_map/ppermute | solution.py:772
  86.8 2.1 %shard_map.423 = (f32[9,320,128]{2,1,0:T(8,128)}, f32[512,128]{1,0:T(8,128)}, f32[128,512]{1,0:T(8,128)}, f32[128,128]{1,0:T(8,128)}, f32[128,128]{1,0:T(8,128)}...) custom-call(s32[3]{0:T(128)S(1)} %pad_add_fusion.info, ...), custom_call_target="tpu_custom_call" | custom-call | bytes 10332000 | tf_op jit(solution)/shard_map/pallas_call | solution.py:799
  (48 shorter events, 0.2 us)
Async XLA Ops:
  0.7 12.2 %copy-start.6 = (bf16[320,9,128]{2,0,1:T(8,128)(2,1)S(1)}, bf16[320,9,128]{2,0,1:T(8,128)(2,1)}, u32[]{:S(2)}) copy-start(bf16[320,9,128]{2,0,1:T(8,128)(2,1)} %param.47) | copy-start | bytes 2211844
  3.2 22.5 %all-to-all-start = ((bf16[32,80,128]{2,1,0:T(8,128)(2,1)}), bf16[32,80,128]{2,1,0:T(8,128)(2,1)S(1)}, u32[]{:S(2)}, u32[]{:S(2)}) async-start(bf16[32,80,128]{2,1,0:T(8,128)(2,1)} %shard_map.416), calls=%async_computation | async-start | bytes 1310720 | tf_op jit(solution)/shard_map/all_to_all | solution.py:627
  12.9 2.2 %copy-start.9 = (bf16[320]{0:T(512)(128)(2,1)S(1)}, bf16[320]{0:T(512)(128)(2,1)}, u32[]{:S(2)}) copy-start(bf16[320]{0:T(512)(128)(2,1)} %param.48) | copy-start | bytes 1924
  12.9 2.3 %copy-start.7 = (bf16[32,384]{1,0:T(8,128)(2,1)S(1)}, bf16[32,384]{1,0:T(8,128)(2,1)}, u32[]{:S(2)}) copy-start(bf16[32,384]{1,0:T(8,128)(2,1)} %param.37) | copy-start | bytes 73732
  12.9 2.3 %copy-start.13 = (bf16[32]{0:T(256)(128)(2,1)S(1)}, bf16[32]{0:T(256)(128)(2,1)}, u32[]{:S(2)}) copy-start(bf16[32]{0:T(256)(128)(2,1)} %param.36) | copy-start | bytes 196
  12.9 2.4 %copy-start.14 = (s32[32]{0:T(128)S(1)}, s32[32]{0:T(128)}, u32[]{:S(2)}) copy-start(s32[32]{0:T(128)} %param.26) | copy-start | bytes 388
  12.9 3.7 %copy-start.15 = (bf16[128]{0:T(256)(128)(2,1)S(1)}, bf16[128]{0:T(256)(128)(2,1)}, u32[]{:S(2)}) copy-start(bf16[128]{0:T(256)(128)(2,1)} %param.28) | copy-start | bytes 772
  13.0 3.7 %copy-start.16 = (bf16[128]{0:T(256)(128)(2,1)S(1)}, bf16[128]{0:T(256)(128)(2,1)}, u32[]{:S(2)}) copy-start(bf16[128]{0:T(256)(128)(2,1)} %param.29) | copy-start | bytes 772
  13.0 3.7 %copy-start.17 = (bf16[128]{0:T(256)(128)(2,1)S(1)}, bf16[128]{0:T(256)(128)(2,1)}, u32[]{:S(2)}) copy-start(bf16[128]{0:T(256)(128)(2,1)} %param.31) | copy-start | bytes 772
  13.0 3.7 %copy-start.18 = (bf16[128]{0:T(256)(128)(2,1)S(1)}, bf16[128]{0:T(256)(128)(2,1)}, u32[]{:S(2)}) copy-start(bf16[128]{0:T(256)(128)(2,1)} %param.33) | copy-start | bytes 772
  13.0 3.7 %copy-start.19 = (bf16[128]{0:T(256)(128)(2,1)S(1)}, bf16[128]{0:T(256)(128)(2,1)}, u32[]{:S(2)}) copy-start(bf16[128]{0:T(256)(128)(2,1)} %param.40) | copy-start | bytes 772
  13.0 3.7 %copy-start.20 = (bf16[128]{0:T(256)(128)(2,1)S(1)}, bf16[128]{0:T(256)(128)(2,1)}, u32[]{:S(2)}) copy-start(bf16[128]{0:T(256)(128)(2,1)} %param.41) | copy-start | bytes 772
  13.0 3.7 %copy-start.21 = (bf16[128]{0:T(256)(128)(2,1)S(1)}, bf16[128]{0:T(256)(128)(2,1)}, u32[]{:S(2)}) copy-start(bf16[128]{0:T(256)(128)(2,1)} %param.42) | copy-start | bytes 772
  13.0 3.7 %copy-start.22 = (bf16[128]{0:T(256)(128)(2,1)S(1)}, bf16[128]{0:T(256)(128)(2,1)}, u32[]{:S(2)}) copy-start(bf16[128]{0:T(256)(128)(2,1)} %param.46) | copy-start | bytes 772
  13.0 3.8 %copy-start.10 = (bf16[512]{0:T(512)(128)(2,1)S(1)}, bf16[512]{0:T(512)(128)(2,1)}, u32[]{:S(2)}) copy-start(bf16[512]{0:T(512)(128)(2,1)} %param.44) | copy-start | bytes 3076
  13.1 3.8 %copy-start.11 = (bf16[384]{0:T(512)(128)(2,1)S(1)}, bf16[384]{0:T(512)(128)(2,1)}, u32[]{:S(2)}) copy-start(bf16[384]{0:T(512)(128)(2,1)} %param.38) | copy-start | bytes 2308
  13.1 3.9 %copy-start.12 = (s32[2,128]{1,0:T(2,128)S(1)}, s32[2,128]{1,0:T(2,128)}, u32[]{:S(2)}) copy-start(s32[2,128]{1,0:T(2,128)} %param.27) | copy-start | bytes 3076
  13.1 3.9 %copy-start.8 = (bf16[128,32]{0,1:T(8,128)(2,1)S(1)}, bf16[128,32]{0,1:T(8,128)(2,1)}, u32[]{:S(2)}) copy-start(bf16[128,32]{0,1:T(8,128)(2,1)} %param.35) | copy-start | bytes 24580
  13.1 12.7 %copy-start = (bf16[128,512]{1,0:T(8,128)(2,1)S(1)}, bf16[128,512]{1,0:T(8,128)(2,1)}, u32[]{:S(2)}) copy-start(bf16[128,512]{1,0:T(8,128)(2,1)} %xw.1) | copy-start | bytes 393220
  13.1 12.7 %copy-start.1 = (bf16[512,128]{1,0:T(8,128)(2,1)S(1)}, bf16[512,128]{1,0:T(8,128)(2,1)}, u32[]{:S(2)}) copy-start(bf16[512,128]{1,0:T(8,128)(2,1)} %rw.1) | copy-start | bytes 393220
  13.1 12.7 %copy-start.2 = (bf16[128,128]{1,0:T(8,128)(2,1)S(1)}, bf16[128,128]{1,0:T(8,128)(2,1)}, u32[]{:S(2)}) copy-start(bf16[128,128]{1,0:T(8,128)(2,1)} %hw.1) | copy-start | bytes 98308
  13.1 12.7 %copy-start.3 = (bf16[128,128]{1,0:T(8,128)(2,1)S(1)}, bf16[128,128]{1,0:T(8,128)(2,1)}, u32[]{:S(2)}) copy-start(bf16[128,128]{1,0:T(8,128)(2,1)} %ww.1) | copy-start | bytes 98308
  13.1 12.7 %copy-start.4 = (bf16[128,128]{1,0:T(8,128)(2,1)S(1)}, bf16[128,128]{1,0:T(8,128)(2,1)}, u32[]{:S(2)}) copy-start(bf16[128,128]{1,0:T(8,128)(2,1)} %cw.1) | copy-start | bytes 98308
  13.1 12.7 %copy-start.5 = (bf16[128,128]{1,0:T(8,128)(2,1)S(1)}, bf16[128,128]{1,0:T(8,128)(2,1)}, u32[]{:S(2)}) copy-start(bf16[128,128]{1,0:T(8,128)(2,1)} %ow.1) | copy-start | bytes 98308
  36.0 2.6 %collective-permute-start = (bf16[16,144,128]{2,1,0:T(8,128)(2,1)S(1)}, bf16[16,144,128]{2,1,0:T(8,128)(2,1)S(1)}, u32[]{:S(2)}, u32[]{:S(2)}) collective-permute-start(bf16[16,144,128]{2,1,0:T(8,128)(2,1)S(1)} %get-tuple-element.63), channel_id=1, source_target_pairs={{0,4},{4,0},{8,12},{12,8},{16,20},{20,16},{24,28},{28,24},{32,36},... | collective-permute-start | bytes 1769480 | tf_op jit(solution)/shard_map/ppermute | solution.py:700
  53.0 14.8 %all-to-all-start.2 = ((bf16[16,2,80,128]{3,2,1,0:T(8,128)(2,1)}), bf16[16,2,80,128]{3,2,1,0:T(8,128)(2,1)S(1)}, u32[]{:S(2)}, u32[]{:S(2)}) async-start(bf16[16,2,80,128]{3,2,1,0:T(8,128)(2,1)} %bitcast.8), calls=%async_computation.2 | async-start | bytes 1310720 | tf_op jit(solution)/shard_map/all_to_all | solution.py:723
  56.7 4.9 %collective-permute-start.1 = (bf16[144,128]{1,0:T(8,128)(2,1)S(1)}, bf16[144,128]{1,0:T(8,128)(2,1)S(1)}, u32[]{:S(2)}, u32[]{:S(2)}) collective-permute-start(bf16[144,128]{1,0:T(8,128)(2,1)S(1)} %shard_map.420.mine), channel_id=1, source_target_pairs={{0,1},{1,2},{2,3},{3,0},{4,5},{5,6},{6,7},{7,4},{8,9},{9,10},{10,1... | collective-permute-start | bytes 110600 | tf_op jit(solution)/shard_map/ppermute | solution.py:739
  57.9 4.3 %collective-permute-start.2 = (bf16[144,128]{1,0:T(8,128)(2,1)S(1)}, bf16[144,128]{1,0:T(8,128)(2,1)S(1)}, u32[]{:S(2)}, u32[]{:S(2)}) collective-permute-start(bf16[144,128]{1,0:T(8,128)(2,1)S(1)} %shard_map.420.mine), channel_id=1, source_target_pairs={{0,2},{1,3},{2,0},{3,1},{4,6},{5,7},{6,4},{7,5},{8,10},{9,11},{10,... | collective-permute-start | bytes 110600 | tf_op jit(solution)/shard_map/ppermute | solution.py:739
  60.4 3.1 %collective-permute-start.3 = (bf16[144,128]{1,0:T(8,128)(2,1)S(1)}, bf16[144,128]{1,0:T(8,128)(2,1)S(1)}, u32[]{:S(2)}, u32[]{:S(2)}) collective-permute-start(bf16[144,128]{1,0:T(8,128)(2,1)S(1)} %shard_map.420.mine), channel_id=1, source_target_pairs={{0,3},{1,0},{2,1},{3,2},{4,7},{5,4},{6,5},{7,6},{8,11},{9,8},{10,9... | collective-permute-start | bytes 110600 | tf_op jit(solution)/shard_map/ppermute | solution.py:739
  67.8 12.9 %all-to-all-start.3 = ((bf16[16,144,128]{2,1,0:T(8,128)(2,1)}), bf16[16,144,128]{2,1,0:T(8,128)(2,1)S(1)}, u32[]{:S(2)}, u32[]{:S(2)}) async-start(bf16[16,144,128]{2,1,0:T(8,128)(2,1)} %shard_map.421), calls=%async_computation.3 | async-start | bytes 1179648 | tf_op jit(solution)/shard_map/all_to_all | solution.py:723
  71.4 4.7 %collective-permute-start.4 = (bf16[16,80,128]{2,1,0:T(8,128)(2,1)S(1)}, bf16[16,80,128]{2,1,0:T(8,128)(2,1)S(1)}, u32[]{:S(2)}, u32[]{:S(2)}) collective-permute-start(bf16[16,80,128]{2,1,0:T(8,128)(2,1)S(1)} %get-tuple-element.95), channel_id=1, source_target_pairs={{0,4},{4,0},{8,12},{12,8},{16,20},{20,16},{24,28},{28,24},{32,36},... | collective-permute-start | bytes 983048 | tf_op jit(solution)/shard_map/ppermute | solution.py:753
  80.7 6.2 %collective-permute-start.5 = (bf16[16,144,128]{2,1,0:T(8,128)(2,1)S(1)}, bf16[16,144,128]{2,1,0:T(8,128)(2,1)S(1)}, u32[]{:S(2)}, u32[]{:S(2)}) collective-permute-start(bf16[16,144,128]{2,1,0:T(8,128)(2,1)S(1)} %all-to-all-done.3.own), channel_id=1, source_target_pairs={{0,4},{4,0},{8,12},{12,8},{16,20},{20,16},{24,28},{28,24},{32,36},... | collective-permute-start | bytes 1769480 | tf_op jit(solution)/shard_map/ppermute | solution.py:772

commit v5 on v4

--- a/solution.py
+++ b/solution.py
@@ -16,8 +16,6 @@
 WIDE = 40
 FLAT = SIDE * WIDE
 GUARD = 48
-ROWS = 1440
-STEPS = FLAT // ROWS
 EPS = 1e-05
 LANES = 128
 WIN = 11
@@ -146,20 +144,16 @@
     hidden_b,
     slope,
     block,
+    planes,
     taps,
     spread,
-    planes,
     gblock,
     gresid,
     gmixed,
     grows,
     gcols,
-    gnorm,
-    acc_r,
-    acc_x,
-    acc_s,
+    gpre_b,
     sums,
-    gpre_b,
     rows_out,
 ):
     shift = info[0]
@@ -179,7 +173,10 @@
             rows_out[slot, chunk // 2, inner : inner + size, :] = value[done : done + size, :]
             done += size
 
-    cf[...] = jnp.zeros_like(cf)
+    def total_of(row, value):
+        sums[row : row + 1, :] = col_sum(value)
+
+    cf[OUT:, :] = jnp.zeros((cf.shape[0] - OUT, cf.shape[1]), F32)
     for s in range(recv.shape[0]):
         piece = recv[s].astype(F32)
         for t in range(WIN):
@@ -203,60 +200,37 @@
     for ref in (norm, block, grows, gcols):
         ref[0:GUARD, :] = edge
         ref[GUARD + FLAT : FLAT + 2 * GUARD, :] = edge
-    acc_r[...] = jnp.zeros_like(acc_r)
-    acc_x[...] = jnp.zeros_like(acc_x)
-    acc_s[...] = jnp.zeros_like(acc_s)
     sums[...] = jnp.zeros_like(sums)
 
-    def rows_at(i):
-        return pl.ds(pl.multiple_of(i * ROWS, 16), ROWS)
-
-    def guarded(i, extra=0, size=ROWS):
-        return pl.ds(pl.multiple_of(i * ROWS + GUARD + extra, 8), size)
-
-    def first_norm(i, carry):
-        here = rows_at(i)
-        x = canvas[here, :]
-        center = x - lane_mean(x)
-        scale = lax.rsqrt(lane_mean(center * center) + EPS)
-        unit = center * scale
-        xhat[here, :] = unit
-        rstd[here, :] = jnp.broadcast_to(scale, unit.shape)
-        value = jnp.where(valid[here, :] > 0, unit * vec(0) + vec(1), 0.0)
-        norm[guarded(i), :] = value.astype(BF16).astype(F32)
-        return carry
-
-    lax.fori_loop(0, STEPS, first_norm, 0)
-
-    def near(ref, i):
-        wide = ref[guarded(i, -8, ROWS + 16), :]
-        back = pltpu.roll(wide, 1, 0)[8 : 8 + ROWS, :]
-        ahead = pltpu.roll(wide, ROWS + 15, 0)[8 : 8 + ROWS, :]
-        return back, ahead
-
-    def branches(i, total):
-        here = rows_at(i)
-        plain = norm[guarded(i), :]
-        above = norm[guarded(i, -WIDE), :]
-        below = norm[guarded(i, WIDE), :]
-        left, right = near(norm, i)
-        by_row = vec(15)
-        by_col = vec(16)
-        sr = jnp.where(by_row < 0, above, jnp.where(by_row > 0, below, plain)).astype(BF16)
-        sc = jnp.where(by_col < 0, left, jnp.where(by_col > 0, right, plain)).astype(BF16)
-        nb = plain.astype(BF16)
-        rows_b[here, :] = sr
-        cols_b[here, :] = sc
-        norm_b[here, :] = nb
-        bh = nn(sr, hw[...]) + vec(2)
-        bw = nn(sc, ww[...]) + vec(3)
-        bc = nn(nb, cw[...])
-        branch_h[here, :] = bh
-        branch_w[here, :] = bw
-        branch_c[here, :] = bc
-        return total + col_sum(valid[here, :] * (bh + bw + bc))
-
-    total = lax.fori_loop(0, STEPS, branches, jnp.zeros((1, CH), F32))
+    def moved(ref, by):
+        return ref[GUARD + by : GUARD + by + FLAT, :]
+
+    x = canvas[...]
+    center = x - lane_mean(x)
+    scale = lax.rsqrt(lane_mean(center * center) + EPS)
+    unit = center * scale
+    xhat[...] = unit
+    rstd[...] = jnp.broadcast_to(scale, unit.shape)
+    value = jnp.where(valid[...] > 0, unit * vec(0) + vec(1), 0.0)
+    norm[GUARD : GUARD + FLAT, :] = value.astype(BF16).astype(F32)
+
+    by_row = vec(15)
+    by_col = vec(16)
+    plain = moved(norm, 0)
+    rows_b[...] = jnp.where(
+        by_row < 0, moved(norm, -WIDE), jnp.where(by_row > 0, moved(norm, WIDE), plain)
+    ).astype(BF16)
+    cols_b[...] = jnp.where(
+        by_col < 0, moved(norm, -1), jnp.where(by_col > 0, moved(norm, 1), plain)
+    ).astype(BF16)
+    norm_b[...] = plain.astype(BF16)
+    bh = nn(rows_b[...], hw[...]) + vec(2)
+    bw = nn(cols_b[...], ww[...]) + vec(3)
+    bc = nn(norm_b[...], cw[...])
+    branch_h[...] = bh
+    branch_w[...] = bw
+    branch_c[...] = bc
+    total = col_sum(valid[...] * (bh + bw + bc))
 
     count = jnp.full((1, CH), side * side, jnp.int32).astype(F32)
     means = total / count
@@ -270,59 +244,57 @@
     whole = grown[0] + grown[1] + grown[2]
     mix = [v / whole for v in grown]
 
-    def forward(i, carry):
-        here = rows_at(i)
-        mixed = mix[0] * branch_h[here, :] + mix[1] * branch_w[here, :] + mix[2] * branch_c[here, :]
-        mixed = mixed.astype(BF16)
-        mixed_b[here, :] = mixed
-        resid = canvas[here, :] + nn(mixed, ow[...]) + vec(4)
-        center = resid - lane_mean(resid)
-        scale = lax.rsqrt(lane_mean(center * center) + EPS)
-        unit = center * scale
-        xhat2[here, :] = unit
-        rstd2[here, :] = jnp.broadcast_to(scale, unit.shape)
-        n2 = (unit * vec(5) + vec(6)).astype(BF16)
-        norm2_b[here, :] = n2
-        total2 = resid + vec(7)
-        for j in range(FF // CH):
-            lanes = slice(j * CH, (j + 1) * CH)
-            pre = nn(n2, xw[:, lanes]) + vec(8 + j)
-            cdf, density = normal_parts(pre)
-            hid = (pre * cdf).astype(BF16)
-            hidden_b[here, lanes] = hid
-            slope[here, lanes] = cdf + density
-        total2 = total2 + nn(hidden_b[here, :], rw[...])
-        value = jnp.where(valid[here, :] > 0, total2, 0.0)
-        block[guarded(i), :] = value.astype(BF16).astype(F32)
-        return carry
-
-    lax.fori_loop(0, STEPS, forward, 0)
-
-    taps[OPIX:, :] = jnp.zeros((taps.shape[0] - OPIX, taps.shape[1]), F32)
+    mixed = mix[0] * branch_h[...] + mix[1] * branch_w[...] + mix[2] * branch_c[...]
+    mixed_b[...] = mixed.astype(BF16)
+    resid = canvas[...] + nn(mixed_b[...], ow[...]) + vec(4)
+    center = resid - lane_mean(resid)
+    scale = lax.rsqrt(lane_mean(center * center) + EPS)
+    unit = center * scale
+    xhat2[...] = unit
+    rstd2[...] = jnp.broadcast_to(scale, unit.shape)
+    norm2_b[...] = (unit * vec(5) + vec(6)).astype(BF16)
+    through = resid + vec(7)
+    for j in range(FF // CH):
+        lanes = slice(j * CH, (j + 1) * CH)
+        pre = nn(norm2_b[...], xw[:, lanes]) + vec(8 + j)
+        cdf, density = normal_parts(pre)
+        hidden_b[:, lanes] = (pre * cdf).astype(BF16)
+        slope[:, lanes] = cdf + density
+    through = through + nn(hidden_b[...], rw[...])
+    value = jnp.where(valid[...] > 0, through, 0.0)
+    block[GUARD : GUARD + FLAT, :] = value.astype(BF16).astype(F32)
+
+    top_rows = 24
+    for p in range(4):
+        planes[p, 0:top_rows, :] = jnp.zeros((top_rows, CH), F32)
+        planes[p, top_rows + OPIX :, :] = jnp.zeros((planes.shape[1] - top_rows - OPIX, CH), F32)
+        for i in range(HALF):
+            at = GUARD + (2 * i + p // 2) * WIDE + p % 2
+            row = top_rows + i * HALF
+            planes[p, row : row + HALF, :] = block[pl.ds(at, HALF, stride=2), :]
+    used = 336
+    row_id = lax.broadcasted_iota(jnp.int32, (used, CH), 0)
+    row_of = ((row_id.astype(F32) + 0.5) * (1.0 / HALF)).astype(jnp.int32)
+    out_column = row_id - row_of * HALF
     for a in range(3):
         for b in range(3):
-            lanes = slice((3 * a + b) * CH, (3 * a + b + 1) * CH)
-            for i in range(HALF):
-                at = GUARD + (2 * i + a - 1) * WIDE + b - 1
-                taps[i * HALF : (i + 1) * HALF, lanes] = block[pl.ds(at, HALF, stride=2), :]
-    tap_b = taps[...].astype(BF16)
+            plane = 2 * ((a + 1) % 2) + (b + 1) % 2
+            row = top_rows - HALF * (a == 0) - (b == 0)
+            value = planes[plane, row : row + used, :]
+            if b == 0:
+                value = jnp.where(out_column > 0, value, 0.0)
+            taps[0:used, (3 * a + b) * CH : (3 * a + b + 1) * CH] = value.astype(BF16)
+    taps[used:, :] = jnp.zeros((taps.shape[0] - used, taps.shape[1]), BF16)
     index = lax.broadcasted_iota(jnp.int32, (1, OTILE * LANES), 1)
-    out_row = ((index.astype(F32) + 0.5) * (1.0 / HALF)).astype(jnp.int32)
-    out_col = index - out_row * HALF
-    out_keep = (2 * out_row < side) & (2 * out_col < side)
+    lane_row = ((index.astype(F32) + 0.5) * (1.0 / HALF)).astype(jnp.int32)
+    lane_col = index - lane_row * HALF
+    out_keep = (2 * lane_row < side) & (2 * lane_col < side)
     cot = jnp.where(out_keep, cf[...], 0.0)
     cot_b = cot[0:OUT, :].astype(BF16)
     cot_t = cot.T.astype(BF16)[:, 0:OUT]
-    section = nt(kw[...], tap_b) + kbias[...]
-    section_out[...] = jnp.where(out_keep, section, 0.0)
-    conv = nn(cot_b, tap_b)
-    for t in range(9):
-        put(AT_CONV + t * OUT, conv[:, t * CH : (t + 1) * CH])
     kb_rows = jnp.sum(cot, axis=1, keepdims=True)
     spread[...] = nn(cot_t, kw[...])
-    row_id = lax.broadcasted_iota(jnp.int32, (OPIX, CH), 0)
-    row_of = ((row_id.astype(F32) + 0.5) * (1.0 / HALF)).astype(jnp.int32)
-    inside = row_id - row_of * HALF < HALF - 1
+    inside = out_column[0:OPIX, :] < HALF - 1
 
     def part(tap, ahead, masked):
         value = spread[ahead : ahead + OPIX, tap * CH : (tap + 1) * CH]
@@ -340,42 +312,36 @@
             at = (2 * i + p // 2) * WIDE + p % 2
             gblock[pl.ds(at, HALF, stride=2), :] = planes[p, i * HALF : (i + 1) * HALF, :]
 
-    def add(row, value):
-        sums[row : row + 1, :] += value
-
-    def backward(i, carry):
-        here = rows_at(i)
-        gb = jnp.where(valid[here, :] > 0, gblock[here, :], 0.0)
-        gred = gb.astype(BF16)
-        add(7, col_sum(gred.astype(F32)))
-        acc_r[...] += tn(gred, hidden_b[here, :])
-        n2 = norm2_b[here, :]
-        for j in range(FF // CH):
-            lanes = slice(j * CH, (j + 1) * CH)
-            gpre = (nt(gred, rw[lanes, :]) * slope[here, lanes]).astype(BF16)
-            add(8 + j, col_sum(gpre.astype(F32)))
-            gpre_b[:, lanes] = gpre
-        acc_x[...] += tn(n2, gpre_b[...])
-        gn2 = nt(gpre_b[...], xw[...])
-        unit = xhat2[here, :]
-        add(5, col_sum(gn2 * unit))
-        add(6, col_sum(gn2))
-        gy = gn2 * vec(5)
-        gr = gb + rstd2[here, :] * (gy - lane_mean(gy) - unit * lane_mean(gy * unit))
-        gresid[here, :] = gr
-        gproj = gr.astype(BF16)
-        add(4, col_sum(gproj.astype(F32)))
-        acc_s[3] += tn(mixed_b[here, :], gproj)
-        gm = nt(gproj, ow[...])
-        gmixed[here, :] = gm
-        add(20, col_sum(gm * branch_h[here, :]))
-        add(21, col_sum(gm * branch_w[here, :]))
-        add(22, col_sum(gm * branch_c[here, :]))
-        return carry
-
-    lax.fori_loop(0, STEPS, backward, 0)
-
-    gmix = [sums[20 + j : 21 + j, :] for j in range(3)]
+    gb = jnp.where(valid[...] > 0, gblock[...], 0.0)
+    gred = gb.astype(BF16)
+    total_of(7, gred.astype(F32))
+    for j in range(FF // (2 * CH)):
+        lanes = slice(2 * j * CH, 2 * (j + 1) * CH)
+        gpre = (nt(gred, rw[lanes, :]) * slope[:, lanes]).astype(BF16)
+        total_of(8 + 2 * j, gpre[:, 0:CH].astype(F32))
+        total_of(9 + 2 * j, gpre[:, CH:].astype(F32))
+        gpre_b[:, lanes] = gpre
+    gn2 = nt(gpre_b[...], xw[...])
+    conv = nn(cot_b, taps[...])
+    for t in range(9):
+        put(AT_CONV + t * OUT, conv[:, t * CH : (t + 1) * CH])
+    unit = xhat2[...]
+    total_of(5, gn2 * unit)
+    total_of(6, gn2)
+    gy = gn2 * vec(5)
+    gr = gb + rstd2[...] * (gy - lane_mean(gy) - unit * lane_mean(gy * unit))
+    gresid[...] = gr
+    gproj = gr.astype(BF16)
+    total_of(4, gproj.astype(F32))
+    grown = tn(gred, hidden_b[...])
+    for j in range(FF // CH):
+        put(AT_REDUCE + j * CH, grown[:, j * CH : (j + 1) * CH].T)
+    gm = nt(gproj, ow[...])
+    gmixed[...] = gm
+    section = nt(kw[...], taps[...]) + kbias[...]
+    section_out[...] = jnp.where(out_keep, section, 0.0)
+    gmix = [col_sum(gm * branch[...]) for branch in (branch_h, branch_w, branch_c)]
+    put(AT_OUTPUT, tn(mixed_b[...], gproj))
     inner_dot = mix[0] * gmix[0] + mix[1] * gmix[1] + mix[2] * gmix[2]
     glogit = [mix[j] * (gmix[j] - inner_dot) for j in range(3)]
     ginner = jnp.zeros((RED, 1), F32)
@@ -388,61 +354,44 @@
     put(AT_SQ_BIAS, jnp.broadcast_to(ginner, (RED, CH)))
     gmeans = col_sum(sqt[...] * ginner) / count
 
-    def branch_back(i, carry):
-        here = rows_at(i)
-        gm = gmixed[here, :]
-        level = valid[here, :] * gmeans
-        gh = (mix[0] * gm + level).astype(BF16)
-        gw = (mix[1] * gm + level).astype(BF16)
-        gc = (mix[2] * gm + level).astype(BF16)
-        add(2, col_sum(gh.astype(F32)))
-        add(3, col_sum(gw.astype(F32)))
-        acc_s[0] += tn(rows_b[here, :], gh)
-        acc_s[1] += tn(cols_b[here, :], gw)
-        acc_s[2] += tn(norm_b[here, :], gc)
-        grows[guarded(i), :] = nt(gh, hw[...])
-        gcols[guarded(i), :] = nt(gw, ww[...])
-        gnorm[here, :] = nt(gc, cw[...])
-        return carry
-
-    lax.fori_loop(0, STEPS, branch_back, 0)
-
-    def last(i, carry):
-        here = rows_at(i)
-        by_row = vec(15)
-        by_col = vec(16)
-        plain = grows[guarded(i), :]
-        above = grows[guarded(i, -WIDE), :]
-        below = grows[guarded(i, WIDE), :]
-        left, right = near(gcols, i)
-        level = gcols[guarded(i), :]
-        value = (
-            gnorm[here, :]
-            + jnp.where(by_row < 0, below, jnp.where(by_row > 0, above, plain))
-            + jnp.where(by_col < 0, right, jnp.where(by_col > 0, left, level))
-        )
-        keep = valid[here, :] > 0
-        value = jnp.where(keep, value, 0.0)
-        unit = xhat[here, :]
-        add(0, col_sum(value * unit))
-        add(1, col_sum(value))
-        gy = value * vec(0)
-        back = rstd[here, :] * (gy - lane_mean(gy) - unit * lane_mean(gy * unit))
-        grad[here, :] = jnp.where(keep, gresid[here, :] + back, 0.0)
-        return carry
-
-    lax.fori_loop(0, STEPS, last, 0)
-
+    gm = gmixed[...]
+    level = valid[...] * gmeans
+    gh = (mix[0] * gm + level).astype(BF16)
+    gw = (mix[1] * gm + level).astype(BF16)
+    gc = (mix[2] * gm + level).astype(BF16)
+    total_of(2, gh.astype(F32))
+    total_of(3, gw.astype(F32))
+    grown = tn(norm2_b[...], gpre_b[...])
     for j in range(FF // CH):
-        put(AT_REDUCE + j * CH, acc_r[:, j * CH : (j + 1) * CH].T)
-        put(AT_EXPAND + j * CH, acc_x[:, j * CH : (j + 1) * CH])
-    for j, at in enumerate((AT_HEIGHT, AT_WIDTH, AT_CHANNEL, AT_OUTPUT)):
-        put(at, acc_s[j])
+        put(AT_EXPAND + j * CH, grown[:, j * CH : (j + 1) * CH])
+    grows[GUARD : GUARD + FLAT, :] = nt(gh, hw[...])
+    gcols[GUARD : GUARD + FLAT, :] = nt(gw, ww[...])
+    value = nt(gc, cw[...])
+    put(AT_HEIGHT, tn(rows_b[...], gh))
+    put(AT_WIDTH, tn(cols_b[...], gw))
+    put(AT_CHANNEL, tn(norm_b[...], gc))
+    value = value + jnp.where(
+        by_row < 0,
+        moved(grows, WIDE),
+        jnp.where(by_row > 0, moved(grows, -WIDE), moved(grows, 0)),
+    )
+    value = value + jnp.where(
+        by_col < 0, moved(gcols, 1), jnp.where(by_col > 0, moved(gcols, -1), moved(gcols, 0))
+    )
+    keep = valid[...] > 0
+    value = jnp.where(keep, value, 0.0)
+    unit = xhat[...]
+    total_of(0, value * unit)
+    total_of(1, value)
+    gy = value * vec(0)
+    back = rstd[...] * (gy - lane_mean(gy) - unit * lane_mean(gy * unit))
+    grad[...] = jnp.where(keep, gresid[...] + back, 0.0)
+
     same = lax.broadcasted_iota(jnp.int32, (LANES, LANES), 0) == lax.broadcasted_iota(
         jnp.int32, (LANES, LANES), 1
     )
     for j in range(OTILE):
-        add(15 + j, col_sum(jnp.where(same, kb_rows[j * LANES : (j + 1) * LANES, :], 0.0)))
+        total_of(15 + j, jnp.where(same, kb_rows[j * LANES : (j + 1) * LANES, :], 0.0))
     put(AT_VECTOR, sums[...])
     keep_out[...] = rows_out[0]
     send_out[...] = rows_out[1].astype(BF16)
@@ -662,20 +611,16 @@
             pltpu.VMEM((FLAT, FF), BF16),
             pltpu.VMEM((FLAT, FF), F32),
             guarded,
+            pltpu.VMEM((4, 360, CH), F32),
+            pltpu.VMEM((OTILE * LANES, 9 * CH), BF16),
             pltpu.VMEM((OTILE * LANES, 9 * CH), F32),
-            pltpu.VMEM((OTILE * LANES, 9 * CH), F32),
-            pltpu.VMEM((4, 328, CH), F32),
             canvas,
             canvas,
             canvas,
             guarded,
             guarded,
-            canvas,
-            pltpu.VMEM((CH, FF), F32),
-            pltpu.VMEM((CH, FF), F32),
-            pltpu.VMEM((4, CH, CH), F32),
+            pltpu.VMEM((FLAT, FF), BF16),
             pltpu.VMEM((RED, CH), F32),
-            pltpu.VMEM((ROWS, FF), BF16),
             pltpu.VMEM((2, shards // 2, WROWS, LANES), F32),
         ],
         compiler_params=params(42),
@@ -716,6 +661,8 @@
         pair_kernel,
         cost_estimate=cost(2.3),
         out_shape=jax.ShapeDtypeStruct(kept.shape, BF16),
+        in_specs=[whole] * 2,
+        out_specs=whole,
         compiler_params=params(3),
     )(kept, met)
 
@@ -742,6 +689,8 @@
     copies = pl.pallas_call(
         copies_kernel,
         cost_estimate=cost(1.7),
+        in_specs=[whole] * 4,
+        out_specs=whole,
         out_shape=jax.ShapeDtypeStruct((shards // 2, WROWS, LANES), BF16),
         compiler_params=params(2),
     )(mine, *other)

time: 89.5 us -> 88.4 us (0.988)
  Pallas kernels: 19.6 us -> 18.4 us
    pallas_call x1, Pallas kernels: 10.2 us -> 9.08 us  [body(): pl.pallas_call(main_kernel, cost_estimate=cost(22), out_shape=(jax.ShapeD...]
where the time goes in v5:
time: 88.4 us; the launch traced here: 87.9 us
  starting transfers between devices  30.8 us (35%)
  waiting for transfers between devices  19.4 us (22%)
  Pallas kernels  18.4 us (21%)
  blocking collectives  14.2 us (16%)
  local copies, waits for them, and re-layouts  2.9 us (3%)
  between operations  2.03 us (2%)
    all_to_all x1, blocking collectives, exchange(): lax.all_to_all(v, 'ch', split_axis=0, concat_axis=0, tiled=True, axis_ind...  14.2 us
    all_to_all x1, starting transfers between devices, body(): lax.all_to_all(chunks, 'ch', split_axis=0, concat_axis=0, tiled=True)  9.61 us
    pallas_call x1, Pallas kernels, body(): pl.pallas_call(main_kernel, cost_estimate=cost(22), out_shape=(jax.ShapeD...  9.08 us
    all_to_all x1, waiting for transfers between devices, body(): lax.all_to_all(chunks, 'ch', split_axis=0, concat_axis=0, tiled=True)  8.8 us
    all_to_all x2, starting transfers between devices, exchange(): lax.all_to_all(v, 'ch', split_axis=0, concat_axis=0, tiled=True, axis_ind...  7.18 us
    all_to_all x2, waiting for transfers between devices, exchange(): lax.all_to_all(v, 'ch', split_axis=0, concat_axis=0, tiled=True, axis_ind...  5.77 us
    ppermute x3, starting transfers between devices, body(): lax.ppermute(mine, 'img', [(i, (i + d) % groups) for i in range(groups)])  5.07 us
    ppermute x1, starting transfers between devices, body(): other_half = lax.ppermute(own_half, 'ch', other_core)  4.71 us
  transfers between devices with their start and end apart: 9, of which 7 were waited for; matrix products, arithmetic and copies ran while one was open for 3% of the time, Pallas kernels for 5%

profile of v5, /device:TPU:1, one launch (start us, length us, event | category | flops | bytes accessed | tf_op | source)
XLA Modules:
  0.0 87.9 jit_solution(4648479724594382523)
XLA Ops:
  0.7 2.6 %shard_map.416 = bf16[32,80,128]{2,1,0:T(8,128)(2,1)} custom-call(bf16[4,41472]{1,0:T(4,128)(2,1)} %feat_hbm.1, bf16[10,10368]{1,0:T(8,128)(2,1)} %cot_hbm.1), custom_call_target="tpu_custom_call" | custom-call | bytes 9225000 | tf_op jit(solution)/shard_map/pallas_call | solution.py:561
  3.2 9.6 %all-to-all-start = ((bf16[32,80,128]{2,1,0:T(8,128)(2,1)}), bf16[32,80,128]{2,1,0:T(8,128)(2,1)S(1)}, u32[]{:S(2)}, u32[]{:S(2)}) async-start(bf16[32,80,128]{2,1,0:T(8,128)(2,1)} %shard_map.416), calls=%async_computation | async-start | bytes 1310720 | tf_op jit(solution)/shard_map/all_to_all | solution.py:576
  12.9 0.0 copy-start.9
  12.9 0.0 copy-start.7
  12.9 0.0 copy-start.13
  12.9 0.0 copy-start.14
  12.9 0.0 copy-start.15
  13.0 0.0 copy-start.16
  13.0 0.0 copy-start.17
  13.0 0.0 copy-start.18
  13.0 0.0 copy-start.19
  13.0 0.0 copy-start.20
  13.0 0.0 copy-start.21
  13.0 0.0 copy-start.22
  13.1 0.0 copy-start.12
  13.1 0.0 copy-start.8
  13.1 0.0 copy-start.2
  13.1 0.0 copy-start.3
  13.2 1.1 %copy.56 = bf16[320,9,128]{0,2,1:T(8,128)(2,1)S(1)} copy(bf16[320,9,128]{2,0,1:T(8,128)(2,1)S(1)} %copy-done.6) | data formatting | bytes 1474560 | tf_op args[22]
  14.3 0.8 copy.59.kw
  15.1 0.1 reshape.69.kbias
  15.3 0.1 copy.57.sqb
  15.4 0.6 dynamic_slice.11
  16.8 0.1 pad_add_fusion.info
  17.0 8.8 %all-to-all-done.recv = bf16[32,80,128]{2,1,0:T(8,128)(2,1)S(1)} async-done(((bf16[32,80,128]{2,1,0:T(8,128)(2,1)}), bf16[32,80,128]{2,1,0:T(8,128)(2,1)S(1)}, u32[]{:S(2)}, u32[]{:S(2)}) %all-to-all-start) | async-done | bytes 655392 | tf_op jit(solution)/shard_map/all_to_all | solution.py:576
  25.8 9.1 %shard_map.417 = (f32[16,144,128]{2,1,0:T(8,128)S(1)}, bf16[16,144,128]{2,1,0:T(8,128)(2,1)S(1)}, f32[1440,128]{1,0:T(8,128)S(1)}, f32[320,384]{1,0:T(8,128)S(1)}) custom-call(s32[3]{0:T(128)S(1)} %pad_add_fusion.info, bf16[32,80,128]{2,1,0:T(8,128)(2,1)S(1)} %all-to-all-done.recv, f32[17,128]{1,0:T(8,128)S(1)} %bitcast.20, ...), custom_call_target="tpu_custom_call" | custom-call | bytes 81180000 | tf_op jit(solution)/shard_map/pallas_call | solution.py:581
  34.9 0.6 collective-permute-start
  35.5 1.8 %shard_map.418 = bf16[32,80,128]{2,1,0:T(8,128)(2,1)} custom-call(s32[3]{0:T(128)S(1)} %pad_add_fusion.info, f32[1440,128]{1,0:T(8,128)S(1)} %get-tuple-element.60.grad, f32[320,384]{1,0:T(8,128)S(1)} %get-tuple-element.61.section), custom_call_target="tpu_custom_call" | custom-call | bytes 9225000 | tf_op jit(solution)/shard_map/pallas_call | solution.py:646
  37.3 0.1 shard_map.419
  37.5 14.2 %all_to_all.20.recv = bf16[16,144,128]{2,1,0:T(8,128)(2,1)S(1)} all-to-all(bf16[16,144,128]{2,1,0:T(8,128)(2,1)S(1)} %shard_map.419), channel_id=1, replica_groups={{0,8,16,24,32,40,48,56,64,72,80,88,96,104,112,120},{4,12,20,28,36,44,52..., dimensions={0} | all-to-all | bytes 1179648 | tf_op jit(solution)/shard_map/all_to_all | solution.py:670
  51.6 3.6 %all-to-all-start.2 = ((bf16[16,2,80,128]{3,2,1,0:T(8,128)(2,1)}), bf16[16,2,80,128]{3,2,1,0:T(8,128)(2,1)S(1)}, u32[]{:S(2)}, u32[]{:S(2)}) async-start(bf16[16,2,80,128]{3,2,1,0:T(8,128)(2,1)} %bitcast.8), calls=%async_computation.2 | async-start | bytes 1310720 | tf_op jit(solution)/shard_map/all_to_all | solution.py:670
  55.2 0.1 shard_map.420.mine
  55.3 1.5 %collective-permute-start.1 = (bf16[144,128]{1,0:T(8,128)(2,1)S(1)}, bf16[144,128]{1,0:T(8,128)(2,1)S(1)}, u32[]{:S(2)}, u32[]{:S(2)}) collective-permute-start(bf16[144,128]{1,0:T(8,128)(2,1)S(1)} %shard_map.420.mine), channel_id=1, source_target_pairs={{0,1},{1,2},{2,3},{3,0},{4,5},{5,6},{6,7},{7,4},{8,9},{9,10},{10,1... | collective-permute-start | bytes 110600 | tf_op jit(solution)/shard_map/ppermute | solution.py:686
  56.8 2.4 %collective-permute-start.2 = (bf16[144,128]{1,0:T(8,128)(2,1)S(1)}, bf16[144,128]{1,0:T(8,128)(2,1)S(1)}, u32[]{:S(2)}, u32[]{:S(2)}) collective-permute-start(bf16[144,128]{1,0:T(8,128)(2,1)S(1)} %shard_map.420.mine), channel_id=1, source_target_pairs={{0,2},{1,3},{2,0},{3,1},{4,6},{5,7},{6,4},{7,5},{8,10},{9,11},{10,... | collective-permute-start | bytes 110600 | tf_op jit(solution)/shard_map/ppermute | solution.py:686
  59.2 1.2 %collective-permute-start.3 = (bf16[144,128]{1,0:T(8,128)(2,1)S(1)}, bf16[144,128]{1,0:T(8,128)(2,1)S(1)}, u32[]{:S(2)}, u32[]{:S(2)}) collective-permute-start(bf16[144,128]{1,0:T(8,128)(2,1)S(1)} %shard_map.420.mine), channel_id=1, source_target_pairs={{0,3},{1,0},{2,1},{3,2},{4,7},{5,4},{6,5},{7,6},{8,11},{9,8},{10,9... | collective-permute-start | bytes 110600 | tf_op jit(solution)/shard_map/ppermute | solution.py:686
  60.4 0.7 collective-permute-done.2.two
  61.1 1.2 %collective-permute-done.3.three = bf16[144,128]{1,0:T(8,128)(2,1)S(1)} collective-permute-done((bf16[144,128]{1,0:T(8,128)(2,1)S(1)}, bf16[144,128]{1,0:T(8,128)(2,1)S(1)}, u32[]{:S(2)}, u32[]{:S(2)}) %collective-permute-start.3) | collective-permute-done | bytes 36896 | tf_op jit(solution)/shard_map/ppermute | solution.py:686
  62.3 0.9 shard_map.421
  63.2 3.2 %all-to-all-done.2 = bf16[16,2,80,128]{3,2,1,0:T(8,128)(2,1)S(1)} async-done(((bf16[16,2,80,128]{3,2,1,0:T(8,128)(2,1)}), bf16[16,2,80,128]{3,2,1,0:T(8,128)(2,1)S(1)}, u32[]{:S(2)}, u32[]{:S(2)}) %all-to-all-start.2) | async-done | bytes 655392 | tf_op jit(solution)/shard_map/all_to_all | solution.py:670
  66.4 3.6 %all-to-all-start.3 = ((bf16[16,144,128]{2,1,0:T(8,128)(2,1)}), bf16[16,144,128]{2,1,0:T(8,128)(2,1)S(1)}, u32[]{:S(2)}, u32[]{:S(2)}) async-start(bf16[16,144,128]{2,1,0:T(8,128)(2,1)} %shard_map.421), calls=%async_computation.3 | async-start | bytes 1179648 | tf_op jit(solution)/shard_map/all_to_all | solution.py:670
  70.1 0.1 dynamic-slice_bitcast_fusion
  70.1 3.6 %collective-permute-start.4 = (bf16[16,80,128]{2,1,0:T(8,128)(2,1)S(1)}, bf16[16,80,128]{2,1,0:T(8,128)(2,1)S(1)}, u32[]{:S(2)}, u32[]{:S(2)}) collective-permute-start(bf16[16,80,128]{2,1,0:T(8,128)(2,1)S(1)} %get-tuple-element.95), channel_id=1, source_target_pairs={{0,4},{4,0},{8,12},{12,8},{16,20},{20,16},{24,28},{28,24},{32,36},... | collective-permute-start | bytes 983048 | tf_op jit(solution)/shard_map/ppermute | solution.py:702
  73.7 1.3 %collective-permute-done.4.far = bf16[16,80,128]{2,1,0:T(8,128)(2,1)S(1)} collective-permute-done((bf16[16,80,128]{2,1,0:T(8,128)(2,1)S(1)}, bf16[16,80,128]{2,1,0:T(8,128)(2,1)S(1)}, u32[]{:S(2)}, u32[]{:S(2)}) %collective-permute-start.4) | collective-permute-done | bytes 327712 | tf_op jit(solution)/shard_map/ppermute | solution.py:702
  75.0 1.8 %shard_map.422 = (f32[4,41472]{1,0:T(4,128)}, bf16[10,10368]{1,0:T(8,128)(2,1)}) custom-call(s32[3]{0:T(128)S(1)} %pad_add_fusion.info, bf16[16,80,128]{2,1,0:T(8,128)(2,1)S(1)} %get-tuple-element.96.near, bf16[16,80,128]{2,1,0:T(8,128)(2,1)S(1)} %collective-permute-done.4.far), custom_call_target="tpu_custom_call" | custom-call | bytes 9225000 | tf_op jit(solution)/shard_map/pallas_call | solution.py:704
  76.8 2.5 %all-to-all-done.3.own = bf16[16,144,128]{2,1,0:T(8,128)(2,1)S(1)} async-done(((bf16[16,144,128]{2,1,0:T(8,128)(2,1)}), bf16[16,144,128]{2,1,0:T(8,128)(2,1)S(1)}, u32[]{:S(2)}, u32[]{:S(2)}) %all-to-all-start.3) | async-done | bytes 589856 | tf_op jit(solution)/shard_map/all_to_all | solution.py:670
  79.3 4.7 %collective-permute-start.5 = (bf16[16,144,128]{2,1,0:T(8,128)(2,1)S(1)}, bf16[16,144,128]{2,1,0:T(8,128)(2,1)S(1)}, u32[]{:S(2)}, u32[]{:S(2)}) collective-permute-start(bf16[16,144,128]{2,1,0:T(8,128)(2,1)S(1)} %all-to-all-done.3.own), channel_id=1, source_target_pairs={{0,4},{4,0},{8,12},{12,8},{16,20},{20,16},{24,28},{28,24},{32,36},... | collective-permute-start | bytes 1769480 | tf_op jit(solution)/shard_map/ppermute | solution.py:721
  84.1 1.6 %collective-permute-done.5.other = bf16[16,144,128]{2,1,0:T(8,128)(2,1)S(1)} collective-permute-done((bf16[16,144,128]{2,1,0:T(8,128)(2,1)S(1)}, bf16[16,144,128]{2,1,0:T(8,128)(2,1)S(1)}, u32[]{:S(2)}, u32[]{:S(2)}) %collective-permute-start.5) | collective-permute-done | bytes 589856 | tf_op jit(solution)/shard_map/ppermute | solution.py:721
  85.7 2.1 %shard_map.423 = (f32[9,320,128]{2,1,0:T(8,128)}, f32[512,128]{1,0:T(8,128)}, f32[128,512]{1,0:T(8,128)}, f32[128,128]{1,0:T(8,128)}, f32[128,128]{1,0:T(8,128)}...) custom-call(s32[3]{0:T(128)S(1)} %pad_add_fusion.info, ...), custom_call_target="tpu_custom_call" | custom-call | bytes 10332000 | tf_op jit(solution)/shard_map/pallas_call | solution.py:748
  (48 shorter events, 0.2 us)
Async XLA Ops:
  0.7 12.2 %copy-start.6 = (bf16[320,9,128]{2,0,1:T(8,128)(2,1)S(1)}, bf16[320,9,128]{2,0,1:T(8,128)(2,1)}, u32[]{:S(2)}) copy-start(bf16[320,9,128]{2,0,1:T(8,128)(2,1)} %param.47) | copy-start | bytes 2211844
  3.2 22.5 %all-to-all-start = ((bf16[32,80,128]{2,1,0:T(8,128)(2,1)}), bf16[32,80,128]{2,1,0:T(8,128)(2,1)S(1)}, u32[]{:S(2)}, u32[]{:S(2)}) async-start(bf16[32,80,128]{2,1,0:T(8,128)(2,1)} %shard_map.416), calls=%async_computation | async-start | bytes 1310720 | tf_op jit(solution)/shard_map/all_to_all | solution.py:576
  12.9 2.2 %copy-start.9 = (bf16[320]{0:T(512)(128)(2,1)S(1)}, bf16[320]{0:T(512)(128)(2,1)}, u32[]{:S(2)}) copy-start(bf16[320]{0:T(512)(128)(2,1)} %param.48) | copy-start | bytes 1924
  12.9 2.3 %copy-start.7 = (bf16[32,384]{1,0:T(8,128)(2,1)S(1)}, bf16[32,384]{1,0:T(8,128)(2,1)}, u32[]{:S(2)}) copy-start(bf16[32,384]{1,0:T(8,128)(2,1)} %param.37) | copy-start | bytes 73732
  12.9 2.3 %copy-start.13 = (bf16[32]{0:T(256)(128)(2,1)S(1)}, bf16[32]{0:T(256)(128)(2,1)}, u32[]{:S(2)}) copy-start(bf16[32]{0:T(256)(128)(2,1)} %param.36) | copy-start | bytes 196
  12.9 2.4 %copy-start.14 = (s32[32]{0:T(128)S(1)}, s32[32]{0:T(128)}, u32[]{:S(2)}) copy-start(s32[32]{0:T(128)} %param.26) | copy-start | bytes 388
  12.9 3.7 %copy-start.15 = (bf16[128]{0:T(256)(128)(2,1)S(1)}, bf16[128]{0:T(256)(128)(2,1)}, u32[]{:S(2)}) copy-start(bf16[128]{0:T(256)(128)(2,1)} %param.28) | copy-start | bytes 772
  13.0 3.7 %copy-start.16 = (bf16[128]{0:T(256)(128)(2,1)S(1)}, bf16[128]{0:T(256)(128)(2,1)}, u32[]{:S(2)}) copy-start(bf16[128]{0:T(256)(128)(2,1)} %param.29) | copy-start | bytes 772
  13.0 3.7 %copy-start.17 = (bf16[128]{0:T(256)(128)(2,1)S(1)}, bf16[128]{0:T(256)(128)(2,1)}, u32[]{:S(2)}) copy-start(bf16[128]{0:T(256)(128)(2,1)} %param.31) | copy-start | bytes 772
  13.0 3.7 %copy-start.18 = (bf16[128]{0:T(256)(128)(2,1)S(1)}, bf16[128]{0:T(256)(128)(2,1)}, u32[]{:S(2)}) copy-start(bf16[128]{0:T(256)(128)(2,1)} %param.33) | copy-start | bytes 772
  13.0 3.7 %copy-start.19 = (bf16[128]{0:T(256)(128)(2,1)S(1)}, bf16[128]{0:T(256)(128)(2,1)}, u32[]{:S(2)}) copy-start(bf16[128]{0:T(256)(128)(2,1)} %param.40) | copy-start | bytes 772
  13.0 3.7 %copy-start.20 = (bf16[128]{0:T(256)(128)(2,1)S(1)}, bf16[128]{0:T(256)(128)(2,1)}, u32[]{:S(2)}) copy-start(bf16[128]{0:T(256)(128)(2,1)} %param.41) | copy-start | bytes 772
  13.0 3.7 %copy-start.21 = (bf16[128]{0:T(256)(128)(2,1)S(1)}, bf16[128]{0:T(256)(128)(2,1)}, u32[]{:S(2)}) copy-start(bf16[128]{0:T(256)(128)(2,1)} %param.42) | copy-start | bytes 772
  13.0 3.7 %copy-start.22 = (bf16[128]{0:T(256)(128)(2,1)S(1)}, bf16[128]{0:T(256)(128)(2,1)}, u32[]{:S(2)}) copy-start(bf16[128]{0:T(256)(128)(2,1)} %param.46) | copy-start | bytes 772
  13.0 3.8 %copy-start.10 = (bf16[512]{0:T(512)(128)(2,1)S(1)}, bf16[512]{0:T(512)(128)(2,1)}, u32[]{:S(2)}) copy-start(bf16[512]{0:T(512)(128)(2,1)} %param.44) | copy-start | bytes 3076
  13.1 3.8 %copy-start.11 = (bf16[384]{0:T(512)(128)(2,1)S(1)}, bf16[384]{0:T(512)(128)(2,1)}, u32[]{:S(2)}) copy-start(bf16[384]{0:T(512)(128)(2,1)} %param.38) | copy-start | bytes 2308
  13.1 3.9 %copy-start.12 = (s32[2,128]{1,0:T(2,128)S(1)}, s32[2,128]{1,0:T(2,128)}, u32[]{:S(2)}) copy-start(s32[2,128]{1,0:T(2,128)} %param.27) | copy-start | bytes 3076
  13.1 3.9 %copy-start.8 = (bf16[128,32]{0,1:T(8,128)(2,1)S(1)}, bf16[128,32]{0,1:T(8,128)(2,1)}, u32[]{:S(2)}) copy-start(bf16[128,32]{0,1:T(8,128)(2,1)} %param.35) | copy-start | bytes 24580
  13.1 12.7 %copy-start = (bf16[128,512]{1,0:T(8,128)(2,1)S(1)}, bf16[128,512]{1,0:T(8,128)(2,1)}, u32[]{:S(2)}) copy-start(bf16[128,512]{1,0:T(8,128)(2,1)} %xw.1) | copy-start | bytes 393220
  13.1 12.7 %copy-start.1 = (bf16[512,128]{1,0:T(8,128)(2,1)S(1)}, bf16[512,128]{1,0:T(8,128)(2,1)}, u32[]{:S(2)}) copy-start(bf16[512,128]{1,0:T(8,128)(2,1)} %rw.1) | copy-start | bytes 393220
  13.1 12.7 %copy-start.2 = (bf16[128,128]{1,0:T(8,128)(2,1)S(1)}, bf16[128,128]{1,0:T(8,128)(2,1)}, u32[]{:S(2)}) copy-start(bf16[128,128]{1,0:T(8,128)(2,1)} %hw.1) | copy-start | bytes 98308
  13.1 12.7 %copy-start.3 = (bf16[128,128]{1,0:T(8,128)(2,1)S(1)}, bf16[128,128]{1,0:T(8,128)(2,1)}, u32[]{:S(2)}) copy-start(bf16[128,128]{1,0:T(8,128)(2,1)} %ww.1) | copy-start | bytes 98308
  13.1 12.7 %copy-start.4 = (bf16[128,128]{1,0:T(8,128)(2,1)S(1)}, bf16[128,128]{1,0:T(8,128)(2,1)}, u32[]{:S(2)}) copy-start(bf16[128,128]{1,0:T(8,128)(2,1)} %cw.1) | copy-start | bytes 98308
  13.1 12.7 %copy-start.5 = (bf16[128,128]{1,0:T(8,128)(2,1)S(1)}, bf16[128,128]{1,0:T(8,128)(2,1)}, u32[]{:S(2)}) copy-start(bf16[128,128]{1,0:T(8,128)(2,1)} %ow.1) | copy-start | bytes 98308
  34.9 2.5 %collective-permute-start = (bf16[16,144,128]{2,1,0:T(8,128)(2,1)S(1)}, bf16[16,144,128]{2,1,0:T(8,128)(2,1)S(1)}, u32[]{:S(2)}, u32[]{:S(2)}) collective-permute-start(bf16[16,144,128]{2,1,0:T(8,128)(2,1)S(1)} %get-tuple-element.63), channel_id=1, source_target_pairs={{0,4},{4,0},{8,12},{12,8},{16,20},{20,16},{24,28},{28,24},{32,36},... | collective-permute-start | bytes 1769480 | tf_op jit(solution)/shard_map/ppermute | solution.py:645
  51.6 14.8 %all-to-all-start.2 = ((bf16[16,2,80,128]{3,2,1,0:T(8,128)(2,1)}), bf16[16,2,80,128]{3,2,1,0:T(8,128)(2,1)S(1)}, u32[]{:S(2)}, u32[]{:S(2)}) async-start(bf16[16,2,80,128]{3,2,1,0:T(8,128)(2,1)} %bitcast.8), calls=%async_computation.2 | async-start | bytes 1310720 | tf_op jit(solution)/shard_map/all_to_all | solution.py:670
  55.3 5.1 %collective-permute-start.1 = (bf16[144,128]{1,0:T(8,128)(2,1)S(1)}, bf16[144,128]{1,0:T(8,128)(2,1)S(1)}, u32[]{:S(2)}, u32[]{:S(2)}) collective-permute-start(bf16[144,128]{1,0:T(8,128)(2,1)S(1)} %shard_map.420.mine), channel_id=1, source_target_pairs={{0,1},{1,2},{2,3},{3,0},{4,5},{5,6},{6,7},{7,4},{8,9},{9,10},{10,1... | collective-permute-start | bytes 110600 | tf_op jit(solution)/shard_map/ppermute | solution.py:686
  56.8 4.3 %collective-permute-start.2 = (bf16[144,128]{1,0:T(8,128)(2,1)S(1)}, bf16[144,128]{1,0:T(8,128)(2,1)S(1)}, u32[]{:S(2)}, u32[]{:S(2)}) collective-permute-start(bf16[144,128]{1,0:T(8,128)(2,1)S(1)} %shard_map.420.mine), channel_id=1, source_target_pairs={{0,2},{1,3},{2,0},{3,1},{4,6},{5,7},{6,4},{7,5},{8,10},{9,11},{10,... | collective-permute-start | bytes 110600 | tf_op jit(solution)/shard_map/ppermute | solution.py:686
  59.2 3.1 %collective-permute-start.3 = (bf16[144,128]{1,0:T(8,128)(2,1)S(1)}, bf16[144,128]{1,0:T(8,128)(2,1)S(1)}, u32[]{:S(2)}, u32[]{:S(2)}) collective-permute-start(bf16[144,128]{1,0:T(8,128)(2,1)S(1)} %shard_map.420.mine), channel_id=1, source_target_pairs={{0,3},{1,0},{2,1},{3,2},{4,7},{5,4},{6,5},{7,6},{8,11},{9,8},{10,9... | collective-permute-start | bytes 110600 | tf_op jit(solution)/shard_map/ppermute | solution.py:686
  66.4 12.9 %all-to-all-start.3 = ((bf16[16,144,128]{2,1,0:T(8,128)(2,1)}), bf16[16,144,128]{2,1,0:T(8,128)(2,1)S(1)}, u32[]{:S(2)}, u32[]{:S(2)}) async-start(bf16[16,144,128]{2,1,0:T(8,128)(2,1)} %shard_map.421), calls=%async_computation.3 | async-start | bytes 1179648 | tf_op jit(solution)/shard_map/all_to_all | solution.py:670
  70.1 4.9 %collective-permute-start.4 = (bf16[16,80,128]{2,1,0:T(8,128)(2,1)S(1)}, bf16[16,80,128]{2,1,0:T(8,128)(2,1)S(1)}, u32[]{:S(2)}, u32[]{:S(2)}) collective-permute-start(bf16[16,80,128]{2,1,0:T(8,128)(2,1)S(1)} %get-tuple-element.95), channel_id=1, source_target_pairs={{0,4},{4,0},{8,12},{12,8},{16,20},{20,16},{24,28},{28,24},{32,36},... | collective-permute-start | bytes 983048 | tf_op jit(solution)/shard_map/ppermute | solution.py:702
  79.3 6.3 %collective-permute-start.5 = (bf16[16,144,128]{2,1,0:T(8,128)(2,1)S(1)}, bf16[16,144,128]{2,1,0:T(8,128)(2,1)S(1)}, u32[]{:S(2)}, u32[]{:S(2)}) collective-permute-start(bf16[16,144,128]{2,1,0:T(8,128)(2,1)S(1)} %all-to-all-done.3.own), channel_id=1, source_target_pairs={{0,4},{4,0},{8,12},{12,8},{16,20},{20,16},{24,28},{28,24},{32,36},... | collective-permute-start | bytes 1769480 | tf_op jit(solution)/shard_map/ppermute | solution.py:721

commit v6 on v5

--- a/solution.py
+++ b/solution.py
@@ -232,6 +232,15 @@
     branch_c[...] = bc
     total = col_sum(valid[...] * (bh + bw + bc))
 
+    index = lax.broadcasted_iota(jnp.int32, (1, OTILE * LANES), 1)
+    lane_row = ((index.astype(F32) + 0.5) * (1.0 / HALF)).astype(jnp.int32)
+    lane_col = index - lane_row * HALF
+    out_keep = (2 * lane_row < side) & (2 * lane_col < side)
+    cot = jnp.where(out_keep, cf[...], 0.0)
+    cot_b = cot[0:OUT, :].astype(BF16)
+    cot_t = cot.T.astype(BF16)[:, 0:OUT]
+    kb_rows = jnp.sum(cot, axis=1, keepdims=True)
+    spread[...] = nn(cot_t, kw[...])
     count = jnp.full((1, CH), side * side, jnp.int32).astype(F32)
     means = total / count
     inner_pre = jnp.sum(sqt[...] * means, axis=1, keepdims=True) + sqb[...]
@@ -253,47 +262,10 @@
     xhat2[...] = unit
     rstd2[...] = jnp.broadcast_to(scale, unit.shape)
     norm2_b[...] = (unit * vec(5) + vec(6)).astype(BF16)
-    through = resid + vec(7)
-    for j in range(FF // CH):
-        lanes = slice(j * CH, (j + 1) * CH)
-        pre = nn(norm2_b[...], xw[:, lanes]) + vec(8 + j)
-        cdf, density = normal_parts(pre)
-        hidden_b[:, lanes] = (pre * cdf).astype(BF16)
-        slope[:, lanes] = cdf + density
-    through = through + nn(hidden_b[...], rw[...])
-    value = jnp.where(valid[...] > 0, through, 0.0)
-    block[GUARD : GUARD + FLAT, :] = value.astype(BF16).astype(F32)
-
-    top_rows = 24
-    for p in range(4):
-        planes[p, 0:top_rows, :] = jnp.zeros((top_rows, CH), F32)
-        planes[p, top_rows + OPIX :, :] = jnp.zeros((planes.shape[1] - top_rows - OPIX, CH), F32)
-        for i in range(HALF):
-            at = GUARD + (2 * i + p // 2) * WIDE + p % 2
-            row = top_rows + i * HALF
-            planes[p, row : row + HALF, :] = block[pl.ds(at, HALF, stride=2), :]
     used = 336
     row_id = lax.broadcasted_iota(jnp.int32, (used, CH), 0)
     row_of = ((row_id.astype(F32) + 0.5) * (1.0 / HALF)).astype(jnp.int32)
     out_column = row_id - row_of * HALF
-    for a in range(3):
-        for b in range(3):
-            plane = 2 * ((a + 1) % 2) + (b + 1) % 2
-            row = top_rows - HALF * (a == 0) - (b == 0)
-            value = planes[plane, row : row + used, :]
-            if b == 0:
-                value = jnp.where(out_column > 0, value, 0.0)
-            taps[0:used, (3 * a + b) * CH : (3 * a + b + 1) * CH] = value.astype(BF16)
-    taps[used:, :] = jnp.zeros((taps.shape[0] - used, taps.shape[1]), BF16)
-    index = lax.broadcasted_iota(jnp.int32, (1, OTILE * LANES), 1)
-    lane_row = ((index.astype(F32) + 0.5) * (1.0 / HALF)).astype(jnp.int32)
-    lane_col = index - lane_row * HALF
-    out_keep = (2 * lane_row < side) & (2 * lane_col < side)
-    cot = jnp.where(out_keep, cf[...], 0.0)
-    cot_b = cot[0:OUT, :].astype(BF16)
-    cot_t = cot.T.astype(BF16)[:, 0:OUT]
-    kb_rows = jnp.sum(cot, axis=1, keepdims=True)
-    spread[...] = nn(cot_t, kw[...])
     inside = out_column[0:OPIX, :] < HALF - 1
 
     def part(tap, ahead, masked):
@@ -312,6 +284,34 @@
             at = (2 * i + p // 2) * WIDE + p % 2
             gblock[pl.ds(at, HALF, stride=2), :] = planes[p, i * HALF : (i + 1) * HALF, :]
 
+    through = resid + vec(7)
+    for j in range(FF // CH):
+        lanes = slice(j * CH, (j + 1) * CH)
+        pre = nn(norm2_b[...], xw[:, lanes]) + vec(8 + j)
+        cdf, density = normal_parts(pre)
+        hidden_b[:, lanes] = (pre * cdf).astype(BF16)
+        slope[:, lanes] = cdf + density
+    through = through + nn(hidden_b[...], rw[...])
+    value = jnp.where(valid[...] > 0, through, 0.0)
+    block[GUARD : GUARD + FLAT, :] = value.astype(BF16).astype(F32)
+
+    top_rows = 24
+    for p in range(4):
+        planes[p, 0:top_rows, :] = jnp.zeros((top_rows, CH), F32)
+        planes[p, top_rows + OPIX :, :] = jnp.zeros((planes.shape[1] - top_rows - OPIX, CH), F32)
+        for i in range(HALF):
+            at = GUARD + (2 * i + p // 2) * WIDE + p % 2
+            row = top_rows + i * HALF
+            planes[p, row : row + HALF, :] = block[pl.ds(at, HALF, stride=2), :]
+    for a in range(3):
+        for b in range(3):
+            plane = 2 * ((a + 1) % 2) + (b + 1) % 2
+            row = top_rows - HALF * (a == 0) - (b == 0)
+            value = planes[plane, row : row + used, :]
+            if b == 0:
+                value = jnp.where(out_column > 0, value, 0.0)
+            taps[0:used, (3 * a + b) * CH : (3 * a + b + 1) * CH] = value.astype(BF16)
+    taps[used:, :] = jnp.zeros((taps.shape[0] - used, taps.shape[1]), BF16)
     gb = jnp.where(valid[...] > 0, gblock[...], 0.0)
     gred = gb.astype(BF16)
     total_of(7, gred.astype(F32))

time: 88.4 us -> 87.7 us (level)
  no operation moved by 1% of the time
where the time goes in v6:
time: 87.7 us; the launch traced here: 87.3 us
  starting transfers between devices  30.3 us (35%)
  waiting for transfers between devices  19.8 us (23%)
  Pallas kernels  18.1 us (21%)
  blocking collectives  14.2 us (16%)
  local copies, waits for them, and re-layouts  2.9 us (3%)
  between operations  1.87 us (2%)
    all_to_all x1, blocking collectives, exchange(): lax.all_to_all(v, 'ch', split_axis=0, concat_axis=0, tiled=True, axis_ind...  14.2 us
    all_to_all x1, starting transfers between devices, body(): lax.all_to_all(chunks, 'ch', split_axis=0, concat_axis=0, tiled=True)  9.61 us
    all_to_all x1, waiting for transfers between devices, body(): lax.all_to_all(chunks, 'ch', split_axis=0, concat_axis=0, tiled=True)  8.8 us
    pallas_call x1, Pallas kernels, body(): pl.pallas_call(main_kernel, cost_estimate=cost(22), out_shape=(jax.ShapeD...  8.75 us
    all_to_all x2, starting transfers between devices, exchange(): lax.all_to_all(v, 'ch', split_axis=0, concat_axis=0, tiled=True, axis_ind...  7.18 us
    all_to_all x2, waiting for transfers between devices, exchange(): lax.all_to_all(v, 'ch', split_axis=0, concat_axis=0, tiled=True, axis_ind...  6.11 us
    ppermute x3, starting transfers between devices, body(): lax.ppermute(mine, 'img', [(i, (i + d) % groups) for i in range(groups)])  4.88 us
    ppermute x1, starting transfers between devices, body(): other_half = lax.ppermute(own_half, 'ch', other_core)  4.54 us
  transfers between devices with their start and end apart: 9, of which 7 were waited for; matrix products, arithmetic and copies ran while one was open for 3% of the time, Pallas kernels for 5%

profile of v6, /device:TPU:1, one launch (start us, length us, event | category | flops | bytes accessed | tf_op | source)
XLA Modules:
  0.0 87.3 jit_solution(8421778774784553552)
XLA Ops:
  0.7 2.6 %shard_map.416 = bf16[32,80,128]{2,1,0:T(8,128)(2,1)} custom-call(bf16[4,41472]{1,0:T(4,128)(2,1)} %feat_hbm.1, bf16[10,10368]{1,0:T(8,128)(2,1)} %cot_hbm.1), custom_call_target="tpu_custom_call" | custom-call | bytes 9225000 | tf_op jit(solution)/shard_map/pallas_call | solution.py:561
  3.2 9.6 %all-to-all-start = ((bf16[32,80,128]{2,1,0:T(8,128)(2,1)}), bf16[32,80,128]{2,1,0:T(8,128)(2,1)S(1)}, u32[]{:S(2)}, u32[]{:S(2)}) async-start(bf16[32,80,128]{2,1,0:T(8,128)(2,1)} %shard_map.416), calls=%async_computation | async-start | bytes 1310720 | tf_op jit(solution)/shard_map/all_to_all | solution.py:576
  12.9 0.0 copy-start.9
  12.9 0.0 copy-start.7
  12.9 0.0 copy-start.13
  12.9 0.0 copy-start.14
  12.9 0.0 copy-start.15
  13.0 0.0 copy-start.16
  13.0 0.0 copy-start.17
  13.0 0.0 copy-start.18
  13.0 0.0 copy-start.19
  13.0 0.0 copy-start.20
  13.0 0.0 copy-start.22
  13.0 0.0 copy-start.10
  13.1 0.0 copy-start.8
  13.1 0.0 copy-start
  13.1 0.0 copy-start.2
  13.1 0.0 copy-start.3
  13.2 1.1 %copy.56 = bf16[320,9,128]{0,2,1:T(8,128)(2,1)S(1)} copy(bf16[320,9,128]{2,0,1:T(8,128)(2,1)S(1)} %copy-done.6) | data formatting | bytes 1474560 | tf_op args[22]
  14.3 0.8 copy.59.kw
  15.1 0.1 reshape.69.kbias
  15.3 0.1 copy.57.sqb
  15.4 0.6 dynamic_slice.11
  16.8 0.1 pad_add_fusion.info
  17.0 8.8 %all-to-all-done.recv = bf16[32,80,128]{2,1,0:T(8,128)(2,1)S(1)} async-done(((bf16[32,80,128]{2,1,0:T(8,128)(2,1)}), bf16[32,80,128]{2,1,0:T(8,128)(2,1)S(1)}, u32[]{:S(2)}, u32[]{:S(2)}) %all-to-all-start) | async-done | bytes 655392 | tf_op jit(solution)/shard_map/all_to_all | solution.py:576
  25.8 8.8 %shard_map.417 = (f32[16,144,128]{2,1,0:T(8,128)S(1)}, bf16[16,144,128]{2,1,0:T(8,128)(2,1)S(1)}, f32[1440,128]{1,0:T(8,128)S(1)}, f32[320,384]{1,0:T(8,128)S(1)}) custom-call(s32[3]{0:T(128)S(1)} %pad_add_fusion.info, bf16[32,80,128]{2,1,0:T(8,128)(2,1)S(1)} %all-to-all-done.recv, f32[17,128]{1,0:T(8,128)S(1)} %bitcast.20, ...), custom_call_target="tpu_custom_call" | custom-call | bytes 81180000 | tf_op jit(solution)/shard_map/pallas_call | solution.py:581
  34.6 0.6 collective-permute-start
  35.2 1.8 %shard_map.418 = bf16[32,80,128]{2,1,0:T(8,128)(2,1)} custom-call(s32[3]{0:T(128)S(1)} %pad_add_fusion.info, f32[1440,128]{1,0:T(8,128)S(1)} %get-tuple-element.60.grad, f32[320,384]{1,0:T(8,128)S(1)} %get-tuple-element.61.section), custom_call_target="tpu_custom_call" | custom-call | bytes 9225000 | tf_op jit(solution)/shard_map/pallas_call | solution.py:646
  37.0 0.1 shard_map.419
  37.1 14.2 %all_to_all.20.recv = bf16[16,144,128]{2,1,0:T(8,128)(2,1)S(1)} all-to-all(bf16[16,144,128]{2,1,0:T(8,128)(2,1)S(1)} %shard_map.419), channel_id=1, replica_groups={{0,8,16,24,32,40,48,56,64,72,80,88,96,104,112,120},{4,12,20,28,36,44,52..., dimensions={0} | all-to-all | bytes 1179648 | tf_op jit(solution)/shard_map/all_to_all | solution.py:670
  51.3 3.6 %all-to-all-start.2 = ((bf16[16,2,80,128]{3,2,1,0:T(8,128)(2,1)}), bf16[16,2,80,128]{3,2,1,0:T(8,128)(2,1)S(1)}, u32[]{:S(2)}, u32[]{:S(2)}) async-start(bf16[16,2,80,128]{3,2,1,0:T(8,128)(2,1)} %bitcast.8), calls=%async_computation.2 | async-start | bytes 1310720 | tf_op jit(solution)/shard_map/all_to_all | solution.py:670
  54.9 0.1 shard_map.420.mine
  55.0 1.3 %collective-permute-start.1 = (bf16[144,128]{1,0:T(8,128)(2,1)S(1)}, bf16[144,128]{1,0:T(8,128)(2,1)S(1)}, u32[]{:S(2)}, u32[]{:S(2)}) collective-permute-start(bf16[144,128]{1,0:T(8,128)(2,1)S(1)} %shard_map.420.mine), channel_id=1, source_target_pairs={{0,1},{1,2},{2,3},{3,0},{4,5},{5,6},{6,7},{7,4},{8,9},{9,10},{10,1... | collective-permute-start | bytes 110600 | tf_op jit(solution)/shard_map/ppermute | solution.py:686
  56.3 2.5 %collective-permute-start.2 = (bf16[144,128]{1,0:T(8,128)(2,1)S(1)}, bf16[144,128]{1,0:T(8,128)(2,1)S(1)}, u32[]{:S(2)}, u32[]{:S(2)}) collective-permute-start(bf16[144,128]{1,0:T(8,128)(2,1)S(1)} %shard_map.420.mine), channel_id=1, source_target_pairs={{0,2},{1,3},{2,0},{3,1},{4,6},{5,7},{6,4},{7,5},{8,10},{9,11},{10,... | collective-permute-start | bytes 110600 | tf_op jit(solution)/shard_map/ppermute | solution.py:686
  58.8 1.1 %collective-permute-start.3 = (bf16[144,128]{1,0:T(8,128)(2,1)S(1)}, bf16[144,128]{1,0:T(8,128)(2,1)S(1)}, u32[]{:S(2)}, u32[]{:S(2)}) collective-permute-start(bf16[144,128]{1,0:T(8,128)(2,1)S(1)} %shard_map.420.mine), channel_id=1, source_target_pairs={{0,3},{1,0},{2,1},{3,2},{4,7},{5,4},{6,5},{7,6},{8,11},{9,8},{10,9... | collective-permute-start | bytes 110600 | tf_op jit(solution)/shard_map/ppermute | solution.py:686
  59.9 0.7 collective-permute-done.2.two
  60.6 1.2 %collective-permute-done.3.three = bf16[144,128]{1,0:T(8,128)(2,1)S(1)} collective-permute-done((bf16[144,128]{1,0:T(8,128)(2,1)S(1)}, bf16[144,128]{1,0:T(8,128)(2,1)S(1)}, u32[]{:S(2)}, u32[]{:S(2)}) %collective-permute-start.3) | collective-permute-done | bytes 36896 | tf_op jit(solution)/shard_map/ppermute | solution.py:686
  61.9 0.9 shard_map.421
  62.7 3.4 %all-to-all-done.2 = bf16[16,2,80,128]{3,2,1,0:T(8,128)(2,1)S(1)} async-done(((bf16[16,2,80,128]{3,2,1,0:T(8,128)(2,1)}), bf16[16,2,80,128]{3,2,1,0:T(8,128)(2,1)S(1)}, u32[]{:S(2)}, u32[]{:S(2)}) %all-to-all-start.2) | async-done | bytes 655392 | tf_op jit(solution)/shard_map/all_to_all | solution.py:670
  66.1 3.6 %all-to-all-start.3 = ((bf16[16,144,128]{2,1,0:T(8,128)(2,1)}), bf16[16,144,128]{2,1,0:T(8,128)(2,1)S(1)}, u32[]{:S(2)}, u32[]{:S(2)}) async-start(bf16[16,144,128]{2,1,0:T(8,128)(2,1)} %shard_map.421), calls=%async_computation.3 | async-start | bytes 1179648 | tf_op jit(solution)/shard_map/all_to_all | solution.py:670
  69.7 0.1 dynamic-slice_bitcast_fusion
  69.8 3.4 %collective-permute-start.4 = (bf16[16,80,128]{2,1,0:T(8,128)(2,1)S(1)}, bf16[16,80,128]{2,1,0:T(8,128)(2,1)S(1)}, u32[]{:S(2)}, u32[]{:S(2)}) collective-permute-start(bf16[16,80,128]{2,1,0:T(8,128)(2,1)S(1)} %get-tuple-element.95), channel_id=1, source_target_pairs={{0,4},{4,0},{8,12},{12,8},{16,20},{20,16},{24,28},{28,24},{32,36},... | collective-permute-start | bytes 983048 | tf_op jit(solution)/shard_map/ppermute | solution.py:702
  73.2 1.3 %collective-permute-done.4.far = bf16[16,80,128]{2,1,0:T(8,128)(2,1)S(1)} collective-permute-done((bf16[16,80,128]{2,1,0:T(8,128)(2,1)S(1)}, bf16[16,80,128]{2,1,0:T(8,128)(2,1)S(1)}, u32[]{:S(2)}, u32[]{:S(2)}) %collective-permute-start.4) | collective-permute-done | bytes 327712 | tf_op jit(solution)/shard_map/ppermute | solution.py:702
  74.5 1.8 %shard_map.422 = (f32[4,41472]{1,0:T(4,128)}, bf16[10,10368]{1,0:T(8,128)(2,1)}) custom-call(s32[3]{0:T(128)S(1)} %pad_add_fusion.info, bf16[16,80,128]{2,1,0:T(8,128)(2,1)S(1)} %get-tuple-element.96.near, bf16[16,80,128]{2,1,0:T(8,128)(2,1)S(1)} %collective-permute-done.4.far), custom_call_target="tpu_custom_call" | custom-call | bytes 9225000 | tf_op jit(solution)/shard_map/pallas_call | solution.py:704
  76.3 2.7 %all-to-all-done.3.own = bf16[16,144,128]{2,1,0:T(8,128)(2,1)S(1)} async-done(((bf16[16,144,128]{2,1,0:T(8,128)(2,1)}), bf16[16,144,128]{2,1,0:T(8,128)(2,1)S(1)}, u32[]{:S(2)}, u32[]{:S(2)}) %all-to-all-start.3) | async-done | bytes 589856 | tf_op jit(solution)/shard_map/all_to_all | solution.py:670
  79.0 4.5 %collective-permute-start.5 = (bf16[16,144,128]{2,1,0:T(8,128)(2,1)S(1)}, bf16[16,144,128]{2,1,0:T(8,128)(2,1)S(1)}, u32[]{:S(2)}, u32[]{:S(2)}) collective-permute-start(bf16[16,144,128]{2,1,0:T(8,128)(2,1)S(1)} %all-to-all-done.3.own), channel_id=1, source_target_pairs={{0,4},{4,0},{8,12},{12,8},{16,20},{20,16},{24,28},{28,24},{32,36},... | collective-permute-start | bytes 1769480 | tf_op jit(solution)/shard_map/ppermute | solution.py:721
  83.6 1.6 %collective-permute-done.5.other = bf16[16,144,128]{2,1,0:T(8,128)(2,1)S(1)} collective-permute-done((bf16[16,144,128]{2,1,0:T(8,128)(2,1)S(1)}, bf16[16,144,128]{2,1,0:T(8,128)(2,1)S(1)}, u32[]{:S(2)}, u32[]{:S(2)}) %collective-permute-start.5) | collective-permute-done | bytes 589856 | tf_op jit(solution)/shard_map/ppermute | solution.py:721
  85.2 2.1 %shard_map.423 = (f32[9,320,128]{2,1,0:T(8,128)}, f32[512,128]{1,0:T(8,128)}, f32[128,512]{1,0:T(8,128)}, f32[128,128]{1,0:T(8,128)}, f32[128,128]{1,0:T(8,128)}...) custom-call(s32[3]{0:T(128)S(1)} %pad_add_fusion.info, ...), custom_call_target="tpu_custom_call" | custom-call | bytes 10332000 | tf_op jit(solution)/shard_map/pallas_call | solution.py:748
  (48 shorter events, 0.2 us)
Async XLA Ops:
  0.7 12.2 %copy-start.6 = (bf16[320,9,128]{2,0,1:T(8,128)(2,1)S(1)}, bf16[320,9,128]{2,0,1:T(8,128)(2,1)}, u32[]{:S(2)}) copy-start(bf16[320,9,128]{2,0,1:T(8,128)(2,1)} %param.47) | copy-start | bytes 2211844
  3.2 22.5 %all-to-all-start = ((bf16[32,80,128]{2,1,0:T(8,128)(2,1)}), bf16[32,80,128]{2,1,0:T(8,128)(2,1)S(1)}, u32[]{:S(2)}, u32[]{:S(2)}) async-start(bf16[32,80,128]{2,1,0:T(8,128)(2,1)} %shard_map.416), calls=%async_computation | async-start | bytes 1310720 | tf_op jit(solution)/shard_map/all_to_all | solution.py:576
  12.9 2.2 %copy-start.9 = (bf16[320]{0:T(512)(128)(2,1)S(1)}, bf16[320]{0:T(512)(128)(2,1)}, u32[]{:S(2)}) copy-start(bf16[320]{0:T(512)(128)(2,1)} %param.48) | copy-start | bytes 1924
  12.9 2.3 %copy-start.7 = (bf16[32,384]{1,0:T(8,128)(2,1)S(1)}, bf16[32,384]{1,0:T(8,128)(2,1)}, u32[]{:S(2)}) copy-start(bf16[32,384]{1,0:T(8,128)(2,1)} %param.37) | copy-start | bytes 73732
  12.9 2.3 %copy-start.13 = (bf16[32]{0:T(256)(128)(2,1)S(1)}, bf16[32]{0:T(256)(128)(2,1)}, u32[]{:S(2)}) copy-start(bf16[32]{0:T(256)(128)(2,1)} %param.36) | copy-start | bytes 196
  12.9 2.4 %copy-start.14 = (s32[32]{0:T(128)S(1)}, s32[32]{0:T(128)}, u32[]{:S(2)}) copy-start(s32[32]{0:T(128)} %param.26) | copy-start | bytes 388
  12.9 3.7 %copy-start.15 = (bf16[128]{0:T(256)(128)(2,1)S(1)}, bf16[128]{0:T(256)(128)(2,1)}, u32[]{:S(2)}) copy-start(bf16[128]{0:T(256)(128)(2,1)} %param.28) | copy-start | bytes 772
  13.0 3.7 %copy-start.16 = (bf16[128]{0:T(256)(128)(2,1)S(1)}, bf16[128]{0:T(256)(128)(2,1)}, u32[]{:S(2)}) copy-start(bf16[128]{0:T(256)(128)(2,1)} %param.29) | copy-start | bytes 772
  13.0 3.7 %copy-start.17 = (bf16[128]{0:T(256)(128)(2,1)S(1)}, bf16[128]{0:T(256)(128)(2,1)}, u32[]{:S(2)}) copy-start(bf16[128]{0:T(256)(128)(2,1)} %param.31) | copy-start | bytes 772
  13.0 3.7 %copy-start.18 = (bf16[128]{0:T(256)(128)(2,1)S(1)}, bf16[128]{0:T(256)(128)(2,1)}, u32[]{:S(2)}) copy-start(bf16[128]{0:T(256)(128)(2,1)} %param.33) | copy-start | bytes 772
  13.0 3.7 %copy-start.19 = (bf16[128]{0:T(256)(128)(2,1)S(1)}, bf16[128]{0:T(256)(128)(2,1)}, u32[]{:S(2)}) copy-start(bf16[128]{0:T(256)(128)(2,1)} %param.40) | copy-start | bytes 772
  13.0 3.7 %copy-start.20 = (bf16[128]{0:T(256)(128)(2,1)S(1)}, bf16[128]{0:T(256)(128)(2,1)}, u32[]{:S(2)}) copy-start(bf16[128]{0:T(256)(128)(2,1)} %param.41) | copy-start | bytes 772
  13.0 3.7 %copy-start.21 = (bf16[128]{0:T(256)(128)(2,1)S(1)}, bf16[128]{0:T(256)(128)(2,1)}, u32[]{:S(2)}) copy-start(bf16[128]{0:T(256)(128)(2,1)} %param.42) | copy-start | bytes 772
  13.0 3.7 %copy-start.22 = (bf16[128]{0:T(256)(128)(2,1)S(1)}, bf16[128]{0:T(256)(128)(2,1)}, u32[]{:S(2)}) copy-start(bf16[128]{0:T(256)(128)(2,1)} %param.46) | copy-start | bytes 772
  13.0 3.8 %copy-start.10 = (bf16[512]{0:T(512)(128)(2,1)S(1)}, bf16[512]{0:T(512)(128)(2,1)}, u32[]{:S(2)}) copy-start(bf16[512]{0:T(512)(128)(2,1)} %param.44) | copy-start | bytes 3076
  13.1 3.8 %copy-start.11 = (bf16[384]{0:T(512)(128)(2,1)S(1)}, bf16[384]{0:T(512)(128)(2,1)}, u32[]{:S(2)}) copy-start(bf16[384]{0:T(512)(128)(2,1)} %param.38) | copy-start | bytes 2308
  13.1 3.9 %copy-start.12 = (s32[2,128]{1,0:T(2,128)S(1)}, s32[2,128]{1,0:T(2,128)}, u32[]{:S(2)}) copy-start(s32[2,128]{1,0:T(2,128)} %param.27) | copy-start | bytes 3076
  13.1 3.9 %copy-start.8 = (bf16[128,32]{0,1:T(8,128)(2,1)S(1)}, bf16[128,32]{0,1:T(8,128)(2,1)}, u32[]{:S(2)}) copy-start(bf16[128,32]{0,1:T(8,128)(2,1)} %param.35) | copy-start | bytes 24580
  13.1 12.7 %copy-start = (bf16[128,512]{1,0:T(8,128)(2,1)S(1)}, bf16[128,512]{1,0:T(8,128)(2,1)}, u32[]{:S(2)}) copy-start(bf16[128,512]{1,0:T(8,128)(2,1)} %xw.1) | copy-start | bytes 393220
  13.1 12.7 %copy-start.1 = (bf16[512,128]{1,0:T(8,128)(2,1)S(1)}, bf16[512,128]{1,0:T(8,128)(2,1)}, u32[]{:S(2)}) copy-start(bf16[512,128]{1,0:T(8,128)(2,1)} %rw.1) | copy-start | bytes 393220
  13.1 12.7 %copy-start.2 = (bf16[128,128]{1,0:T(8,128)(2,1)S(1)}, bf16[128,128]{1,0:T(8,128)(2,1)}, u32[]{:S(2)}) copy-start(bf16[128,128]{1,0:T(8,128)(2,1)} %hw.1) | copy-start | bytes 98308
  13.1 12.7 %copy-start.3 = (bf16[128,128]{1,0:T(8,128)(2,1)S(1)}, bf16[128,128]{1,0:T(8,128)(2,1)}, u32[]{:S(2)}) copy-start(bf16[128,128]{1,0:T(8,128)(2,1)} %ww.1) | copy-start | bytes 98308
  13.1 12.7 %copy-start.4 = (bf16[128,128]{1,0:T(8,128)(2,1)S(1)}, bf16[128,128]{1,0:T(8,128)(2,1)}, u32[]{:S(2)}) copy-start(bf16[128,128]{1,0:T(8,128)(2,1)} %cw.1) | copy-start | bytes 98308
  13.1 12.7 %copy-start.5 = (bf16[128,128]{1,0:T(8,128)(2,1)S(1)}, bf16[128,128]{1,0:T(8,128)(2,1)}, u32[]{:S(2)}) copy-start(bf16[128,128]{1,0:T(8,128)(2,1)} %ow.1) | copy-start | bytes 98308
  34.6 2.5 %collective-permute-start = (bf16[16,144,128]{2,1,0:T(8,128)(2,1)S(1)}, bf16[16,144,128]{2,1,0:T(8,128)(2,1)S(1)}, u32[]{:S(2)}, u32[]{:S(2)}) collective-permute-start(bf16[16,144,128]{2,1,0:T(8,128)(2,1)S(1)} %get-tuple-element.63), channel_id=1, source_target_pairs={{0,4},{4,0},{8,12},{12,8},{16,20},{20,16},{24,28},{28,24},{32,36},... | collective-permute-start | bytes 1769480 | tf_op jit(solution)/shard_map/ppermute | solution.py:645
  51.3 14.8 %all-to-all-start.2 = ((bf16[16,2,80,128]{3,2,1,0:T(8,128)(2,1)}), bf16[16,2,80,128]{3,2,1,0:T(8,128)(2,1)S(1)}, u32[]{:S(2)}, u32[]{:S(2)}) async-start(bf16[16,2,80,128]{3,2,1,0:T(8,128)(2,1)} %bitcast.8), calls=%async_computation.2 | async-start | bytes 1310720 | tf_op jit(solution)/shard_map/all_to_all | solution.py:670
  55.0 4.9 %collective-permute-start.1 = (bf16[144,128]{1,0:T(8,128)(2,1)S(1)}, bf16[144,128]{1,0:T(8,128)(2,1)S(1)}, u32[]{:S(2)}, u32[]{:S(2)}) collective-permute-start(bf16[144,128]{1,0:T(8,128)(2,1)S(1)} %shard_map.420.mine), channel_id=1, source_target_pairs={{0,1},{1,2},{2,3},{3,0},{4,5},{5,6},{6,7},{7,4},{8,9},{9,10},{10,1... | collective-permute-start | bytes 110600 | tf_op jit(solution)/shard_map/ppermute | solution.py:686
  56.3 4.3 %collective-permute-start.2 = (bf16[144,128]{1,0:T(8,128)(2,1)S(1)}, bf16[144,128]{1,0:T(8,128)(2,1)S(1)}, u32[]{:S(2)}, u32[]{:S(2)}) collective-permute-start(bf16[144,128]{1,0:T(8,128)(2,1)S(1)} %shard_map.420.mine), channel_id=1, source_target_pairs={{0,2},{1,3},{2,0},{3,1},{4,6},{5,7},{6,4},{7,5},{8,10},{9,11},{10,... | collective-permute-start | bytes 110600 | tf_op jit(solution)/shard_map/ppermute | solution.py:686
  58.8 3.1 %collective-permute-start.3 = (bf16[144,128]{1,0:T(8,128)(2,1)S(1)}, bf16[144,128]{1,0:T(8,128)(2,1)S(1)}, u32[]{:S(2)}, u32[]{:S(2)}) collective-permute-start(bf16[144,128]{1,0:T(8,128)(2,1)S(1)} %shard_map.420.mine), channel_id=1, source_target_pairs={{0,3},{1,0},{2,1},{3,2},{4,7},{5,4},{6,5},{7,6},{8,11},{9,8},{10,9... | collective-permute-start | bytes 110600 | tf_op jit(solution)/shard_map/ppermute | solution.py:686
  66.1 12.9 %all-to-all-start.3 = ((bf16[16,144,128]{2,1,0:T(8,128)(2,1)}), bf16[16,144,128]{2,1,0:T(8,128)(2,1)S(1)}, u32[]{:S(2)}, u32[]{:S(2)}) async-start(bf16[16,144,128]{2,1,0:T(8,128)(2,1)} %shard_map.421), calls=%async_computation.3 | async-start | bytes 1179648 | tf_op jit(solution)/shard_map/all_to_all | solution.py:670
  69.8 4.7 %collective-permute-start.4 = (bf16[16,80,128]{2,1,0:T(8,128)(2,1)S(1)}, bf16[16,80,128]{2,1,0:T(8,128)(2,1)S(1)}, u32[]{:S(2)}, u32[]{:S(2)}) collective-permute-start(bf16[16,80,128]{2,1,0:T(8,128)(2,1)S(1)} %get-tuple-element.95), channel_id=1, source_target_pairs={{0,4},{4,0},{8,12},{12,8},{16,20},{20,16},{24,28},{28,24},{32,36},... | collective-permute-start | bytes 983048 | tf_op jit(solution)/shard_map/ppermute | solution.py:702
  79.0 6.2 %collective-permute-start.5 = (bf16[16,144,128]{2,1,0:T(8,128)(2,1)S(1)}, bf16[16,144,128]{2,1,0:T(8,128)(2,1)S(1)}, u32[]{:S(2)}, u32[]{:S(2)}) collective-permute-start(bf16[16,144,128]{2,1,0:T(8,128)(2,1)S(1)} %all-to-all-done.3.own), channel_id=1, source_target_pairs={{0,4},{4,0},{8,12},{12,8},{16,20},{20,16},{24,28},{28,24},{32,36},... | collective-permute-start | bytes 1769480 | tf_op jit(solution)/shard_map/ppermute | solution.py:721

commit v7 on v6

--- a/solution.py
+++ b/solution.py
@@ -80,19 +80,11 @@
 
 def pack_kernel(feat_hbm, cot_hbm, out, stage, cots, feat, cot, ready):
     images = out.shape[0]
-    first = pltpu.make_async_copy(feat_hbm, feat, ready.at[0])
-    second = pltpu.make_async_copy(cot_hbm, cot, ready.at[1])
+    first = pltpu.make_async_copy(cot_hbm, cot, ready.at[0])
+    second = pltpu.make_async_copy(feat_hbm, feat, ready.at[1])
     first.start()
     second.start()
     first.wait()
-    for k in range(images):
-        base = k * PIXROWS
-        begin = first_tile(k) * LANES
-        for t in range(WIN):
-            stage[base + 4 * t : base + 4 * t + 4, :] = feat[
-                :, begin + t * LANES : begin + (t + 1) * LANES
-            ].astype(F32)
-    second.wait()
     cots[...] = cot[...].astype(F32)
     for k in range(images):
         base = k * PIXROWS
@@ -101,6 +93,14 @@
             at = k * OPIX + j * LANES
             row = base + 44 + 10 * j
             stage[row : row + 10, 0:width] = cots[:, at : at + width]
+    second.wait()
+    for k in range(images):
+        base = k * PIXROWS
+        begin = first_tile(k) * LANES
+        for t in range(WIN):
+            stage[base + 4 * t : base + 4 * t + 4, :] = feat[
+                :, begin + t * LANES : begin + (t + 1) * LANES
+            ].astype(F32)
         out[k] = stage[base : base + PIXROWS, :].astype(BF16)
 
 

time: 87.7 us -> 87.6 us (level)
  no operation moved by 1% of the time
where the time goes in v7:
time: 87.6 us; the launch traced here: 87.2 us
  starting transfers between devices  30.3 us (35%)
  waiting for transfers between devices  19.8 us (23%)
  Pallas kernels  18 us (21%)
  blocking collectives  14.2 us (16%)
  local copies, waits for them, and re-layouts  2.9 us (3%)
  between operations  1.87 us (2%)
    all_to_all x1, blocking collectives, exchange(): lax.all_to_all(v, 'ch', split_axis=0, concat_axis=0, tiled=True, axis_ind...  14.2 us
    all_to_all x1, starting transfers between devices, body(): lax.all_to_all(chunks, 'ch', split_axis=0, concat_axis=0, tiled=True)  9.61 us
    all_to_all x1, waiting for transfers between devices, body(): lax.all_to_all(chunks, 'ch', split_axis=0, concat_axis=0, tiled=True)  8.8 us
    pallas_call x1, Pallas kernels, body(): pl.pallas_call(main_kernel, cost_estimate=cost(22), out_shape=(jax.ShapeD...  8.75 us
    all_to_all x2, starting transfers between devices, exchange(): lax.all_to_all(v, 'ch', split_axis=0, concat_axis=0, tiled=True, axis_ind...  7.18 us
    all_to_all x2, waiting for transfers between devices, exchange(): lax.all_to_all(v, 'ch', split_axis=0, concat_axis=0, tiled=True, axis_ind...  6.12 us
    ppermute x3, starting transfers between devices, body(): lax.ppermute(mine, 'img', [(i, (i + d) % groups) for i in range(groups)])  4.89 us
    ppermute x1, starting transfers between devices, body(): other_half = lax.ppermute(own_half, 'ch', other_core)  4.54 us
  transfers between devices with their start and end apart: 9, of which 7 were waited for; matrix products, arithmetic and copies ran while one was open for 3% of the time, Pallas kernels for 5%

profile of v7, /device:TPU:1, one launch (start us, length us, event | category | flops | bytes accessed | tf_op | source)
XLA Modules:
  0.0 87.2 jit_solution(6697996840821986682)
XLA Ops:
  0.7 2.5 %shard_map.416 = bf16[32,80,128]{2,1,0:T(8,128)(2,1)} custom-call(bf16[4,41472]{1,0:T(4,128)(2,1)} %feat_hbm.1, bf16[10,10368]{1,0:T(8,128)(2,1)} %cot_hbm.1), custom_call_target="tpu_custom_call" | custom-call | bytes 9225000 | tf_op jit(solution)/shard_map/pallas_call | solution.py:561
  3.1 9.6 %all-to-all-start = ((bf16[32,80,128]{2,1,0:T(8,128)(2,1)}), bf16[32,80,128]{2,1,0:T(8,128)(2,1)S(1)}, u32[]{:S(2)}, u32[]{:S(2)}) async-start(bf16[32,80,128]{2,1,0:T(8,128)(2,1)} %shard_map.416), calls=%async_computation | async-start | bytes 1310720 | tf_op jit(solution)/shard_map/all_to_all | solution.py:576
  12.8 0.0 copy-start.9
  12.8 0.0 copy-start.7
  12.8 0.0 copy-start.13
  12.8 0.0 copy-start.14
  12.8 0.0 copy-start.15
  12.8 0.0 copy-start.16
  12.9 0.0 copy-start.17
  12.9 0.0 copy-start.18
  12.9 0.0 copy-start.19
  12.9 0.0 copy-start.20
  12.9 0.0 copy-start.21
  12.9 0.0 copy-start.22
  13.0 0.0 copy-start.12
  13.0 0.0 copy-start.8
  13.0 0.0 copy-start.2
  13.0 0.0 copy-start.3
  13.1 1.1 %copy.56 = bf16[320,9,128]{0,2,1:T(8,128)(2,1)S(1)} copy(bf16[320,9,128]{2,0,1:T(8,128)(2,1)S(1)} %copy-done.6) | data formatting | bytes 1474560 | tf_op args[22]
  14.2 0.8 copy.59.kw
  15.0 0.1 reshape.69.kbias
  15.2 0.1 copy.57.sqb
  15.3 0.6 dynamic_slice.11
  16.7 0.1 pad_add_fusion.info
  16.9 8.8 %all-to-all-done.recv = bf16[32,80,128]{2,1,0:T(8,128)(2,1)S(1)} async-done(((bf16[32,80,128]{2,1,0:T(8,128)(2,1)}), bf16[32,80,128]{2,1,0:T(8,128)(2,1)S(1)}, u32[]{:S(2)}, u32[]{:S(2)}) %all-to-all-start) | async-done | bytes 655392 | tf_op jit(solution)/shard_map/all_to_all | solution.py:576
  25.7 8.8 %shard_map.417 = (f32[16,144,128]{2,1,0:T(8,128)S(1)}, bf16[16,144,128]{2,1,0:T(8,128)(2,1)S(1)}, f32[1440,128]{1,0:T(8,128)S(1)}, f32[320,384]{1,0:T(8,128)S(1)}) custom-call(s32[3]{0:T(128)S(1)} %pad_add_fusion.info, bf16[32,80,128]{2,1,0:T(8,128)(2,1)S(1)} %all-to-all-done.recv, f32[17,128]{1,0:T(8,128)S(1)} %bitcast.20, ...), custom_call_target="tpu_custom_call" | custom-call | bytes 81180000 | tf_op jit(solution)/shard_map/pallas_call | solution.py:581
  34.5 0.6 collective-permute-start
  35.1 1.8 %shard_map.418 = bf16[32,80,128]{2,1,0:T(8,128)(2,1)} custom-call(s32[3]{0:T(128)S(1)} %pad_add_fusion.info, f32[1440,128]{1,0:T(8,128)S(1)} %get-tuple-element.60.grad, f32[320,384]{1,0:T(8,128)S(1)} %get-tuple-element.61.section), custom_call_target="tpu_custom_call" | custom-call | bytes 9225000 | tf_op jit(solution)/shard_map/pallas_call | solution.py:646
  36.9 0.1 shard_map.419
  37.0 14.2 %all_to_all.20.recv = bf16[16,144,128]{2,1,0:T(8,128)(2,1)S(1)} all-to-all(bf16[16,144,128]{2,1,0:T(8,128)(2,1)S(1)} %shard_map.419), channel_id=1, replica_groups={{0,8,16,24,32,40,48,56,64,72,80,88,96,104,112,120},{4,12,20,28,36,44,52..., dimensions={0} | all-to-all | bytes 1179648 | tf_op jit(solution)/shard_map/all_to_all | solution.py:670
  51.2 3.6 %all-to-all-start.2 = ((bf16[16,2,80,128]{3,2,1,0:T(8,128)(2,1)}), bf16[16,2,80,128]{3,2,1,0:T(8,128)(2,1)S(1)}, u32[]{:S(2)}, u32[]{:S(2)}) async-start(bf16[16,2,80,128]{3,2,1,0:T(8,128)(2,1)} %bitcast.8), calls=%async_computation.2 | async-start | bytes 1310720 | tf_op jit(solution)/shard_map/all_to_all | solution.py:670
  54.8 0.1 shard_map.420.mine
  54.9 1.3 %collective-permute-start.1 = (bf16[144,128]{1,0:T(8,128)(2,1)S(1)}, bf16[144,128]{1,0:T(8,128)(2,1)S(1)}, u32[]{:S(2)}, u32[]{:S(2)}) collective-permute-start(bf16[144,128]{1,0:T(8,128)(2,1)S(1)} %shard_map.420.mine), channel_id=1, source_target_pairs={{0,1},{1,2},{2,3},{3,0},{4,5},{5,6},{6,7},{7,4},{8,9},{9,10},{10,1... | collective-permute-start | bytes 110600 | tf_op jit(solution)/shard_map/ppermute | solution.py:686
  56.2 2.4 %collective-permute-start.2 = (bf16[144,128]{1,0:T(8,128)(2,1)S(1)}, bf16[144,128]{1,0:T(8,128)(2,1)S(1)}, u32[]{:S(2)}, u32[]{:S(2)}) collective-permute-start(bf16[144,128]{1,0:T(8,128)(2,1)S(1)} %shard_map.420.mine), channel_id=1, source_target_pairs={{0,2},{1,3},{2,0},{3,1},{4,6},{5,7},{6,4},{7,5},{8,10},{9,11},{10,... | collective-permute-start | bytes 110600 | tf_op jit(solution)/shard_map/ppermute | solution.py:686
  58.6 1.2 %collective-permute-start.3 = (bf16[144,128]{1,0:T(8,128)(2,1)S(1)}, bf16[144,128]{1,0:T(8,128)(2,1)S(1)}, u32[]{:S(2)}, u32[]{:S(2)}) collective-permute-start(bf16[144,128]{1,0:T(8,128)(2,1)S(1)} %shard_map.420.mine), channel_id=1, source_target_pairs={{0,3},{1,0},{2,1},{3,2},{4,7},{5,4},{6,5},{7,6},{8,11},{9,8},{10,9... | collective-permute-start | bytes 110600 | tf_op jit(solution)/shard_map/ppermute | solution.py:686
  59.8 0.7 collective-permute-done.2.two
  60.5 1.2 %collective-permute-done.3.three = bf16[144,128]{1,0:T(8,128)(2,1)S(1)} collective-permute-done((bf16[144,128]{1,0:T(8,128)(2,1)S(1)}, bf16[144,128]{1,0:T(8,128)(2,1)S(1)}, u32[]{:S(2)}, u32[]{:S(2)}) %collective-permute-start.3) | collective-permute-done | bytes 36896 | tf_op jit(solution)/shard_map/ppermute | solution.py:686
  61.8 0.9 shard_map.421
  62.6 3.4 %all-to-all-done.2 = bf16[16,2,80,128]{3,2,1,0:T(8,128)(2,1)S(1)} async-done(((bf16[16,2,80,128]{3,2,1,0:T(8,128)(2,1)}), bf16[16,2,80,128]{3,2,1,0:T(8,128)(2,1)S(1)}, u32[]{:S(2)}, u32[]{:S(2)}) %all-to-all-start.2) | async-done | bytes 655392 | tf_op jit(solution)/shard_map/all_to_all | solution.py:670
  66.0 3.6 %all-to-all-start.3 = ((bf16[16,144,128]{2,1,0:T(8,128)(2,1)}), bf16[16,144,128]{2,1,0:T(8,128)(2,1)S(1)}, u32[]{:S(2)}, u32[]{:S(2)}) async-start(bf16[16,144,128]{2,1,0:T(8,128)(2,1)} %shard_map.421), calls=%async_computation.3 | async-start | bytes 1179648 | tf_op jit(solution)/shard_map/all_to_all | solution.py:670
  69.6 0.1 dynamic-slice_bitcast_fusion
  69.7 3.4 %collective-permute-start.4 = (bf16[16,80,128]{2,1,0:T(8,128)(2,1)S(1)}, bf16[16,80,128]{2,1,0:T(8,128)(2,1)S(1)}, u32[]{:S(2)}, u32[]{:S(2)}) collective-permute-start(bf16[16,80,128]{2,1,0:T(8,128)(2,1)S(1)} %get-tuple-element.95), channel_id=1, source_target_pairs={{0,4},{4,0},{8,12},{12,8},{16,20},{20,16},{24,28},{28,24},{32,36},... | collective-permute-start | bytes 983048 | tf_op jit(solution)/shard_map/ppermute | solution.py:702
  73.1 1.3 %collective-permute-done.4.far = bf16[16,80,128]{2,1,0:T(8,128)(2,1)S(1)} collective-permute-done((bf16[16,80,128]{2,1,0:T(8,128)(2,1)S(1)}, bf16[16,80,128]{2,1,0:T(8,128)(2,1)S(1)}, u32[]{:S(2)}, u32[]{:S(2)}) %collective-permute-start.4) | collective-permute-done | bytes 327712 | tf_op jit(solution)/shard_map/ppermute | solution.py:702
  74.4 1.8 %shard_map.422 = (f32[4,41472]{1,0:T(4,128)}, bf16[10,10368]{1,0:T(8,128)(2,1)}) custom-call(s32[3]{0:T(128)S(1)} %pad_add_fusion.info, bf16[16,80,128]{2,1,0:T(8,128)(2,1)S(1)} %get-tuple-element.96.near, bf16[16,80,128]{2,1,0:T(8,128)(2,1)S(1)} %collective-permute-done.4.far), custom_call_target="tpu_custom_call" | custom-call | bytes 9225000 | tf_op jit(solution)/shard_map/pallas_call | solution.py:704
  76.2 2.7 %all-to-all-done.3.own = bf16[16,144,128]{2,1,0:T(8,128)(2,1)S(1)} async-done(((bf16[16,144,128]{2,1,0:T(8,128)(2,1)}), bf16[16,144,128]{2,1,0:T(8,128)(2,1)S(1)}, u32[]{:S(2)}, u32[]{:S(2)}) %all-to-all-start.3) | async-done | bytes 589856 | tf_op jit(solution)/shard_map/all_to_all | solution.py:670
  78.9 4.5 %collective-permute-start.5 = (bf16[16,144,128]{2,1,0:T(8,128)(2,1)S(1)}, bf16[16,144,128]{2,1,0:T(8,128)(2,1)S(1)}, u32[]{:S(2)}, u32[]{:S(2)}) collective-permute-start(bf16[16,144,128]{2,1,0:T(8,128)(2,1)S(1)} %all-to-all-done.3.own), channel_id=1, source_target_pairs={{0,4},{4,0},{8,12},{12,8},{16,20},{20,16},{24,28},{28,24},{32,36},... | collective-permute-start | bytes 1769480 | tf_op jit(solution)/shard_map/ppermute | solution.py:721
  83.5 1.6 %collective-permute-done.5.other = bf16[16,144,128]{2,1,0:T(8,128)(2,1)S(1)} collective-permute-done((bf16[16,144,128]{2,1,0:T(8,128)(2,1)S(1)}, bf16[16,144,128]{2,1,0:T(8,128)(2,1)S(1)}, u32[]{:S(2)}, u32[]{:S(2)}) %collective-permute-start.5) | collective-permute-done | bytes 589856 | tf_op jit(solution)/shard_map/ppermute | solution.py:721
  85.1 2.1 %shard_map.423 = (f32[9,320,128]{2,1,0:T(8,128)}, f32[512,128]{1,0:T(8,128)}, f32[128,512]{1,0:T(8,128)}, f32[128,128]{1,0:T(8,128)}, f32[128,128]{1,0:T(8,128)}...) custom-call(s32[3]{0:T(128)S(1)} %pad_add_fusion.info, ...), custom_call_target="tpu_custom_call" | custom-call | bytes 10332000 | tf_op jit(solution)/shard_map/pallas_call | solution.py:748
  (48 shorter events, 0.2 us)
Async XLA Ops:
  0.7 12.1 %copy-start.6 = (bf16[320,9,128]{2,0,1:T(8,128)(2,1)S(1)}, bf16[320,9,128]{2,0,1:T(8,128)(2,1)}, u32[]{:S(2)}) copy-start(bf16[320,9,128]{2,0,1:T(8,128)(2,1)} %param.47) | copy-start | bytes 2211844
  3.1 22.5 %all-to-all-start = ((bf16[32,80,128]{2,1,0:T(8,128)(2,1)}), bf16[32,80,128]{2,1,0:T(8,128)(2,1)S(1)}, u32[]{:S(2)}, u32[]{:S(2)}) async-start(bf16[32,80,128]{2,1,0:T(8,128)(2,1)} %shard_map.416), calls=%async_computation | async-start | bytes 1310720 | tf_op jit(solution)/shard_map/all_to_all | solution.py:576
  12.8 2.2 %copy-start.9 = (bf16[320]{0:T(512)(128)(2,1)S(1)}, bf16[320]{0:T(512)(128)(2,1)}, u32[]{:S(2)}) copy-start(bf16[320]{0:T(512)(128)(2,1)} %param.48) | copy-start | bytes 1924
  12.8 2.3 %copy-start.7 = (bf16[32,384]{1,0:T(8,128)(2,1)S(1)}, bf16[32,384]{1,0:T(8,128)(2,1)}, u32[]{:S(2)}) copy-start(bf16[32,384]{1,0:T(8,128)(2,1)} %param.37) | copy-start | bytes 73732
  12.8 2.3 %copy-start.13 = (bf16[32]{0:T(256)(128)(2,1)S(1)}, bf16[32]{0:T(256)(128)(2,1)}, u32[]{:S(2)}) copy-start(bf16[32]{0:T(256)(128)(2,1)} %param.36) | copy-start | bytes 196
  12.8 2.4 %copy-start.14 = (s32[32]{0:T(128)S(1)}, s32[32]{0:T(128)}, u32[]{:S(2)}) copy-start(s32[32]{0:T(128)} %param.26) | copy-start | bytes 388
  12.8 3.7 %copy-start.15 = (bf16[128]{0:T(256)(128)(2,1)S(1)}, bf16[128]{0:T(256)(128)(2,1)}, u32[]{:S(2)}) copy-start(bf16[128]{0:T(256)(128)(2,1)} %param.28) | copy-start | bytes 772
  12.8 3.7 %copy-start.16 = (bf16[128]{0:T(256)(128)(2,1)S(1)}, bf16[128]{0:T(256)(128)(2,1)}, u32[]{:S(2)}) copy-start(bf16[128]{0:T(256)(128)(2,1)} %param.29) | copy-start | bytes 772
  12.9 3.7 %copy-start.17 = (bf16[128]{0:T(256)(128)(2,1)S(1)}, bf16[128]{0:T(256)(128)(2,1)}, u32[]{:S(2)}) copy-start(bf16[128]{0:T(256)(128)(2,1)} %param.31) | copy-start | bytes 772
  12.9 3.7 %copy-start.18 = (bf16[128]{0:T(256)(128)(2,1)S(1)}, bf16[128]{0:T(256)(128)(2,1)}, u32[]{:S(2)}) copy-start(bf16[128]{0:T(256)(128)(2,1)} %param.33) | copy-start | bytes 772
  12.9 3.7 %copy-start.19 = (bf16[128]{0:T(256)(128)(2,1)S(1)}, bf16[128]{0:T(256)(128)(2,1)}, u32[]{:S(2)}) copy-start(bf16[128]{0:T(256)(128)(2,1)} %param.40) | copy-start | bytes 772
  12.9 3.7 %copy-start.20 = (bf16[128]{0:T(256)(128)(2,1)S(1)}, bf16[128]{0:T(256)(128)(2,1)}, u32[]{:S(2)}) copy-start(bf16[128]{0:T(256)(128)(2,1)} %param.41) | copy-start | bytes 772
  12.9 3.7 %copy-start.21 = (bf16[128]{0:T(256)(128)(2,1)S(1)}, bf16[128]{0:T(256)(128)(2,1)}, u32[]{:S(2)}) copy-start(bf16[128]{0:T(256)(128)(2,1)} %param.42) | copy-start | bytes 772
  12.9 3.7 %copy-start.22 = (bf16[128]{0:T(256)(128)(2,1)S(1)}, bf16[128]{0:T(256)(128)(2,1)}, u32[]{:S(2)}) copy-start(bf16[128]{0:T(256)(128)(2,1)} %param.46) | copy-start | bytes 772
  12.9 3.8 %copy-start.10 = (bf16[512]{0:T(512)(128)(2,1)S(1)}, bf16[512]{0:T(512)(128)(2,1)}, u32[]{:S(2)}) copy-start(bf16[512]{0:T(512)(128)(2,1)} %param.44) | copy-start | bytes 3076
  12.9 3.8 %copy-start.11 = (bf16[384]{0:T(512)(128)(2,1)S(1)}, bf16[384]{0:T(512)(128)(2,1)}, u32[]{:S(2)}) copy-start(bf16[384]{0:T(512)(128)(2,1)} %param.38) | copy-start | bytes 2308
  13.0 3.9 %copy-start.12 = (s32[2,128]{1,0:T(2,128)S(1)}, s32[2,128]{1,0:T(2,128)}, u32[]{:S(2)}) copy-start(s32[2,128]{1,0:T(2,128)} %param.27) | copy-start | bytes 3076
  13.0 3.9 %copy-start.8 = (bf16[128,32]{0,1:T(8,128)(2,1)S(1)}, bf16[128,32]{0,1:T(8,128)(2,1)}, u32[]{:S(2)}) copy-start(bf16[128,32]{0,1:T(8,128)(2,1)} %param.35) | copy-start | bytes 24580
  13.0 12.7 %copy-start = (bf16[128,512]{1,0:T(8,128)(2,1)S(1)}, bf16[128,512]{1,0:T(8,128)(2,1)}, u32[]{:S(2)}) copy-start(bf16[128,512]{1,0:T(8,128)(2,1)} %xw.1) | copy-start | bytes 393220
  13.0 12.7 %copy-start.1 = (bf16[512,128]{1,0:T(8,128)(2,1)S(1)}, bf16[512,128]{1,0:T(8,128)(2,1)}, u32[]{:S(2)}) copy-start(bf16[512,128]{1,0:T(8,128)(2,1)} %rw.1) | copy-start | bytes 393220
  13.0 12.7 %copy-start.2 = (bf16[128,128]{1,0:T(8,128)(2,1)S(1)}, bf16[128,128]{1,0:T(8,128)(2,1)}, u32[]{:S(2)}) copy-start(bf16[128,128]{1,0:T(8,128)(2,1)} %hw.1) | copy-start | bytes 98308
  13.0 12.7 %copy-start.3 = (bf16[128,128]{1,0:T(8,128)(2,1)S(1)}, bf16[128,128]{1,0:T(8,128)(2,1)}, u32[]{:S(2)}) copy-start(bf16[128,128]{1,0:T(8,128)(2,1)} %ww.1) | copy-start | bytes 98308
  13.0 12.7 %copy-start.4 = (bf16[128,128]{1,0:T(8,128)(2,1)S(1)}, bf16[128,128]{1,0:T(8,128)(2,1)}, u32[]{:S(2)}) copy-start(bf16[128,128]{1,0:T(8,128)(2,1)} %cw.1) | copy-start | bytes 98308
  13.0 12.7 %copy-start.5 = (bf16[128,128]{1,0:T(8,128)(2,1)S(1)}, bf16[128,128]{1,0:T(8,128)(2,1)}, u32[]{:S(2)}) copy-start(bf16[128,128]{1,0:T(8,128)(2,1)} %ow.1) | copy-start | bytes 98308
  34.5 2.5 %collective-permute-start = (bf16[16,144,128]{2,1,0:T(8,128)(2,1)S(1)}, bf16[16,144,128]{2,1,0:T(8,128)(2,1)S(1)}, u32[]{:S(2)}, u32[]{:S(2)}) collective-permute-start(bf16[16,144,128]{2,1,0:T(8,128)(2,1)S(1)} %get-tuple-element.63), channel_id=1, source_target_pairs={{0,4},{4,0},{8,12},{12,8},{16,20},{20,16},{24,28},{28,24},{32,36},... | collective-permute-start | bytes 1769480 | tf_op jit(solution)/shard_map/ppermute | solution.py:645
  51.2 14.8 %all-to-all-start.2 = ((bf16[16,2,80,128]{3,2,1,0:T(8,128)(2,1)}), bf16[16,2,80,128]{3,2,1,0:T(8,128)(2,1)S(1)}, u32[]{:S(2)}, u32[]{:S(2)}) async-start(bf16[16,2,80,128]{3,2,1,0:T(8,128)(2,1)} %bitcast.8), calls=%async_computation.2 | async-start | bytes 1310720 | tf_op jit(solution)/shard_map/all_to_all | solution.py:670
  54.9 4.9 %collective-permute-start.1 = (bf16[144,128]{1,0:T(8,128)(2,1)S(1)}, bf16[144,128]{1,0:T(8,128)(2,1)S(1)}, u32[]{:S(2)}, u32[]{:S(2)}) collective-permute-start(bf16[144,128]{1,0:T(8,128)(2,1)S(1)} %shard_map.420.mine), channel_id=1, source_target_pairs={{0,1},{1,2},{2,3},{3,0},{4,5},{5,6},{6,7},{7,4},{8,9},{9,10},{10,1... | collective-permute-start | bytes 110600 | tf_op jit(solution)/shard_map/ppermute | solution.py:686
  56.2 4.3 %collective-permute-start.2 = (bf16[144,128]{1,0:T(8,128)(2,1)S(1)}, bf16[144,128]{1,0:T(8,128)(2,1)S(1)}, u32[]{:S(2)}, u32[]{:S(2)}) collective-permute-start(bf16[144,128]{1,0:T(8,128)(2,1)S(1)} %shard_map.420.mine), channel_id=1, source_target_pairs={{0,2},{1,3},{2,0},{3,1},{4,6},{5,7},{6,4},{7,5},{8,10},{9,11},{10,... | collective-permute-start | bytes 110600 | tf_op jit(solution)/shard_map/ppermute | solution.py:686
  58.6 3.1 %collective-permute-start.3 = (bf16[144,128]{1,0:T(8,128)(2,1)S(1)}, bf16[144,128]{1,0:T(8,128)(2,1)S(1)}, u32[]{:S(2)}, u32[]{:S(2)}) collective-permute-start(bf16[144,128]{1,0:T(8,128)(2,1)S(1)} %shard_map.420.mine), channel_id=1, source_target_pairs={{0,3},{1,0},{2,1},{3,2},{4,7},{5,4},{6,5},{7,6},{8,11},{9,8},{10,9... | collective-permute-start | bytes 110600 | tf_op jit(solution)/shard_map/ppermute | solution.py:686
  66.0 12.9 %all-to-all-start.3 = ((bf16[16,144,128]{2,1,0:T(8,128)(2,1)}), bf16[16,144,128]{2,1,0:T(8,128)(2,1)S(1)}, u32[]{:S(2)}, u32[]{:S(2)}) async-start(bf16[16,144,128]{2,1,0:T(8,128)(2,1)} %shard_map.421), calls=%async_computation.3 | async-start | bytes 1179648 | tf_op jit(solution)/shard_map/all_to_all | solution.py:670
  69.7 4.7 %collective-permute-start.4 = (bf16[16,80,128]{2,1,0:T(8,128)(2,1)S(1)}, bf16[16,80,128]{2,1,0:T(8,128)(2,1)S(1)}, u32[]{:S(2)}, u32[]{:S(2)}) collective-permute-start(bf16[16,80,128]{2,1,0:T(8,128)(2,1)S(1)} %get-tuple-element.95), channel_id=1, source_target_pairs={{0,4},{4,0},{8,12},{12,8},{16,20},{20,16},{24,28},{28,24},{32,36},... | collective-permute-start | bytes 983048 | tf_op jit(solution)/shard_map/ppermute | solution.py:702
  78.9 6.2 %collective-permute-start.5 = (bf16[16,144,128]{2,1,0:T(8,128)(2,1)S(1)}, bf16[16,144,128]{2,1,0:T(8,128)(2,1)S(1)}, u32[]{:S(2)}, u32[]{:S(2)}) collective-permute-start(bf16[16,144,128]{2,1,0:T(8,128)(2,1)S(1)} %all-to-all-done.3.own), channel_id=1, source_target_pairs={{0,4},{4,0},{8,12},{12,8},{16,20},{20,16},{24,28},{28,24},{32,36},... | collective-permute-start | bytes 1769480 | tf_op jit(solution)/shard_map/ppermute | solution.py:721

commit v8 on v6

--- a/solution.py
+++ b/solution.py
@@ -25,6 +25,8 @@
 
 F32 = jnp.float32
 BF16 = jnp.bfloat16
+
+CHIPS = (1, 6, 8, 9, 13, 4, 2, 14, 10, 7, 15, 11, 3, 0, 5, 12)
 
 AT_CONV = 0
 AT_REDUCE = 2880
@@ -415,7 +417,7 @@
             stage[base + 44 + 10 * j : base + 54 + 10 * j, :] = section[
                 10 * s : 10 * s + 10, j * LANES : (j + 1) * LANES
             ]
-        out[s] = stage[base : base + PIXROWS, :].astype(BF16)
+        out[2 * CHIPS.index(s // 2) + s % 2] = stage[base : base + PIXROWS, :].astype(BF16)
 
 
 def pair_kernel(kept, met, out):
@@ -441,8 +443,8 @@
 def pixel_kernel(info, near, far, feat, section, stage, recv):
     core = info[2]
     for i in range(near.shape[0]):
-        recv[2 * i + core] = near[i]
-        recv[2 * i + 1 - core] = far[i]
+        recv[2 * CHIPS[i] + core] = near[i]
+        recv[2 * CHIPS[i] + 1 - core] = far[i]
     for k in range(recv.shape[0]):
         piece = recv[k].astype(F32)
         tile = first_tile(k)
@@ -641,7 +643,7 @@
         stride_weight.reshape(OUT, 9 * CH),
     )
     other_core = [(i, i ^ 1) for i in range(shards)]
-    same_core = [[2 * i + c for i in range(shards // 2)] for c in range(2)]
+    same_core = [[2 * i + c for i in CHIPS] for c in range(2)]
     met = lax.ppermute(sent, "ch", other_core)
     pixels = pl.pallas_call(
         send_kernel,

time: 87.7 us -> 87.9 us (level)
  waiting for transfers between devices: 19.8 us -> 18.3 us
  starting transfers between devices: 30.3 us -> 31.4 us
    all_to_all x2, waiting for transfers between devices: 6.11 us -> 4.61 us  [exchange(): lax.all_to_all(v, 'ch', split_axis=0, concat_axis=0, tiled=True, axis_ind...]
where the time goes in v8:
time: 87.9 us; the launch traced here: 87.4 us
  starting transfers between devices  31.4 us (36%)
  waiting for transfers between devices  18.3 us (21%)
  Pallas kernels  18.1 us (21%)
  blocking collectives  14.7 us (17%)
  local copies, waits for them, and re-layouts  2.89 us (3%)
  between operations  1.84 us (2%)
    all_to_all x1, blocking collectives, exchange(): lax.all_to_all(v, 'ch', split_axis=0, concat_axis=0, tiled=True, axis_ind...  14.7 us
    all_to_all x1, starting transfers between devices, body(): lax.all_to_all(chunks, 'ch', split_axis=0, concat_axis=0, tiled=True)  9.61 us
    all_to_all x1, waiting for transfers between devices, body(): lax.all_to_all(chunks, 'ch', split_axis=0, concat_axis=0, tiled=True)  8.8 us
    pallas_call x1, Pallas kernels, body(): pl.pallas_call(main_kernel, cost_estimate=cost(22), out_shape=(jax.ShapeD...  8.75 us
    all_to_all x2, starting transfers between devices, exchange(): lax.all_to_all(v, 'ch', split_axis=0, concat_axis=0, tiled=True, axis_ind...  7.8 us
    ppermute x3, starting transfers between devices, body(): lax.ppermute(mine, 'img', [(i, (i + d) % groups) for i in range(groups)])  4.88 us
    all_to_all x2, waiting for transfers between devices, exchange(): lax.all_to_all(v, 'ch', split_axis=0, concat_axis=0, tiled=True, axis_ind...  4.61 us
    ppermute x1, starting transfers between devices, body(): other_half = lax.ppermute(own_half, 'ch', other_core)  4.51 us
  transfers between devices with their start and end apart: 9, of which 7 were waited for; matrix products, arithmetic and copies ran while one was open for 3% of the time, Pallas kernels for 5%

profile of v8, /device:TPU:1, one launch (start us, length us, event | category | flops | bytes accessed | tf_op | source)
XLA Modules:
  0.0 87.4 jit_solution(16427863640342305632)
XLA Ops:
  0.7 2.6 %shard_map.416 = bf16[32,80,128]{2,1,0:T(8,128)(2,1)} custom-call(bf16[4,41472]{1,0:T(4,128)(2,1)} %feat_hbm.1, bf16[10,10368]{1,0:T(8,128)(2,1)} %cot_hbm.1), custom_call_target="tpu_custom_call" | custom-call | bytes 9225000 | tf_op jit(solution)/shard_map/pallas_call | solution.py:563
  3.2 9.6 %all-to-all-start = ((bf16[32,80,128]{2,1,0:T(8,128)(2,1)}), bf16[32,80,128]{2,1,0:T(8,128)(2,1)S(1)}, u32[]{:S(2)}, u32[]{:S(2)}) async-start(bf16[32,80,128]{2,1,0:T(8,128)(2,1)} %shard_map.416), calls=%async_computation | async-start | bytes 1310720 | tf_op jit(solution)/shard_map/all_to_all | solution.py:578
  12.9 0.0 copy-start.9
  12.9 0.0 copy-start.7
  12.9 0.0 copy-start.13
  12.9 0.0 copy-start.14
  12.9 0.0 copy-start.15
  13.0 0.0 copy-start.16
  13.0 0.0 copy-start.17
  13.0 0.0 copy-start.18
  13.0 0.0 copy-start.19
  13.0 0.0 copy-start.20
  13.0 0.0 copy-start.21
  13.0 0.0 copy-start.22
  13.0 0.0 copy-start.10
  13.1 0.0 copy-start.8
  13.1 0.0 copy-start
  13.1 0.0 copy-start.2
  13.1 0.0 copy-start.3
  13.2 1.1 %copy.56 = bf16[320,9,128]{0,2,1:T(8,128)(2,1)S(1)} copy(bf16[320,9,128]{2,0,1:T(8,128)(2,1)S(1)} %copy-done.6) | data formatting | bytes 1474560 | tf_op args[22]
  14.3 0.8 copy.59.kw
  15.1 0.1 reshape.69.kbias
  15.3 0.1 copy.57.sqb
  15.4 0.6 dynamic_slice.11
  16.8 0.1 pad_add_fusion.info
  17.0 8.8 %all-to-all-done.recv = bf16[32,80,128]{2,1,0:T(8,128)(2,1)S(1)} async-done(((bf16[32,80,128]{2,1,0:T(8,128)(2,1)}), bf16[32,80,128]{2,1,0:T(8,128)(2,1)S(1)}, u32[]{:S(2)}, u32[]{:S(2)}) %all-to-all-start) | async-done | bytes 655392 | tf_op jit(solution)/shard_map/all_to_all | solution.py:578
  25.8 8.8 %shard_map.417 = (f32[16,144,128]{2,1,0:T(8,128)S(1)}, bf16[16,144,128]{2,1,0:T(8,128)(2,1)S(1)}, f32[1440,128]{1,0:T(8,128)S(1)}, f32[320,384]{1,0:T(8,128)S(1)}) custom-call(s32[3]{0:T(128)S(1)} %pad_add_fusion.info, bf16[32,80,128]{2,1,0:T(8,128)(2,1)S(1)} %all-to-all-done.recv, f32[17,128]{1,0:T(8,128)S(1)} %bitcast.20, ...), custom_call_target="tpu_custom_call" | custom-call | bytes 81180000 | tf_op jit(solution)/shard_map/pallas_call | solution.py:583
  34.6 0.6 collective-permute-start
  35.2 1.8 %shard_map.418 = bf16[32,80,128]{2,1,0:T(8,128)(2,1)} custom-call(s32[3]{0:T(128)S(1)} %pad_add_fusion.info, f32[1440,128]{1,0:T(8,128)S(1)} %get-tuple-element.60.grad, f32[320,384]{1,0:T(8,128)S(1)} %get-tuple-element.61.section), custom_call_target="tpu_custom_call" | custom-call | bytes 9225000 | tf_op jit(solution)/shard_map/pallas_call | solution.py:648
  37.0 0.1 shard_map.419
  37.1 14.7 %all_to_all.20.recv = bf16[16,144,128]{2,1,0:T(8,128)(2,1)S(1)} all-to-all(bf16[16,144,128]{2,1,0:T(8,128)(2,1)S(1)} %shard_map.419), channel_id=1, replica_groups={{8,48,64,72,104,32,16,112,80,56,120,88,24,0,40,96},{12,52,68,76,108,36,..., dimensions={0} | all-to-all | bytes 1179648 | tf_op jit(solution)/shard_map/all_to_all | solution.py:672
  51.9 3.5 %all-to-all-start.2 = ((bf16[16,2,80,128]{3,2,1,0:T(8,128)(2,1)}), bf16[16,2,80,128]{3,2,1,0:T(8,128)(2,1)S(1)}, u32[]{:S(2)}, u32[]{:S(2)}) async-start(bf16[16,2,80,128]{3,2,1,0:T(8,128)(2,1)} %bitcast.8), calls=%async_computation.2 | async-start | bytes 1310720 | tf_op jit(solution)/shard_map/all_to_all | solution.py:672
  55.4 0.1 shard_map.420.mine
  55.5 1.3 %collective-permute-start.1 = (bf16[144,128]{1,0:T(8,128)(2,1)S(1)}, bf16[144,128]{1,0:T(8,128)(2,1)S(1)}, u32[]{:S(2)}, u32[]{:S(2)}) collective-permute-start(bf16[144,128]{1,0:T(8,128)(2,1)S(1)} %shard_map.420.mine), channel_id=1, source_target_pairs={{0,1},{1,2},{2,3},{3,0},{4,5},{5,6},{6,7},{7,4},{8,9},{9,10},{10,1... | collective-permute-start | bytes 110600 | tf_op jit(solution)/shard_map/ppermute | solution.py:688
  56.7 2.5 %collective-permute-start.2 = (bf16[144,128]{1,0:T(8,128)(2,1)S(1)}, bf16[144,128]{1,0:T(8,128)(2,1)S(1)}, u32[]{:S(2)}, u32[]{:S(2)}) collective-permute-start(bf16[144,128]{1,0:T(8,128)(2,1)S(1)} %shard_map.420.mine), channel_id=1, source_target_pairs={{0,2},{1,3},{2,0},{3,1},{4,6},{5,7},{6,4},{7,5},{8,10},{9,11},{10,... | collective-permute-start | bytes 110600 | tf_op jit(solution)/shard_map/ppermute | solution.py:688
  59.2 1.1 %collective-permute-start.3 = (bf16[144,128]{1,0:T(8,128)(2,1)S(1)}, bf16[144,128]{1,0:T(8,128)(2,1)S(1)}, u32[]{:S(2)}, u32[]{:S(2)}) collective-permute-start(bf16[144,128]{1,0:T(8,128)(2,1)S(1)} %shard_map.420.mine), channel_id=1, source_target_pairs={{0,3},{1,0},{2,1},{3,2},{4,7},{5,4},{6,5},{7,6},{8,11},{9,8},{10,9... | collective-permute-start | bytes 110600 | tf_op jit(solution)/shard_map/ppermute | solution.py:688
  60.3 0.7 collective-permute-done.2.two
  61.1 1.2 %collective-permute-done.3.three = bf16[144,128]{1,0:T(8,128)(2,1)S(1)} collective-permute-done((bf16[144,128]{1,0:T(8,128)(2,1)S(1)}, bf16[144,128]{1,0:T(8,128)(2,1)S(1)}, u32[]{:S(2)}, u32[]{:S(2)}) %collective-permute-start.3) | collective-permute-done | bytes 36896 | tf_op jit(solution)/shard_map/ppermute | solution.py:688
  62.3 0.9 shard_map.421
  63.2 2.6 %all-to-all-done.2 = bf16[16,2,80,128]{3,2,1,0:T(8,128)(2,1)S(1)} async-done(((bf16[16,2,80,128]{3,2,1,0:T(8,128)(2,1)}), bf16[16,2,80,128]{3,2,1,0:T(8,128)(2,1)S(1)}, u32[]{:S(2)}, u32[]{:S(2)}) %all-to-all-start.2) | async-done | bytes 655392 | tf_op jit(solution)/shard_map/all_to_all | solution.py:672
  65.7 4.3 %all-to-all-start.3 = ((bf16[16,144,128]{2,1,0:T(8,128)(2,1)}), bf16[16,144,128]{2,1,0:T(8,128)(2,1)S(1)}, u32[]{:S(2)}, u32[]{:S(2)}) async-start(bf16[16,144,128]{2,1,0:T(8,128)(2,1)} %shard_map.421), calls=%async_computation.3 | async-start | bytes 1179648 | tf_op jit(solution)/shard_map/all_to_all | solution.py:672
  70.1 4.0 %collective-permute-start.4 = (bf16[16,80,128]{2,1,0:T(8,128)(2,1)S(1)}, bf16[16,80,128]{2,1,0:T(8,128)(2,1)S(1)}, u32[]{:S(2)}, u32[]{:S(2)}) collective-permute-start(bf16[16,80,128]{2,1,0:T(8,128)(2,1)S(1)} %get-tuple-element.95), channel_id=1, source_target_pairs={{0,4},{4,0},{8,12},{12,8},{16,20},{20,16},{24,28},{28,24},{32,36},... | collective-permute-start | bytes 983048 | tf_op jit(solution)/shard_map/ppermute | solution.py:704
  74.1 1.3 %collective-permute-done.4.far = bf16[16,80,128]{2,1,0:T(8,128)(2,1)S(1)} collective-permute-done((bf16[16,80,128]{2,1,0:T(8,128)(2,1)S(1)}, bf16[16,80,128]{2,1,0:T(8,128)(2,1)S(1)}, u32[]{:S(2)}, u32[]{:S(2)}) %collective-permute-start.4) | collective-permute-done | bytes 327712 | tf_op jit(solution)/shard_map/ppermute | solution.py:704
  75.3 1.8 %shard_map.422 = (f32[4,41472]{1,0:T(4,128)}, bf16[10,10368]{1,0:T(8,128)(2,1)}) custom-call(s32[3]{0:T(128)S(1)} %pad_add_fusion.info, bf16[16,80,128]{2,1,0:T(8,128)(2,1)S(1)} %get-tuple-element.96.near, bf16[16,80,128]{2,1,0:T(8,128)(2,1)S(1)} %collective-permute-done.4.far), custom_call_target="tpu_custom_call" | custom-call | bytes 9225000 | tf_op jit(solution)/shard_map/pallas_call | solution.py:706
  77.2 2.0 %all-to-all-done.3.own = bf16[16,144,128]{2,1,0:T(8,128)(2,1)S(1)} async-done(((bf16[16,144,128]{2,1,0:T(8,128)(2,1)}), bf16[16,144,128]{2,1,0:T(8,128)(2,1)S(1)}, u32[]{:S(2)}, u32[]{:S(2)}) %all-to-all-start.3) | async-done | bytes 589856 | tf_op jit(solution)/shard_map/all_to_all | solution.py:672
  79.2 4.5 %collective-permute-start.5 = (bf16[16,144,128]{2,1,0:T(8,128)(2,1)S(1)}, bf16[16,144,128]{2,1,0:T(8,128)(2,1)S(1)}, u32[]{:S(2)}, u32[]{:S(2)}) collective-permute-start(bf16[16,144,128]{2,1,0:T(8,128)(2,1)S(1)} %all-to-all-done.3.own), channel_id=1, source_target_pairs={{0,4},{4,0},{8,12},{12,8},{16,20},{20,16},{24,28},{28,24},{32,36},... | collective-permute-start | bytes 1769480 | tf_op jit(solution)/shard_map/ppermute | solution.py:723
  83.7 1.6 %collective-permute-done.5.other = bf16[16,144,128]{2,1,0:T(8,128)(2,1)S(1)} collective-permute-done((bf16[16,144,128]{2,1,0:T(8,128)(2,1)S(1)}, bf16[16,144,128]{2,1,0:T(8,128)(2,1)S(1)}, u32[]{:S(2)}, u32[]{:S(2)}) %collective-permute-start.5) | collective-permute-done | bytes 589856 | tf_op jit(solution)/shard_map/ppermute | solution.py:723
  85.3 2.1 %shard_map.423 = (f32[9,320,128]{2,1,0:T(8,128)}, f32[512,128]{1,0:T(8,128)}, f32[128,512]{1,0:T(8,128)}, f32[128,128]{1,0:T(8,128)}, f32[128,128]{1,0:T(8,128)}...) custom-call(s32[3]{0:T(128)S(1)} %pad_add_fusion.info, ...), custom_call_target="tpu_custom_call" | custom-call | bytes 10332000 | tf_op jit(solution)/shard_map/pallas_call | solution.py:750
  (48 shorter events, 0.2 us)
Async XLA Ops:
  0.7 12.2 %copy-start.6 = (bf16[320,9,128]{2,0,1:T(8,128)(2,1)S(1)}, bf16[320,9,128]{2,0,1:T(8,128)(2,1)}, u32[]{:S(2)}) copy-start(bf16[320,9,128]{2,0,1:T(8,128)(2,1)} %param.47) | copy-start | bytes 2211844
  3.2 22.5 %all-to-all-start = ((bf16[32,80,128]{2,1,0:T(8,128)(2,1)}), bf16[32,80,128]{2,1,0:T(8,128)(2,1)S(1)}, u32[]{:S(2)}, u32[]{:S(2)}) async-start(bf16[32,80,128]{2,1,0:T(8,128)(2,1)} %shard_map.416), calls=%async_computation | async-start | bytes 1310720 | tf_op jit(solution)/shard_map/all_to_all | solution.py:578
  12.9 2.2 %copy-start.9 = (bf16[320]{0:T(512)(128)(2,1)S(1)}, bf16[320]{0:T(512)(128)(2,1)}, u32[]{:S(2)}) copy-start(bf16[320]{0:T(512)(128)(2,1)} %param.48) | copy-start | bytes 1924
  12.9 2.3 %copy-start.7 = (bf16[32,384]{1,0:T(8,128)(2,1)S(1)}, bf16[32,384]{1,0:T(8,128)(2,1)}, u32[]{:S(2)}) copy-start(bf16[32,384]{1,0:T(8,128)(2,1)} %param.37) | copy-start | bytes 73732
  12.9 2.3 %copy-start.13 = (bf16[32]{0:T(256)(128)(2,1)S(1)}, bf16[32]{0:T(256)(128)(2,1)}, u32[]{:S(2)}) copy-start(bf16[32]{0:T(256)(128)(2,1)} %param.36) | copy-start | bytes 196
  12.9 2.4 %copy-start.14 = (s32[32]{0:T(128)S(1)}, s32[32]{0:T(128)}, u32[]{:S(2)}) copy-start(s32[32]{0:T(128)} %param.26) | copy-start | bytes 388
  12.9 3.7 %copy-start.15 = (bf16[128]{0:T(256)(128)(2,1)S(1)}, bf16[128]{0:T(256)(128)(2,1)}, u32[]{:S(2)}) copy-start(bf16[128]{0:T(256)(128)(2,1)} %param.28) | copy-start | bytes 772
  13.0 3.7 %copy-start.16 = (bf16[128]{0:T(256)(128)(2,1)S(1)}, bf16[128]{0:T(256)(128)(2,1)}, u32[]{:S(2)}) copy-start(bf16[128]{0:T(256)(128)(2,1)} %param.29) | copy-start | bytes 772
  13.0 3.7 %copy-start.17 = (bf16[128]{0:T(256)(128)(2,1)S(1)}, bf16[128]{0:T(256)(128)(2,1)}, u32[]{:S(2)}) copy-start(bf16[128]{0:T(256)(128)(2,1)} %param.31) | copy-start | bytes 772
  13.0 3.7 %copy-start.18 = (bf16[128]{0:T(256)(128)(2,1)S(1)}, bf16[128]{0:T(256)(128)(2,1)}, u32[]{:S(2)}) copy-start(bf16[128]{0:T(256)(128)(2,1)} %param.33) | copy-start | bytes 772
  13.0 3.7 %copy-start.19 = (bf16[128]{0:T(256)(128)(2,1)S(1)}, bf16[128]{0:T(256)(128)(2,1)}, u32[]{:S(2)}) copy-start(bf16[128]{0:T(256)(128)(2,1)} %param.40) | copy-start | bytes 772
  13.0 3.7 %copy-start.20 = (bf16[128]{0:T(256)(128)(2,1)S(1)}, bf16[128]{0:T(256)(128)(2,1)}, u32[]{:S(2)}) copy-start(bf16[128]{0:T(256)(128)(2,1)} %param.41) | copy-start | bytes 772
  13.0 3.7 %copy-start.21 = (bf16[128]{0:T(256)(128)(2,1)S(1)}, bf16[128]{0:T(256)(128)(2,1)}, u32[]{:S(2)}) copy-start(bf16[128]{0:T(256)(128)(2,1)} %param.42) | copy-start | bytes 772
  13.0 3.7 %copy-start.22 = (bf16[128]{0:T(256)(128)(2,1)S(1)}, bf16[128]{0:T(256)(128)(2,1)}, u32[]{:S(2)}) copy-start(bf16[128]{0:T(256)(128)(2,1)} %param.46) | copy-start | bytes 772
  13.0 3.8 %copy-start.10 = (bf16[512]{0:T(512)(128)(2,1)S(1)}, bf16[512]{0:T(512)(128)(2,1)}, u32[]{:S(2)}) copy-start(bf16[512]{0:T(512)(128)(2,1)} %param.44) | copy-start | bytes 3076
  13.1 3.8 %copy-start.11 = (bf16[384]{0:T(512)(128)(2,1)S(1)}, bf16[384]{0:T(512)(128)(2,1)}, u32[]{:S(2)}) copy-start(bf16[384]{0:T(512)(128)(2,1)} %param.38) | copy-start | bytes 2308
  13.1 3.9 %copy-start.12 = (s32[2,128]{1,0:T(2,128)S(1)}, s32[2,128]{1,0:T(2,128)}, u32[]{:S(2)}) copy-start(s32[2,128]{1,0:T(2,128)} %param.27) | copy-start | bytes 3076
  13.1 3.9 %copy-start.8 = (bf16[128,32]{0,1:T(8,128)(2,1)S(1)}, bf16[128,32]{0,1:T(8,128)(2,1)}, u32[]{:S(2)}) copy-start(bf16[128,32]{0,1:T(8,128)(2,1)} %param.35) | copy-start | bytes 24580
  13.1 12.7 %copy-start = (bf16[128,512]{1,0:T(8,128)(2,1)S(1)}, bf16[128,512]{1,0:T(8,128)(2,1)}, u32[]{:S(2)}) copy-start(bf16[128,512]{1,0:T(8,128)(2,1)} %xw.1) | copy-start | bytes 393220
  13.1 12.7 %copy-start.1 = (bf16[512,128]{1,0:T(8,128)(2,1)S(1)}, bf16[512,128]{1,0:T(8,128)(2,1)}, u32[]{:S(2)}) copy-start(bf16[512,128]{1,0:T(8,128)(2,1)} %rw.1) | copy-start | bytes 393220
  13.1 12.7 %copy-start.2 = (bf16[128,128]{1,0:T(8,128)(2,1)S(1)}, bf16[128,128]{1,0:T(8,128)(2,1)}, u32[]{:S(2)}) copy-start(bf16[128,128]{1,0:T(8,128)(2,1)} %hw.1) | copy-start | bytes 98308
  13.1 12.7 %copy-start.3 = (bf16[128,128]{1,0:T(8,128)(2,1)S(1)}, bf16[128,128]{1,0:T(8,128)(2,1)}, u32[]{:S(2)}) copy-start(bf16[128,128]{1,0:T(8,128)(2,1)} %ww.1) | copy-start | bytes 98308
  13.1 12.7 %copy-start.4 = (bf16[128,128]{1,0:T(8,128)(2,1)S(1)}, bf16[128,128]{1,0:T(8,128)(2,1)}, u32[]{:S(2)}) copy-start(bf16[128,128]{1,0:T(8,128)(2,1)} %cw.1) | copy-start | bytes 98308
  13.1 12.7 %copy-start.5 = (bf16[128,128]{1,0:T(8,128)(2,1)S(1)}, bf16[128,128]{1,0:T(8,128)(2,1)}, u32[]{:S(2)}) copy-start(bf16[128,128]{1,0:T(8,128)(2,1)} %ow.1) | copy-start | bytes 98308
  34.6 2.5 %collective-permute-start = (bf16[16,144,128]{2,1,0:T(8,128)(2,1)S(1)}, bf16[16,144,128]{2,1,0:T(8,128)(2,1)S(1)}, u32[]{:S(2)}, u32[]{:S(2)}) collective-permute-start(bf16[16,144,128]{2,1,0:T(8,128)(2,1)S(1)} %get-tuple-element.63), channel_id=1, source_target_pairs={{0,4},{4,0},{8,12},{12,8},{16,20},{20,16},{24,28},{28,24},{32,36},... | collective-permute-start | bytes 1769480 | tf_op jit(solution)/shard_map/ppermute | solution.py:647
  51.9 13.9 %all-to-all-start.2 = ((bf16[16,2,80,128]{3,2,1,0:T(8,128)(2,1)}), bf16[16,2,80,128]{3,2,1,0:T(8,128)(2,1)S(1)}, u32[]{:S(2)}, u32[]{:S(2)}) async-start(bf16[16,2,80,128]{3,2,1,0:T(8,128)(2,1)} %bitcast.8), calls=%async_computation.2 | async-start | bytes 1310720 | tf_op jit(solution)/shard_map/all_to_all | solution.py:672
  55.5 4.9 %collective-permute-start.1 = (bf16[144,128]{1,0:T(8,128)(2,1)S(1)}, bf16[144,128]{1,0:T(8,128)(2,1)S(1)}, u32[]{:S(2)}, u32[]{:S(2)}) collective-permute-start(bf16[144,128]{1,0:T(8,128)(2,1)S(1)} %shard_map.420.mine), channel_id=1, source_target_pairs={{0,1},{1,2},{2,3},{3,0},{4,5},{5,6},{6,7},{7,4},{8,9},{9,10},{10,1... | collective-permute-start | bytes 110600 | tf_op jit(solution)/shard_map/ppermute | solution.py:688
  56.7 4.3 %collective-permute-start.2 = (bf16[144,128]{1,0:T(8,128)(2,1)S(1)}, bf16[144,128]{1,0:T(8,128)(2,1)S(1)}, u32[]{:S(2)}, u32[]{:S(2)}) collective-permute-start(bf16[144,128]{1,0:T(8,128)(2,1)S(1)} %shard_map.420.mine), channel_id=1, source_target_pairs={{0,2},{1,3},{2,0},{3,1},{4,6},{5,7},{6,4},{7,5},{8,10},{9,11},{10,... | collective-permute-start | bytes 110600 | tf_op jit(solution)/shard_map/ppermute | solution.py:688
  59.2 3.1 %collective-permute-start.3 = (bf16[144,128]{1,0:T(8,128)(2,1)S(1)}, bf16[144,128]{1,0:T(8,128)(2,1)S(1)}, u32[]{:S(2)}, u32[]{:S(2)}) collective-permute-start(bf16[144,128]{1,0:T(8,128)(2,1)S(1)} %shard_map.420.mine), channel_id=1, source_target_pairs={{0,3},{1,0},{2,1},{3,2},{4,7},{5,4},{6,5},{7,6},{8,11},{9,8},{10,9... | collective-permute-start | bytes 110600 | tf_op jit(solution)/shard_map/ppermute | solution.py:688
  65.7 13.5 %all-to-all-start.3 = ((bf16[16,144,128]{2,1,0:T(8,128)(2,1)}), bf16[16,144,128]{2,1,0:T(8,128)(2,1)S(1)}, u32[]{:S(2)}, u32[]{:S(2)}) async-start(bf16[16,144,128]{2,1,0:T(8,128)(2,1)} %shard_map.421), calls=%async_computation.3 | async-start | bytes 1179648 | tf_op jit(solution)/shard_map/all_to_all | solution.py:672
  70.1 5.3 %collective-permute-start.4 = (bf16[16,80,128]{2,1,0:T(8,128)(2,1)S(1)}, bf16[16,80,128]{2,1,0:T(8,128)(2,1)S(1)}, u32[]{:S(2)}, u32[]{:S(2)}) collective-permute-start(bf16[16,80,128]{2,1,0:T(8,128)(2,1)S(1)} %get-tuple-element.95), channel_id=1, source_target_pairs={{0,4},{4,0},{8,12},{12,8},{16,20},{20,16},{24,28},{28,24},{32,36},... | collective-permute-start | bytes 983048 | tf_op jit(solution)/shard_map/ppermute | solution.py:704
  79.2 6.1 %collective-permute-start.5 = (bf16[16,144,128]{2,1,0:T(8,128)(2,1)S(1)}, bf16[16,144,128]{2,1,0:T(8,128)(2,1)S(1)}, u32[]{:S(2)}, u32[]{:S(2)}) collective-permute-start(bf16[16,144,128]{2,1,0:T(8,128)(2,1)S(1)} %all-to-all-done.3.own), channel_id=1, source_target_pairs={{0,4},{4,0},{8,12},{12,8},{16,20},{20,16},{24,28},{28,24},{32,36},... | collective-permute-start | bytes 1769480 | tf_op jit(solution)/shard_map/ppermute | solution.py:723
